TPU v7x, 32 devices: a whole 2x2x4 slice. The times are simulated.
32 devices in a mesh: grp: 2 (over y), band: 4 (over z), strm: 4 (over x, core).
Axes of the slice: x: 2, y: 2, z: 4, core: 2. Of those that a mesh axis runs over, the one named last changes fastest.
Arguments:
- latents: bfloat16 [8, 2, 4, 16, 384], P(('grp', 'strm'), None, 'band'), parts along dimension 0, may hold values from -6 to 6
- cache_first: bfloat16 [8, 2, 4, 16, 384], P(('grp', 'strm'), None, 'band'), parts along dimension 0, may hold values from -6 to 6
- cache_second: bfloat16 [8, 2, 8, 32, 192], P(('grp', 'strm'), None, 'band'), parts along dimension 0, may hold values from -6 to 6
- gain_first: float32 [384], replicated, may hold values from 0.25 to 1.75
- gain_second: float32 [192], replicated, may hold values from 0.25 to 1.75
- w_first: bfloat16 [3, 3, 3, 384, 768], P(None, None, None, None, 'strm'), may hold values from -0.0625 to 0.0625
- w_second: bfloat16 [3, 3, 3, 192, 192], P(None, None, None, None, 'strm'), may hold values from -0.078125 to 0.078125
- cache_slot: int32 [8], P('grp'), parts along dimension 0, may hold values from 0 to 3, as said below
- block_index: int32 [8], P('grp'), parts along dimension 0, may hold values from 0 to 3, as said below
Outputs:
- decoded: bfloat16 [8, 2, 8, 32, 192], P(('grp', 'strm'), None, 'band'), parts along dimension 0
There are 2 independent parts, one for each index of `grp`. A program takes and returns all parts, laid end to end along the dimension named above; an argument that names none is the same for every part. Nothing has to cross between parts.
Inputs may be any that keep to these rules, and one draw needn't show every extreme that they name: `cache_slot`: each slot holds the caches of exactly one stream. The caches are read only where block_index > 0; exactly one stream of a group has block number 0.
All inputs are finite; a program needn't handle non-finite values.
Results may differ from a plain program's by a relative error of at most 0.0056.
Values may be sent and summed in bfloat16 or wider, within the bound.
No kernel may reach another device: no remote copies, remote signals or barrier semaphores. Data moves between devices by JAX's collectives and lax.ppermute only.
A program may use at most 64 MiB of HBM per device.

v0:
```python
import jax
import jax.numpy as jnp
from jax import lax
from jax.sharding import PartitionSpec as P

epsilon = 1e-06


def padded_2(block, sides, width):
    for axis, dim in sides:
        count = lax.axis_size(axis)
        forward = [(i, i + 1) for i in range(count - 1)]
        backward = [(target, source) for source, target in forward]
        low = lax.ppermute(
            lax.slice_in_dim(block, block.shape[dim] - width, None, axis=dim), axis, forward
        )
        high = lax.ppermute(lax.slice_in_dim(block, 0, width, axis=dim), axis, backward)
        block = jnp.concatenate([low, block, high], axis=dim)
    return block


def norm_silu(values, gain):
    mean_square = jnp.mean(values * values, axis=-1, keepdims=True)
    return jax.nn.silu(values * lax.rsqrt(mean_square + epsilon) * gain)


def causal_conv(inputs, weight):
    padded = jnp.pad(inputs, ((0, 0), (0, 0), (0, 0), (1, 1), (0, 0)))
    count, span, height, width, channels = padded.shape
    frames = span - 2
    rows = height - 2
    columns = width - 2
    outputs = weight.shape[-1]
    summed = jnp.zeros((count * frames * rows * columns, outputs), jnp.float32)
    for frame_tap in range(3):
        for row_tap in range(3):
            window = padded[:, frame_tap : frame_tap + frames, row_tap : row_tap + rows]
            stacked = jnp.concatenate(
                [window[:, :, :, col_tap : col_tap + columns] for col_tap in range(3)], axis=-1
            )
            kernel = weight[frame_tap, row_tap].reshape(3 * channels, outputs)
            summed = summed + jnp.dot(
                stacked.reshape(-1, 3 * channels), kernel, preferred_element_type=jnp.float32
            )
    return summed.reshape(count, frames, rows, columns, outputs)


def earlier_frames(slot_cache, slots, keep_mask):
    chosen = jnp.take(slot_cache, slots, axis=0)
    return jnp.where(keep_mask[:, None, None, None, None], chosen, jnp.zeros_like(chosen))


def body(
    latents,
    cache_first,
    cache_second,
    gain_first,
    gain_second,
    w_first,
    w_second,
    cache_slot,
    block_index,
):
    count_here = latents.shape[0]
    frames = latents.shape[1]
    rows = latents.shape[2]
    columns = latents.shape[3]
    keep_mask = block_index > 0
    first_act = norm_silu(latents.astype(jnp.float32), gain_first).astype(jnp.bfloat16)
    own_stack = jnp.concatenate([cache_first, first_act], axis=1)
    own_bordered = padded_2(own_stack, (("band", 2),), 1)
    everything = lax.all_gather(own_bordered, "strm", axis=0, tiled=True)
    bordered = jnp.concatenate(
        [earlier_frames(everything[:, :2], cache_slot, keep_mask), everything[:, 2:]], axis=1
    )
    phase_piece = causal_conv(bordered, w_first).astype(jnp.bfloat16)
    streams = phase_piece.shape[0]
    quarter = phase_piece.shape[-1]
    sent = phase_piece.reshape(streams, frames, rows, 1, columns * quarter)
    arrived = lax.all_to_all(sent, "strm", split_axis=0, concat_axis=3, tiled=True)
    arrived = arrived.reshape(count_here, frames, rows, 2, 2, columns, quarter)
    upsampled = arrived.transpose(0, 1, 2, 3, 5, 4, 6).reshape(
        count_here, frames, 2 * rows, 2 * columns, quarter
    )
    second_act = norm_silu(upsampled.astype(jnp.float32), gain_second).astype(jnp.bfloat16)
    acts_two, caches_two = (
        lax.all_gather(second_act, "strm", axis=0, tiled=True),
        lax.all_gather(cache_second, "strm", axis=0, tiled=True),
    )
    joined_two = jnp.concatenate(
        [earlier_frames(caches_two, cache_slot, keep_mask), acts_two], axis=1
    )
    bordered_two = padded_2(joined_two, (("band", 2),), 1)
    group_piece = causal_conv(bordered_two, w_second).astype(jnp.bfloat16)
    group_width = group_piece.shape[-1]
    sent_two = group_piece.reshape(streams, frames, 2 * rows, 1, 2 * columns * group_width)
    back = lax.all_to_all(sent_two, "strm", split_axis=0, concat_axis=3, tiled=True)
    back = back.reshape(count_here, frames, 2 * rows, 4, 2 * columns, group_width)
    branch = back.transpose(0, 1, 2, 4, 3, 5).reshape(
        count_here, frames, 2 * rows, 2 * columns, 4 * group_width
    )
    return (upsampled.astype(jnp.float32) + branch.astype(jnp.float32)).astype(jnp.bfloat16)


def solution(mesh):
    in_specs = (
        P(("grp", "strm"), None, "band", None, None),
        P(("grp", "strm"), None, "band", None, None),
        P(("grp", "strm"), None, "band", None, None),
        P(),
        P(),
        P(None, None, None, None, "strm"),
        P(None, None, None, None, "strm"),
        P("grp"),
        P("grp"),
    )
    out_specs = P(("grp", "strm"), None, "band", None, None)
    return jax.shard_map(body, mesh=mesh, in_specs=in_specs, out_specs=out_specs, check_vma=False)
```

profile of v0, /device:TPU:0, one launch (start us, length us, event | category | flops | bytes accessed | tf_op | source)
XLA Modules:
  0.0 87.2 jit_solution(5731138690500192140)
XLA Ops:
  0.0 0.8 fusion.14
  0.8 0.8 fusion.21
  1.7 0.7 pad_maximum_fusion.21
  2.4 4.9 %collective-permute-start = (bf16[1,4,1,16,384]{4,3,2,1,0:T(8,128)(2,1)S(1)}, bf16[1,4,1,16,384]{4,3,2,1,0:T(8,128)(2,1)S(1)}, u32[]{:S(2)}, u32[]{:S(2)}) collective-permute-start(bf16[1,4,1,16,384]{4,3,2,1,0:T(8,128)(2,1)S(1)} %pad_maximum_fusion.21), channel_id=1, source_target_pairs={{0,4},{4,8},{8,12},{1,5},{5,9},{9,13},{2,6},{6,10},{10,14},{3,7},{... | collective-permute-start | bytes 147464 | tf_op jit(solution)/shard_map/ppermute | solution.py:14
  7.4 1.3 %collective-permute-start.1 = (bf16[1,4,1,16,384]{4,3,2,1,0:T(8,128)(2,1)S(1)}, bf16[1,4,1,16,384]{4,3,2,1,0:T(8,128)(2,1)S(1)}, u32[]{:S(2)}, u32[]{:S(2)}) collective-permute-start(bf16[1,4,1,16,384]{4,3,2,1,0:T(8,128)(2,1)S(1)} %pad_maximum_fusion.21), channel_id=1, source_target_pairs={{4,0},{8,4},{12,8},{5,1},{9,5},{13,9},{6,2},{10,6},{14,10},{7,3},{... | collective-permute-start | bytes 147464 | tf_op jit(solution)/shard_map/ppermute | solution.py:17
  8.7 0.7 compare_select_fusion
  9.3 0.7 compare_and_fusion
  10.0 2.5 %fusion.22 = (bf16[1,1,3,384,192]{3,4,2,1,0:T(8,128)(2,1)S(1)}, bf16[1,1,3,384,192]{3,4,2,1,0:T(8,128)(2,1)S(1)}, bf16[1,1,3,384,192]{3,4,2,1,0:T(8,128)(2,1)S(1...) fusion(bf16[3,3,3,384,192]{3,4,2,1,0:T(8,128)(2,1)} %param.14), kind=kLoop, calls=%fused_computation.110 | loop fusion | bytes 7962624 | tf_op jit(solution)/shard_map/slice | solution.py:41
  12.5 0.4 copy.90
  12.9 0.8 copy.119
  13.7 0.4 copy.91
  14.1 0.8 copy.120
  14.9 0.4 copy.92
  15.4 0.4 copy.93
  15.8 0.4 copy.94
  16.3 0.4 copy.95
  16.8 0.4 copy.96
  17.2 0.4 copy.97
  17.7 0.4 copy.98
  18.1 0.8 copy.127
  18.9 5.8 %all_gather.10 = bf16[4,2,2,32,192]{4,3,2,1,0:T(8,128)(2,1)S(1)} all-gather(bf16[1,2,2,32,192]{4,3,2,1,0:T(8,128)(2,1)S(1)} %copy-done.6), channel_id=1, replica_groups=mesh['grp'=2,'band'=4,'strm'=4] {'strm'}, dimensions={0}, use_global_device_ids=true | all-gather | bytes 245760 | tf_op jit(solution)/shard_map/all_gather | solution.py:88
  24.7 1.3 %gather_fusion.1 = bf16[4,2,2,32,192]{4,3,2,1,0:T(8,128)(2,1)} fusion(bf16[4,2,2,32,192]{4,3,2,1,0:T(8,128)(2,1)S(1)} %all_gather.10, s32[1024]{0:T(1024)S(1)} %pad_clamp_fusion), kind=kCustom, calls=%fused_computation.1 | custom fusion | bytes 393232 | tf_op jit(solution)/shard_map/jit(_take)/gather | solution.py:49
  26.0 7.6 %all_gather.9 = bf16[4,4,3,16,384]{4,3,2,1,0:T(8,128)(2,1)S(1)} all-gather(bf16[1,4,3,16,384]{4,3,2,1,0:T(8,128)(2,1)S(1)} %pad_maximum_fusion.20), channel_id=1, replica_groups=mesh['grp'=2,'band'=4,'strm'=4] {'strm'}, dimensions={0}, use_global_device_ids=true | all-gather | bytes 737280 | tf_op jit(solution)/shard_map/all_gather | solution.py:72
  33.6 0.8 fusion.28
  34.4 2.3 %gather_fusion = bf16[4,2,3,16,384]{4,3,2,1,0:T(8,128)(2,1)} fusion(bf16[4,2,3,16,384]{4,3,2,1,0:T(8,128)(2,1)} %get-tuple-element.71, s32[1024]{0:T(1024)S(1)} %pad_clamp_fusion), kind=kCustom, calls=%fused_computation | custom fusion | bytes 589840 | tf_op jit(solution)/shard_map/jit(_take)/gather | solution.py:49
  36.7 1.1 %select_select_fusion = bf16[4,2,3,16,384]{4,3,2,1,0:T(8,128)(2,1)S(1)} fusion(bf16[4,2,3,16,384]{4,3,2,1,0:T(8,128)(2,1)} %gather_fusion, pred[4]{0:T(512)(128)(4,1)S(1)} %get-tuple-element.83, pred[4]{0:T(512)(128)(4,1)S(1)} %get-tuple-element.84), kind=kLoop, calls=%fused_computation.79 | loop fusion | flops 294912 | bytes 589832 | tf_op jit(solution)/shard_map/jit(_where)/select_n | solution.py:50
  38.0 0.4 pad_slice_fusion.1
  38.4 0.5 copy-done.2
  41.7 0.4 copy-done.1
  42.5 0.7 convert_element_type.121
  43.2 3.3 %all-to-all-start = ((bf16[4,2,1,1,3072]{4,1,3,2,0:T(2,128)(2,1)}), bf16[4,2,1,1,3072]{4,1,3,2,0:T(2,128)(2,1)S(1)}, u32[]{:S(2)}, u32[]{:S(2)}) async-start(bf16[4,2,1,1,3072]{4,1,3,2,0:T(2,128)(2,1)} %bitcast.9), calls=%async_computation | async-start | bytes 98304 | tf_op jit(solution)/shard_map/all_to_all | solution.py:80
  46.6 3.9 %all-to-all-done = bf16[4,2,1,1,3072]{4,1,3,2,0:T(2,128)(2,1)S(1)} async-done(((bf16[4,2,1,1,3072]{4,1,3,2,0:T(2,128)(2,1)}), bf16[4,2,1,1,3072]{4,1,3,2,0:T(2,128)(2,1)S(1)}, u32[]{:S(2)}, u32[]{:S(2)}) %all-to-all-start) | async-done | bytes 49184 | tf_op jit(solution)/shard_map/all_to_all | solution.py:80
  51.4 5.8 %all_gather.11 = bf16[4,2,2,32,192]{4,3,2,1,0:T(8,128)(2,1)S(1)} all-gather(bf16[1,2,2,32,192]{4,3,2,1,0:T(8,128)(2,1)S(1)} %multiply_convert_fusion), channel_id=1, replica_groups=mesh['grp'=2,'band'=4,'strm'=4] {'strm'}, dimensions={0}, use_global_device_ids=true | all-gather | bytes 245760 | tf_op jit(solution)/shard_map/all_gather | solution.py:87
  57.3 4.6 %collective-permute-start.2 = (bf16[4,4,1,32,192]{4,3,2,1,0:T(8,128)(2,1)S(1)}, bf16[4,4,1,32,192]{4,3,2,1,0:T(8,128)(2,1)S(1)}, u32[]{:S(2)}, u32[]{:S(2)}) collective-permute-start(bf16[4,4,1,32,192]{4,3,2,1,0:T(8,128)(2,1)S(1)} %get-tuple-element.75), channel_id=1, source_target_pairs={{0,4},{4,8},{8,12},{1,5},{5,9},{9,13},{2,6},{6,10},{10,14},{3,7},{... | collective-permute-start | bytes 589832 | tf_op jit(solution)/shard_map/ppermute | solution.py:14
  61.9 1.5 %collective-permute-start.3 = (bf16[4,4,1,32,192]{4,3,2,1,0:T(8,128)(2,1)S(1)}, bf16[4,4,1,32,192]{4,3,2,1,0:T(8,128)(2,1)S(1)}, u32[]{:S(2)}, u32[]{:S(2)}) collective-permute-start(bf16[4,4,1,32,192]{4,3,2,1,0:T(8,128)(2,1)S(1)} %get-tuple-element.76), channel_id=1, source_target_pairs={{4,0},{8,4},{12,8},{5,1},{9,5},{13,9},{6,2},{10,6},{14,10},{7,3},{... | collective-permute-start | bytes 589832 | tf_op jit(solution)/shard_map/ppermute | solution.py:17
  65.0 2.9 %collective-permute-done.2 = bf16[4,4,1,32,192]{4,3,2,1,0:T(8,128)(2,1)S(1)} collective-permute-done((bf16[4,4,1,32,192]{4,3,2,1,0:T(8,128)(2,1)S(1)}, bf16[4,4,1,32,192]{4,3,2,1,0:T(8,128)(2,1)S(1)}, u32[]{:S(2)}, u32[]{:S(2)}) %collective-permute-start.2) | collective-permute-done | bytes 196640 | tf_op jit(solution)/shard_map/ppermute | solution.py:14
  67.9 4.1 %collective-permute-done.3 = bf16[4,4,1,32,192]{4,3,2,1,0:T(8,128)(2,1)S(1)} collective-permute-done((bf16[4,4,1,32,192]{4,3,2,1,0:T(8,128)(2,1)S(1)}, bf16[4,4,1,32,192]{4,3,2,1,0:T(8,128)(2,1)S(1)}, u32[]{:S(2)}, u32[]{:S(2)}) %collective-permute-start.3) | collective-permute-done | bytes 196640 | tf_op jit(solution)/shard_map/ppermute | solution.py:17
  72.4 0.7 select_maximum_fusion
  73.1 0.9 %fusion.23 = (bf16[4,2,2,32,192]{4,3,2,1,0:T(8,128)(2,1)S(1)}, bf16[4,2,2,32,192]{4,3,2,1,0:T(8,128)(2,1)S(1)}, bf16[4,2,2,32,192]{4,3,2,1,0:T(8,128)(2,1)S(1)},...) fusion(bf16[4,4,4,34,192]{4,3,2,1,0:T(8,128)(2,1)S(1)} %select_, ...), kind=kLoop, calls=%fused_computation.111 | loop fusion | bytes 7077888 | tf_op jit(solution)/shard_map/slice | solution.py:39
  75.9 0.8 pad_maximum_fusion.9
  77.0 0.3 convolution_add_fusion.6
  77.3 0.3 convolution_add_fusion.5
  77.6 0.3 convolution_add_fusion.4
  77.9 0.3 convolution_add_fusion.3
  78.2 0.3 convolution_add_fusion.2
  78.9 0.3 fusion.5
  79.5 6.4 %all_to_all.24 = bf16[4,2,2,1,1536]{4,2,1,3,0:T(2,128)(2,1)S(1)} all-to-all(bf16[4,2,2,1,1536]{4,2,1,3,0:T(2,128)(2,1)S(1)} %bitcast.185), channel_id=1, replica_groups=mesh['grp'=2,'band'=4,'strm'=4] {'strm'}, dimensions={0} | all-to-all | bytes 98304 | tf_op jit(solution)/shard_map/all_to_all | solution.py:97
  86.5 0.6 add_convert_fusion
  (98 shorter events, 9.8 us)
Async XLA Ops:
  2.4 23.5 %collective-permute-start = (bf16[1,4,1,16,384]{4,3,2,1,0:T(8,128)(2,1)S(1)}, bf16[1,4,1,16,384]{4,3,2,1,0:T(8,128)(2,1)S(1)}, u32[]{:S(2)}, u32[]{:S(2)}) collective-permute-start(bf16[1,4,1,16,384]{4,3,2,1,0:T(8,128)(2,1)S(1)} %pad_maximum_fusion.21), channel_id=1, source_target_pairs={{0,4},{4,8},{8,12},{1,5},{5,9},{9,13},{2,6},{6,10},{10,14},{3,7},{... | collective-permute-start | bytes 147464 | tf_op jit(solution)/shard_map/ppermute | solution.py:14
  7.4 18.6 %collective-permute-start.1 = (bf16[1,4,1,16,384]{4,3,2,1,0:T(8,128)(2,1)S(1)}, bf16[1,4,1,16,384]{4,3,2,1,0:T(8,128)(2,1)S(1)}, u32[]{:S(2)}, u32[]{:S(2)}) collective-permute-start(bf16[1,4,1,16,384]{4,3,2,1,0:T(8,128)(2,1)S(1)} %pad_maximum_fusion.21), channel_id=1, source_target_pairs={{4,0},{8,4},{12,8},{5,1},{9,5},{13,9},{6,2},{10,6},{14,10},{7,3},{... | collective-permute-start | bytes 147464 | tf_op jit(solution)/shard_map/ppermute | solution.py:17
  17.6 1.3 %copy-start.6 = (bf16[1,2,2,32,192]{4,3,2,1,0:T(8,128)(2,1)S(1)}, bf16[1,2,2,32,192]{4,3,2,1,0:T(8,128)(2,1)}, u32[]{:S(2)}) copy-start(bf16[1,2,2,32,192]{4,3,2,1,0:T(8,128)(2,1)} %param.11) | copy-start | bytes 147460
  17.7 8.3 %copy-start.5 = (bf16[1,2,1,16,384]{4,3,2,1,0:T(8,128)(2,1)S(1)}, bf16[1,2,1,16,384]{4,3,2,1,0:T(8,128)(2,1)}, u32[]{:S(2)}) copy-start(bf16[1,2,1,16,384]{4,3,2,1,0:T(8,128)(2,1)} %param.10) | copy-start | bytes 73732
  37.9 1.0 %copy-start.2 = (bf16[24,8,3,384]{3,1,2,0:T(8,128)(2,1)S(1)}, bf16[24,8,3,384]{3,1,2,0:T(8,128)(2,1)}, u32[]{:S(2)}) copy-start(bf16[24,8,3,384]{3,1,2,0:T(8,128)(2,1)} %copy.119) | copy-start | bytes 1327108
  38.4 1.0 %copy-start = (bf16[24,8,3,384]{3,1,2,0:T(8,128)(2,1)S(1)}, bf16[24,8,3,384]{3,1,2,0:T(8,128)(2,1)}, u32[]{:S(2)}) copy-start(bf16[24,8,3,384]{3,1,2,0:T(8,128)(2,1)} %copy.120) | copy-start | bytes 1327108
  41.0 1.0 %copy-start.1 = (bf16[24,8,3,384]{3,1,2,0:T(8,128)(2,1)S(1)}, bf16[24,8,3,384]{3,1,2,0:T(8,128)(2,1)}, u32[]{:S(2)}) copy-start(bf16[24,8,3,384]{3,1,2,0:T(8,128)(2,1)} %copy.127) | copy-start | bytes 1327108
  41.4 5.1 %copy-start.3 = (bf16[4,2,2,32,192]{4,3,2,1,0:T(8,128)(2,1)S(1)}, bf16[4,2,2,32,192]{4,3,2,1,0:T(8,128)(2,1)}, u32[]{:S(2)}) copy-start(bf16[4,2,2,32,192]{4,3,2,1,0:T(8,128)(2,1)} %gather_fusion.1) | copy-start | bytes 589828
  42.3 9.0 %copy-start.7 = (f32[192]{0:T(256)S(1)}, f32[192]{0:T(256)}, u32[]{:S(2)}) copy-start(f32[192]{0:T(256)} %param.13) | copy-start | bytes 2308
  43.2 7.3 %all-to-all-start = ((bf16[4,2,1,1,3072]{4,1,3,2,0:T(2,128)(2,1)}), bf16[4,2,1,1,3072]{4,1,3,2,0:T(2,128)(2,1)S(1)}, u32[]{:S(2)}, u32[]{:S(2)}) async-start(bf16[4,2,1,1,3072]{4,1,3,2,0:T(2,128)(2,1)} %bitcast.9), calls=%async_computation | async-start | bytes 98304 | tf_op jit(solution)/shard_map/all_to_all | solution.py:80
  50.6 12.8 %copy-start.4 = (bf16[3,3,3,192,48]{3,4,2,1,0:T(8,128)(2,1)S(1)}, bf16[3,3,3,192,48]{3,4,2,1,0:T(8,128)(2,1)}, u32[]{:S(2)}) copy-start(bf16[3,3,3,192,48]{3,4,2,1,0:T(8,128)(2,1)} %param.15) | copy-start | bytes 1492996
  57.3 10.6 %collective-permute-start.2 = (bf16[4,4,1,32,192]{4,3,2,1,0:T(8,128)(2,1)S(1)}, bf16[4,4,1,32,192]{4,3,2,1,0:T(8,128)(2,1)S(1)}, u32[]{:S(2)}, u32[]{:S(2)}) collective-permute-start(bf16[4,4,1,32,192]{4,3,2,1,0:T(8,128)(2,1)S(1)} %get-tuple-element.75), channel_id=1, source_target_pairs={{0,4},{4,8},{8,12},{1,5},{5,9},{9,13},{2,6},{6,10},{10,14},{3,7},{... | collective-permute-start | bytes 589832 | tf_op jit(solution)/shard_map/ppermute | solution.py:14
  61.9 10.2 %collective-permute-start.3 = (bf16[4,4,1,32,192]{4,3,2,1,0:T(8,128)(2,1)S(1)}, bf16[4,4,1,32,192]{4,3,2,1,0:T(8,128)(2,1)S(1)}, u32[]{:S(2)}, u32[]{:S(2)}) collective-permute-start(bf16[4,4,1,32,192]{4,3,2,1,0:T(8,128)(2,1)S(1)} %get-tuple-element.76), channel_id=1, source_target_pairs={{4,0},{8,4},{12,8},{5,1},{9,5},{13,9},{6,2},{10,6},{14,10},{7,3},{... | collective-permute-start | bytes 589832 | tf_op jit(solution)/shard_map/ppermute | solution.py:17
where the time goes:
time: 87.8 us; the launch traced here: 87.2 us
  blocking collectives  25.6 us (29%)
  local copies, waits for them, and re-layouts  19.5 us (22%)
  starting transfers between devices  15.5 us (18%)
  waiting for transfers between devices  11 us (13%)
  other arithmetic  9.49 us (11%)
  matrix products  5.3 us (6%)
    ppermute x2, starting transfers between devices, padded_2(): lax.ppermute(lax.slice_in_dim(block, block.shape[dim] - width, None, axis...  9.49 us
    all_gather x1, blocking collectives, body(): everything = lax.all_gather(own_bordered, 'strm', axis=0, tiled=True)  7.65 us
    slice x20, local copies, waits for them, and re-layouts, causal_conv(): kernel = weight[frame_tap, row_tap].reshape(3 * channels, outputs)  6.46 us
    all_to_all x1, blocking collectives, body(): lax.all_to_all(sent_two, 'strm', split_axis=0, concat_axis=3, tiled=True)  6.39 us
    all_gather x1, blocking collectives, body(): lax.all_gather(second_act, 'strm', axis=0, tiled=True)  5.79 us
    all_gather x1, blocking collectives, body(): lax.all_gather(cache_second, 'strm', axis=0, tiled=True)  5.77 us
    dot_general x18, matrix products, causal_conv(): jnp.dot(stacked.reshape(-1, 3 * channels), kernel, preferred_element_type...  5.3 us
    ppermute x2, waiting for transfers between devices, padded_2(): lax.ppermute(lax.slice_in_dim(block, 0, width, axis=dim), axis, backward)  4.13 us
  transfers between devices with their start and end apart: 5, of which 3 were waited for; matrix products, arithmetic and copies ran while one was open for 15% of the time, Pallas kernels for 0%

commit v1 on v0

v1 whole, which is shorter than its diff:
```python
import functools

import jax
import jax.numpy as jnp
from jax import lax
from jax.experimental import pallas as pl
from jax.experimental.pallas import tpu as pltpu
from jax.sharding import PartitionSpec as P

epsilon = 1e-06
f32 = jnp.float32
bf16 = jnp.bfloat16


def norm_silu(values, gain):
    mean_square = jnp.mean(values * values, axis=-1, keepdims=True)
    return jax.nn.silu(values * lax.rsqrt(mean_square + epsilon) * gain)


def dot(lhs, rhs, transposed=False):
    dims = (((1,), (1,)), ((), ())) if transposed else (((1,), (0,)), ((), ()))
    return lax.dot_general(lhs, rhs, dims, preferred_element_type=f32)


def shifted(values, width):
    count = values.shape[0]
    place = lax.broadcasted_iota(jnp.int32, values.shape, 0) % width
    left = jnp.where(place == 0, 0.0, pltpu.roll(values, 1, 0))
    right = jnp.where(place == width - 1, 0.0, pltpu.roll(values, count - 1, 0))
    return left, values, right


def first_kernel(frames, columns, meta, *refs):
    latents, firsts, seconds = refs[0:4], refs[4:8], refs[8:12]
    gain, weight = refs[12:14]
    far, near, two, own, mid = refs[14:19]
    slot_first, slot_second = refs[19:21]
    me = meta[8]
    upper = me // 2 == 0
    channels = latents[0].shape[-1]
    outputs = weight.shape[-2]
    for d in range(4):
        slot_first[me ^ d] = firsts[d][...].reshape(2, columns, channels)
        slot_second[me ^ d] = seconds[d][0]

    parts = []
    for d in range(4):
        stream = me ^ d
        chosen = slot_first[meta[stream]].astype(f32)
        chosen = jnp.where(meta[4 + stream] > 0, chosen, 0.0)
        fresh = latents[d][...].reshape(frames * columns, channels).astype(f32)
        parts += [chosen.reshape(2 * columns, channels), norm_silu(fresh, gain[...])]
    views = [
        view.astype(bf16).reshape(4, frames + 2, columns, channels)
        for view in shifted(jnp.concatenate(parts, axis=0), columns)
    ]
    rows = 4 * frames * columns
    sums = [jnp.zeros((rows, outputs), f32) for _ in range(3)]
    taps = [jnp.where(upper, 2, 0), 1, jnp.where(upper, 0, 2)]
    for i in range(3):
        for l in range(3):
            window = views[l][:, i : i + frames].reshape(rows, channels)
            for j in range(3):
                sums[j] = sums[j] + dot(window, weight[i, taps[j], l], True)

    half = rows // 4

    def paired(values):
        return [
            jnp.concatenate([values[2 * p * half : (2 * p + 1) * half], values[(2 * p + 1) * half : (2 * p + 2) * half]], axis=1)
            for p in range(2)
        ]

    u, v, w = paired(sums[0]), paired(sums[1]), paired(sums[2])
    for p in range(2):
        at = pl.ds(p * half, half)
        after = pl.ds((2 + p) * half, half)
        far[at, :] = u[p].astype(bf16)
        far[after, :] = v[p].astype(bf16)
        two[at, :] = u[p].astype(bf16)
        near[at, :] = w[p].astype(bf16)
        own[at, :] = v[p]
        own[after, :] = w[p]

    chosen = slot_second[meta[me]].astype(f32)
    chosen = jnp.where(meta[4 + me] > 0, chosen, 0.0)
    mid[...] = chosen.astype(bf16)
    edges = [jnp.concatenate([chosen[0, r], chosen[1, r]], axis=-1) for r in range(2)]
    width = 2 * columns
    far[pl.ds(4 * half, width), :] = jnp.where(upper, edges[0], edges[1]).astype(bf16)
    near[pl.ds(2 * half, width), :] = jnp.where(upper, edges[1], edges[0]).astype(bf16)


def sum_kernel(half, meta, own, far, near, two, first_pair, second_pair):
    me, place, bands = meta[8], meta[9], meta[10]
    outside = jnp.where(me // 2 == 0, place == bands - 1, place == 0)
    for p, pair in enumerate((first_pair, second_pair)):
        at = pl.ds(p * half, half)
        after = pl.ds((2 + p) * half, half)
        centre = own[at, :] + far[at, :].astype(f32) + near[at, :].astype(f32)
        extra = own[after, :] + far[after, :].astype(f32) + two[at, :].astype(f32)
        pair[pl.ds(0, half), :] = centre.astype(bf16)
        pair[pl.ds(half, half), :] = jnp.where(outside, 0.0, extra).astype(bf16)


def second_kernel(frames, columns, meta, *refs):
    pairs, mid, far, near = refs[0:4], refs[4], refs[5], refs[6]
    weights, gain, out = refs[7:11], refs[11], refs[12]
    taps, quarters, sems = refs[13:16]
    me = meta[8]
    upper = me // 2 == 0
    channels = out.shape[-1]
    group = channels // 4
    half = frames * columns
    width = 2 * columns
    copies = [
        pltpu.make_async_copy(
            weights[d], taps.at[:, :, :, pl.ds(pl.multiple_of((me ^ d) * group, 16), group), :], sems.at[d]
        )
        for d in range(4)
    ]
    for copy in copies:
        copy.start()

    for e in range(4):
        quarters[me ^ e] = pairs[e][:, (e % 2) * channels : (e % 2 + 1) * channels]

    fields = [quarters[q].astype(f32).reshape(2, frames, columns, channels) for q in range(4)]
    row_of = ((1, 1), (0, 0), (1, 0), (0, 1))
    upsampled = jnp.stack(
        [jnp.stack([jnp.stack([fields[2 * a + b][c, t] for b in range(2)]) for a, c in row_of]) for t in range(frames)]
    )
    act = norm_silu(upsampled.reshape(-1, channels), gain[...])
    left, same, right = [
        v.astype(bf16).reshape(frames, 4, 2, columns, channels) for v in shifted(act, columns)
    ]

    def split(first, second):
        return jnp.stack([first, second], axis=2)

    act_views = [
        split(left[:, :, 1], same[:, :, 0]),
        same,
        split(same[:, :, 1], right[:, :, 0]),
    ]

    beyond = far[pl.ds(4 * half, width), :]
    behind = near[pl.ds(2 * half, width), :]
    top = jnp.where(upper, behind.astype(f32), beyond.astype(f32)).astype(bf16)
    bottom = jnp.where(upper, beyond.astype(f32), behind.astype(f32)).astype(bf16)
    stored = jnp.stack(
        [
            jnp.stack([top[:, f * channels : (f + 1) * channels], mid[f, 0], mid[f, 1], bottom[:, f * channels : (f + 1) * channels]])
            for f in range(2)
        ]
    ).reshape(2 * 4 * width, channels)
    size = stored.shape[0]
    row = lax.broadcasted_iota(jnp.int32, (size, size), 0)
    column = lax.broadcasted_iota(jnp.int32, (size, size), 1)
    inside = row % width
    natural = 2 * (inside % columns) + inside // columns
    cache_views = []
    for l in range(3):
        source = natural + (l - 1)
        keep = (source >= 0) & (source < width) & (column == row - inside + source)
        pick = jnp.where(keep, 1.0, 0.0).astype(bf16)
        cache_views.append(dot(pick, stored).astype(bf16).reshape(2, 4, 2, columns, channels))

    for copy in copies:
        copy.wait()

    area = 2 * width
    early = jnp.zeros((area, channels), f32)
    late = jnp.zeros((area, channels), f32)
    for j in range(3):
        for l in range(3):
            c0, c1 = [cache_views[l][f, j : j + 2].reshape(area, channels) for f in range(2)]
            a0, a1 = [act_views[l][f, j : j + 2].reshape(area, channels) for f in range(2)]
            early = early + dot(c0, taps[0, j, l], True) + dot(c1, taps[1, j, l], True) + dot(a0, taps[2, j, l], True)
            late = late + dot(c1, taps[0, j, l], True) + dot(a0, taps[1, j, l], True) + dot(a1, taps[2, j, l], True)

    row = lax.broadcasted_iota(jnp.int32, (area, area), 0)
    column = lax.broadcasted_iota(jnp.int32, (area, area), 1)
    inside = row % width
    keep = column == row - inside + (inside % 2) * columns + inside // 2
    order = jnp.where(keep, 1.0, 0.0).astype(bf16)
    for t, branch in enumerate((early, late)):
        base = upsampled[t, 1:3].reshape(area, channels)
        decoded = (base + branch.astype(bf16).astype(f32)).astype(bf16)
        out[0, t] = dot(order, decoded).astype(bf16).reshape(2, width, channels)


def whole(count):
    return [pl.BlockSpec(memory_space=pltpu.VMEM)] * count


SMEM = pl.BlockSpec(memory_space=pltpu.SMEM)


def body(latents, cache_first, cache_second, gain_first, gain_second, w_first, w_second, cache_slot, block_index):
    frames, columns, channels = latents.shape[1], latents.shape[3], latents.shape[4]
    outputs = w_first.shape[-1]
    bands = lax.axis_size("band")
    streams = lax.axis_size("strm")
    assert streams == 4 and latents.shape[2] == 1 and frames == 2
    half = frames * columns
    width = 2 * columns
    me = lax.axis_index("strm")
    place = lax.axis_index("band")
    meta = jnp.concatenate([cache_slot, block_index, jnp.stack([me, place, jnp.int32(bands)]).astype(jnp.int32)])

    def swapped(value, distance):
        return lax.ppermute(value, "strm", [(i, i ^ distance) for i in range(streams)])

    def along(value, step):
        pairs = []
        for band in range(bands):
            for k in range(streams):
                target = band - step if k // 2 == 0 else band + step
                if 0 <= target < bands:
                    pairs.append((band * streams + k, target * streams + k))
        return lax.ppermute(value, ("band", "strm"), pairs)

    def everyone(value):
        across = swapped(value, 2)
        return [value, swapped(value, 1), across, swapped(across, 1)]

    turned_first = jnp.swapaxes(w_first, 3, 4)
    turned_second = jnp.swapaxes(w_second, 3, 4)
    args = everyone(latents) + everyone(cache_first) + everyone(cache_second)
    pair = jax.ShapeDtypeStruct((2 * half, 2 * outputs), bf16)
    far, near, two, own, mid = pl.pallas_call(
        functools.partial(first_kernel, frames, columns),
        out_shape=[
            jax.ShapeDtypeStruct((4 * half + width, 2 * outputs), bf16),
            jax.ShapeDtypeStruct((2 * half + width, 2 * outputs), bf16),
            pair,
            jax.ShapeDtypeStruct((4 * half, 2 * outputs), f32),
            jax.ShapeDtypeStruct(cache_second.shape[1:], bf16),
        ],
        in_specs=[SMEM] + whole(14),
        out_specs=whole(5),
        scratch_shapes=[
            pltpu.VMEM((4,) + (2, columns, channels), bf16),
            pltpu.VMEM((4,) + cache_second.shape[1:], bf16),
        ],
        compiler_params=pltpu.CompilerParams(vmem_limit_bytes=24 * 2**20),
        name="first_conv",
    )(meta, *args, gain_first.reshape(1, -1), turned_first)
    weights = everyone(turned_second)
    far, near, two = along(far, 1), along(near, -1), along(two, 2)
    first_pair, second_pair = pl.pallas_call(
        functools.partial(sum_kernel, half),
        out_shape=[pair, pair],
        in_specs=[SMEM] + whole(4),
        out_specs=whole(2),
        name="row_sums",
    )(meta, own, far, near, two)
    across = swapped(second_pair, 2)
    pairs = [first_pair, swapped(first_pair, 1), across, swapped(across, 1)]
    decoded = pl.pallas_call(
        functools.partial(second_kernel, frames, columns),
        out_shape=jax.ShapeDtypeStruct((1, frames, 2, width, outputs), bf16),
        in_specs=[SMEM] + whole(7) + [pl.BlockSpec(memory_space=pl.ANY)] * 4 + whole(1),
        out_specs=pl.BlockSpec(memory_space=pltpu.VMEM),
        scratch_shapes=[
            pltpu.VMEM((3, 3, 3, outputs, outputs), bf16),
            pltpu.VMEM((4, 2 * half, outputs), bf16),
            pltpu.SemaphoreType.DMA((4,)),
        ],
        compiler_params=pltpu.CompilerParams(vmem_limit_bytes=24 * 2**20),
        name="second_conv",
    )(meta, *pairs, mid, far, near, *weights, gain_second.reshape(1, -1))
    return decoded


def solution(mesh):
    in_specs = (
        P(("grp", "strm"), None, "band", None, None),
        P(("grp", "strm"), None, "band", None, None),
        P(("grp", "strm"), None, "band", None, None),
        P(),
        P(),
        P(None, None, None, None, "strm"),
        P(None, None, None, None, "strm"),
        P("grp"),
        P("grp"),
    )
    out_specs = P(("grp", "strm"), None, "band", None, None)
    return jax.shard_map(body, mesh=mesh, in_specs=in_specs, out_specs=out_specs, check_vma=False)
```

time: 87.8 us -> 64.9 us (0.74)
  blocking collectives: 25.6 us -> 0 us
  waiting for transfers between devices: 11 us -> 30.5 us
  other arithmetic: 9.49 us -> 0 us
  local copies, waits for them, and re-layouts: 19.5 us -> 10.4 us
  Pallas kernels: 0 us -> 7.83 us
  matrix products: 5.3 us -> 0 us
    ppermute x4 -> x18, waiting for transfers between devices: 7.08 us -> 30.5 us  [the longest x15 24.4 us: swapped(): lax.ppermute(value, 'strm', [(i, i ^ distance) for i in range(streams)])]
    all_gather x3 -> x0, blocking collectives: 19.2 us -> none  [the longest x1 7.65 us: body(): everything = lax.all_gather(own_bordered, 'strm', axis=0, tiled=True)]
    slice x26 -> x0, local copies, waits for them, and re-layouts: 8.77 us -> none  [the longest x20 6.46 us: causal_conv(): kernel = weight[frame_tap, row_tap].reshape(3 * channels, outputs)]
    pallas_call x0 -> x3, Pallas kernels: none -> 7.83 us  [the longest x1 3.86 us: body(): pl.pallas_call(functools.partial(second_kernel, frames, columns), out_sha...]
    all_to_all x1 -> x0, blocking collectives: 6.39 us -> none  [body(): lax.all_to_all(sent_two, 'strm', split_axis=0, concat_axis=3, tiled=True)]
    dot_general x18 -> x0, matrix products: 5.3 us -> none  [causal_conv(): jnp.dot(stacked.reshape(-1, 3 * channels), kernel, preferred_element_type...]
    unnamed x25 -> x30, local copies, waits for them, and re-layouts: 3.9 us -> 8.98 us
    concatenate x23 -> x0, other arithmetic: 4.32 us -> none  [the longest x16 2.37 us: causal_conv(): jnp.concatenate([window[:, :, :, col_tap:col_tap + columns] for col_tap i...]
  transfers between devices with their start and end apart: 5 -> 18, of which waited for: 3 -> 6; matrix products, arithmetic and copies ran while one was open for 15% -> 2% of each run, Pallas kernels for 0% -> 6%
where the time goes in v1:
time: 64.9 us; the launch traced here: 64.4 us
  waiting for transfers between devices  30.5 us (47%)
  starting transfers between devices  15.5 us (24%)
  local copies, waits for them, and re-layouts  10.4 us (16%)
  Pallas kernels  7.83 us (12%)
    ppermute x15, waiting for transfers between devices, swapped(): lax.ppermute(value, 'strm', [(i, i ^ distance) for i in range(streams)])  24.4 us
    unnamed x30, local copies, waits for them, and re-layouts  8.98 us
    ppermute x15, starting transfers between devices, swapped(): lax.ppermute(value, 'strm', [(i, i ^ distance) for i in range(streams)])  8.38 us
    ppermute x3, starting transfers between devices, along(): return lax.ppermute(value, ('band', 'strm'), pairs)  7.12 us
    ppermute x3, waiting for transfers between devices, along(): return lax.ppermute(value, ('band', 'strm'), pairs)  6.11 us
    pallas_call x1, Pallas kernels, body(): pl.pallas_call(functools.partial(second_kernel, frames, columns), out_sha...  3.86 us
    pallas_call x1, Pallas kernels, body(): pl.pallas_call(functools.partial(first_kernel, frames, columns), out_shap...  2.26 us
    pallas_call x1, Pallas kernels, body(): pl.pallas_call(functools.partial(sum_kernel, half), out_shape=[pair, pair...  1.7 us
  transfers between devices with their start and end apart: 18, of which 6 were waited for; matrix products, arithmetic and copies ran while one was open for 2% of the time, Pallas kernels for 6%

profile of v1, /device:TPU:0, one launch (start us, length us, event | category | flops | bytes accessed | tf_op | source)
XLA Modules:
  0.0 64.4 jit_solution(312201944622013460)
XLA Ops:
  0.0 2.9 %collective-permute-start.16 = (bf16[3,3,3,48,192]{4,3,2,1,0:T(8,128)(2,1)}, bf16[3,3,3,48,192]{4,3,2,1,0:T(8,128)(2,1)S(1)}, u32[]{:S(2)}, u32[]{:S(2)}) collective-permute-start(bf16[3,3,3,48,192]{4,3,2,1,0:T(8,128)(2,1)} %bitcast.6), channel_id=1, source_target_pairs={{0,2},{1,3},{2,0},{3,1},{4,6},{5,7},{6,4},{7,5},{8,10},{9,11},{10,... | collective-permute-start | bytes 1493000 | tf_op jit(solution)/shard_map/ppermute | solution.py:213
  2.9 0.0 collective-permute-start.15
  2.9 15.1 %collective-permute-done.16.refs_9_ = bf16[3,3,3,48,192]{4,3,2,1,0:T(8,128)(2,1)S(1)} collective-permute-done((bf16[3,3,3,48,192]{4,3,2,1,0:T(8,128)(2,1)}, bf16[3,3,3,48,192]{4,3,2,1,0:T(8,128)(2,1)S(1)}, u32[]{:S(2)}, u32[]{:S(2)}) %collective-permute-start.16) | collective-permute-done | bytes 497696 | tf_op jit(solution)/shard_map/ppermute | solution.py:213
  18.1 0.0 collective-permute-start.17
  18.1 0.5 collective-permute-start
  18.6 1.7 %collective-permute-start.1 = (bf16[1,2,1,16,384]{4,3,2,1,0:T(8,128)(2,1)}, bf16[1,2,1,16,384]{4,3,2,1,0:T(8,128)(2,1)S(1)}, u32[]{:S(2)}, u32[]{:S(2)}) collective-permute-start(bf16[1,2,1,16,384]{4,3,2,1,0:T(8,128)(2,1)} %refs_0_.1), channel_id=1, source_target_pairs={{0,2},{1,3},{2,0},{3,1},{4,6},{5,7},{6,4},{7,5},{8,10},{9,11},{10,... | collective-permute-start | bytes 73736 | tf_op jit(solution)/shard_map/ppermute | solution.py:213
  20.3 0.3 collective-permute-start.7
  20.6 0.0 collective-permute-done.refs_1_
  20.6 0.0 collective-permute-start.3
  20.6 2.0 %collective-permute-done.1.refs_2_ = bf16[1,2,1,16,384]{4,3,2,1,0:T(8,128)(2,1)S(1)} collective-permute-done((bf16[1,2,1,16,384]{4,3,2,1,0:T(8,128)(2,1)}, bf16[1,2,1,16,384]{4,3,2,1,0:T(8,128)(2,1)S(1)}, u32[]{:S(2)}, u32[]{:S(2)}) %collective-permute-start.1) | collective-permute-done | bytes 24608 | tf_op jit(solution)/shard_map/ppermute | solution.py:213
  22.6 1.7 %collective-permute-start.4 = (bf16[1,2,1,16,384]{4,3,2,1,0:T(8,128)(2,1)}, bf16[1,2,1,16,384]{4,3,2,1,0:T(8,128)(2,1)S(1)}, u32[]{:S(2)}, u32[]{:S(2)}) collective-permute-start(bf16[1,2,1,16,384]{4,3,2,1,0:T(8,128)(2,1)} %refs_4_.1), channel_id=1, source_target_pairs={{0,2},{1,3},{2,0},{3,1},{4,6},{5,7},{6,4},{7,5},{8,10},{9,11},{10,... | collective-permute-start | bytes 73736 | tf_op jit(solution)/shard_map/ppermute | solution.py:213
  24.3 0.0 collective-permute-done.3.refs_5_
  24.4 2.3 %collective-permute-done.4.refs_6_ = bf16[1,2,1,16,384]{4,3,2,1,0:T(8,128)(2,1)S(1)} collective-permute-done((bf16[1,2,1,16,384]{4,3,2,1,0:T(8,128)(2,1)}, bf16[1,2,1,16,384]{4,3,2,1,0:T(8,128)(2,1)S(1)}, u32[]{:S(2)}, u32[]{:S(2)}) %collective-permute-start.4) | collective-permute-done | bytes 24608 | tf_op jit(solution)/shard_map/ppermute | solution.py:213
  26.6 0.0 collective-permute-start.6
  26.6 0.0 collective-permute-done.7.refs_10_
  26.6 0.5 collective-permute-start.8
  27.2 0.0 collective-permute-done.2.refs_3_
  27.2 0.1 collective-permute-start.5
  27.2 0.7 %reshape.6.refs_12_ = f32[1,384]{1,0:T(1,128)S(1)} reshape(f32[384]{0:T(512)} %param.12) | data formatting | bytes 3072 | tf_op jit(solution)/shard_map/reshape | solution.py:249
  27.9 0.7 %concatenate.3.meta = s32[11]{0:T(128)S(1)} concatenate(s32[4]{0:T(128)} %param.16, s32[4]{0:T(128)} %param.17, s32[1]{0:T(128)} %bitcast, s32[1]{0:T(128)} %bitcast.1, s32[1]{0:T(128)} %constant.8.clone.1), dimensions={0} | concatenate | bytes 88 | tf_op jit(solution)/shard_map/concatenate | solution.py:210
  28.7 0.0 collective-permute-done.8.refs_11_
  28.7 0.0 copy-start
  28.7 2.1 %copy-done = bf16[3,3,3,384,192]{3,4,2,1,0:T(8,128)(2,1)S(1)} copy-done((bf16[3,3,3,384,192]{3,4,2,1,0:T(8,128)(2,1)S(1)}, bf16[3,3,3,384,192]{3,4,2,1,0:T(8,128)(2,1)}, u32[]{:S(2)}) %copy-start) | copy-done | bytes 3981336
  30.8 0.8 %copy-done.7 = bf16[1,2,2,32,192]{4,3,2,1,0:T(8,128)(2,1)S(1)} copy-done((bf16[1,2,2,32,192]{4,3,2,1,0:T(8,128)(2,1)S(1)}, bf16[1,2,2,32,192]{4,3,2,1,0:T(8,128)(2,1)}, u32[]{:S(2)}) %copy-start.7) | copy-done | bytes 49176
  31.7 0.7 %copy-done.9 = bf16[1,2,1,16,384]{4,3,2,1,0:T(8,128)(2,1)S(1)} copy-done((bf16[1,2,1,16,384]{4,3,2,1,0:T(8,128)(2,1)S(1)}, bf16[1,2,1,16,384]{4,3,2,1,0:T(8,128)(2,1)}, u32[]{:S(2)}) %copy-start.9) | copy-done | bytes 24600
  32.4 0.7 %copy-done.10 = bf16[1,2,1,16,384]{4,3,2,1,0:T(8,128)(2,1)S(1)} copy-done((bf16[1,2,1,16,384]{4,3,2,1,0:T(8,128)(2,1)S(1)}, bf16[1,2,1,16,384]{4,3,2,1,0:T(8,128)(2,1)}, u32[]{:S(2)}) %copy-start.10) | copy-done | bytes 24600
  33.1 2.3 %first_conv.1 = (bf16[160,384]{1,0:T(8,128)(2,1)S(1)}, bf16[96,384]{1,0:T(8,128)(2,1)S(1)}, bf16[64,384]{1,0:T(8,128)(2,1)S(1)}, f32[128,384]{1,0:T(8,128)S(1)}, bf16[2,2,32,192]{3,2,1,0:T(8,128)(2,1)S(1)}) custom-call(s32[11]{0:T(128)S(1)} %concatenate.3.meta, bf16[1,2,1,16,384]{4,3,2,1,0:T(8,128)(2,1)S(1)} %copy-done.9, ...), custom_call_target="tpu_custom_call" | custom-call | tf_op jit(solution)/shard_map/first_conv/pallas_call | solution.py:232
  35.4 0.7 %copy-done.6 = f32[128,384]{1,0:T(8,128)} copy-done((f32[128,384]{1,0:T(8,128)}, f32[128,384]{1,0:T(8,128)S(1)}, u32[]{:S(2)}) %copy-start.6) | copy-done | bytes 196632
  36.1 1.3 %collective-permute-start.9 = (bf16[160,384]{1,0:T(8,128)(2,1)S(1)}, bf16[160,384]{1,0:T(8,128)(2,1)S(1)}, u32[]{:S(2)}, u32[]{:S(2)}) collective-permute-start(bf16[160,384]{1,0:T(8,128)(2,1)S(1)} %get-tuple-element.13), channel_id=1, source_target_pairs={{2,6},{3,7},{4,0},{5,1},{6,10},{7,11},{8,4},{9,5},{10,14},{11,15},... | collective-permute-start | bytes 368648 | tf_op jit(solution)/shard_map/ppermute | solution.py:222
  37.4 4.5 %collective-permute-start.10 = (bf16[96,384]{1,0:T(8,128)(2,1)S(1)}, bf16[96,384]{1,0:T(8,128)(2,1)S(1)}, u32[]{:S(2)}, u32[]{:S(2)}) collective-permute-start(bf16[96,384]{1,0:T(8,128)(2,1)S(1)} %get-tuple-element.14), channel_id=1, source_target_pairs={{0,4},{1,5},{4,8},{5,9},{6,2},{7,3},{8,12},{9,13},{10,6},{11,7},{1... | collective-permute-start | bytes 221192 | tf_op jit(solution)/shard_map/ppermute | solution.py:222
  41.9 1.3 %collective-permute-start.11 = (bf16[64,384]{1,0:T(8,128)(2,1)S(1)}, bf16[64,384]{1,0:T(8,128)(2,1)S(1)}, u32[]{:S(2)}, u32[]{:S(2)}) collective-permute-start(bf16[64,384]{1,0:T(8,128)(2,1)S(1)} %get-tuple-element.15), channel_id=1, source_target_pairs={{2,10},{3,11},{6,14},{7,15},{8,0},{9,1},{12,4},{13,5},{18,26},{19,... | collective-permute-start | bytes 147464 | tf_op jit(solution)/shard_map/ppermute | solution.py:222
  43.2 6.1 %collective-permute-done.11.two = bf16[64,384]{1,0:T(8,128)(2,1)S(1)} collective-permute-done((bf16[64,384]{1,0:T(8,128)(2,1)S(1)}, bf16[64,384]{1,0:T(8,128)(2,1)S(1)}, u32[]{:S(2)}, u32[]{:S(2)}) %collective-permute-start.11) | collective-permute-done | bytes 49184 | tf_op jit(solution)/shard_map/ppermute | solution.py:222
  49.3 0.0 collective-permute-done.10.near.refs_6_
  49.3 0.0 collective-permute-done.9.far.refs_5_
  49.4 0.6 copy-done.14
  50.0 0.0 copy-done.4
  50.0 0.1 copy-done.2
  50.0 1.7 %row_sums.1 = (bf16[64,384]{1,0:T(8,128)(2,1)}, bf16[64,384]{1,0:T(8,128)(2,1)}) custom-call(s32[11]{0:T(128)} %copy-done.11, f32[128,384]{1,0:T(8,128)} %copy-done.6, bf16[160,384]{1,0:T(8,128)(2,1)} %copy-done.2, bf16[96,384]{1,0:T(8,128)(2,1)} %copy-done.4, bf16[64,384]{1,0:T(8,128)(2,1)} %copy-done.14), custom_call_target="tpu_custom_call" | custom-call | tf_op jit(solution)/shard_map/row_sums/pallas_call | solution.py:252
  51.7 0.6 collective-permute-start.13
  52.3 3.7 %collective-permute-done.13.refs_2_ = bf16[64,384]{1,0:T(8,128)(2,1)S(1)} collective-permute-done((bf16[64,384]{1,0:T(8,128)(2,1)}, bf16[64,384]{1,0:T(8,128)(2,1)S(1)}, u32[]{:S(2)}, u32[]{:S(2)}) %collective-permute-start.13) | collective-permute-done | bytes 49184 | tf_op jit(solution)/shard_map/ppermute | solution.py:213
  56.0 0.0 collective-permute-done.12.refs_1_
  56.0 1.2 %collective-permute-done.14.refs_3_ = bf16[64,384]{1,0:T(8,128)(2,1)S(1)} collective-permute-done((bf16[64,384]{1,0:T(8,128)(2,1)S(1)}, bf16[64,384]{1,0:T(8,128)(2,1)S(1)}, u32[]{:S(2)}, u32[]{:S(2)}) %collective-permute-start.14) | collective-permute-done | bytes 49184 | tf_op jit(solution)/shard_map/ppermute | solution.py:213
  57.3 0.0 collective-permute-done.17.refs_10_
  57.3 0.9 %copy-done.3 = bf16[160,384]{1,0:T(8,128)(2,1)S(1)} copy-done((bf16[160,384]{1,0:T(8,128)(2,1)S(1)}, bf16[160,384]{1,0:T(8,128)(2,1)}, u32[]{:S(2)}) %copy-start.3) | copy-done | bytes 122904
  58.2 0.9 %copy-done.5 = bf16[96,384]{1,0:T(8,128)(2,1)S(1)} copy-done((bf16[96,384]{1,0:T(8,128)(2,1)S(1)}, bf16[96,384]{1,0:T(8,128)(2,1)}, u32[]{:S(2)}) %copy-start.5) | copy-done | bytes 73752
  59.1 0.8 %copy-done.8 = bf16[64,384]{1,0:T(8,128)(2,1)S(1)} copy-done((bf16[64,384]{1,0:T(8,128)(2,1)S(1)}, bf16[64,384]{1,0:T(8,128)(2,1)}, u32[]{:S(2)}) %copy-start.8) | copy-done | bytes 49176
  59.9 0.6 copy-done.12
  60.5 3.9 %second_conv.1 = bf16[1,2,2,32,192]{4,3,2,1,0:T(8,128)(2,1)} custom-call(s32[11]{0:T(128)S(1)} %copy-done.12, bf16[64,384]{1,0:T(8,128)(2,1)S(1)} %copy-done.8, bf16[64,384]{1,0:T(8,128)(2,1)S(1)} %collective-permute-done.12.refs_1_, bf16[64,384]{1,0:T(8,128)(2,1)S(1)} %collective-permute-done.13.refs_2_, ...), custom_call_target="tpu_custom_call" | custom-call | tf_op jit(solution)/shard_map/second_conv/pallas_call | solution.py:261
  (23 shorter events, 0.0 us)
Async XLA Ops:
  0.0 57.3 %copy-start.13 = (f32[192]{0:T(256)S(1)}, f32[192]{0:T(256)}, u32[]{:S(2)}) copy-start(f32[192]{0:T(256)} %param.13) | copy-start | bytes 2308
  0.0 18.1 %collective-permute-start.16 = (bf16[3,3,3,48,192]{4,3,2,1,0:T(8,128)(2,1)}, bf16[3,3,3,48,192]{4,3,2,1,0:T(8,128)(2,1)S(1)}, u32[]{:S(2)}, u32[]{:S(2)}) collective-permute-start(bf16[3,3,3,48,192]{4,3,2,1,0:T(8,128)(2,1)} %bitcast.6), channel_id=1, source_target_pairs={{0,2},{1,3},{2,0},{3,1},{4,6},{5,7},{6,4},{7,5},{8,10},{9,11},{10,... | collective-permute-start | bytes 1493000 | tf_op jit(solution)/shard_map/ppermute | solution.py:213
  2.9 54.3 %collective-permute-start.15 = (bf16[3,3,3,48,192]{4,3,2,1,0:T(8,128)(2,1)}, bf16[3,3,3,48,192]{4,3,2,1,0:T(8,128)(2,1)S(1)}, u32[]{:S(2)}, u32[]{:S(2)}) collective-permute-start(bf16[3,3,3,48,192]{4,3,2,1,0:T(8,128)(2,1)} %bitcast.7), channel_id=1, source_target_pairs={{0,1},{1,0},{2,3},{3,2},{4,5},{5,4},{6,7},{7,6},{8,9},{9,8},{10,11... | collective-permute-start | bytes 1493000 | tf_op jit(solution)/shard_map/ppermute | solution.py:213
  18.1 39.2 %collective-permute-start.17 = (bf16[3,3,3,48,192]{4,3,2,1,0:T(8,128)(2,1)S(1)}, bf16[3,3,3,48,192]{4,3,2,1,0:T(8,128)(2,1)S(1)}, u32[]{:S(2)}, u32[]{:S(2)}) collective-permute-start(bf16[3,3,3,48,192]{4,3,2,1,0:T(8,128)(2,1)S(1)} %collective-permute-done.16.refs_9_), channel_id=1, source_target_pairs={{0,1},{1,0},{2,3},{3,2},{4,5},{5,4},{6,7},{7,6},{8,9},{9,8},{10,11... | collective-permute-start | bytes 1493000 | tf_op jit(solution)/shard_map/ppermute | solution.py:213
  18.1 2.5 %collective-permute-start = (bf16[1,2,1,16,384]{4,3,2,1,0:T(8,128)(2,1)}, bf16[1,2,1,16,384]{4,3,2,1,0:T(8,128)(2,1)S(1)}, u32[]{:S(2)}, u32[]{:S(2)}) collective-permute-start(bf16[1,2,1,16,384]{4,3,2,1,0:T(8,128)(2,1)} %refs_0_.1), channel_id=1, source_target_pairs={{0,1},{1,0},{2,3},{3,2},{4,5},{5,4},{6,7},{7,6},{8,9},{9,8},{10,11... | collective-permute-start | bytes 73736 | tf_op jit(solution)/shard_map/ppermute | solution.py:213
  18.6 4.0 %collective-permute-start.1 = (bf16[1,2,1,16,384]{4,3,2,1,0:T(8,128)(2,1)}, bf16[1,2,1,16,384]{4,3,2,1,0:T(8,128)(2,1)S(1)}, u32[]{:S(2)}, u32[]{:S(2)}) collective-permute-start(bf16[1,2,1,16,384]{4,3,2,1,0:T(8,128)(2,1)} %refs_0_.1), channel_id=1, source_target_pairs={{0,2},{1,3},{2,0},{3,1},{4,6},{5,7},{6,4},{7,5},{8,10},{9,11},{10,... | collective-permute-start | bytes 73736 | tf_op jit(solution)/shard_map/ppermute | solution.py:213
  20.3 6.3 %collective-permute-start.7 = (bf16[1,2,2,32,192]{4,3,2,1,0:T(8,128)(2,1)}, bf16[1,2,2,32,192]{4,3,2,1,0:T(8,128)(2,1)S(1)}, u32[]{:S(2)}, u32[]{:S(2)}) collective-permute-start(bf16[1,2,2,32,192]{4,3,2,1,0:T(8,128)(2,1)} %refs_8_.1), channel_id=1, source_target_pairs={{0,2},{1,3},{2,0},{3,1},{4,6},{5,7},{6,4},{7,5},{8,10},{9,11},{10,... | collective-permute-start | bytes 147464 | tf_op jit(solution)/shard_map/ppermute | solution.py:213
  20.6 3.8 %collective-permute-start.3 = (bf16[1,2,1,16,384]{4,3,2,1,0:T(8,128)(2,1)}, bf16[1,2,1,16,384]{4,3,2,1,0:T(8,128)(2,1)S(1)}, u32[]{:S(2)}, u32[]{:S(2)}) collective-permute-start(bf16[1,2,1,16,384]{4,3,2,1,0:T(8,128)(2,1)} %refs_4_.1), channel_id=1, source_target_pairs={{0,1},{1,0},{2,3},{3,2},{4,5},{5,4},{6,7},{7,6},{8,9},{9,8},{10,11... | collective-permute-start | bytes 73736 | tf_op jit(solution)/shard_map/ppermute | solution.py:213
  22.6 4.0 %collective-permute-start.4 = (bf16[1,2,1,16,384]{4,3,2,1,0:T(8,128)(2,1)}, bf16[1,2,1,16,384]{4,3,2,1,0:T(8,128)(2,1)S(1)}, u32[]{:S(2)}, u32[]{:S(2)}) collective-permute-start(bf16[1,2,1,16,384]{4,3,2,1,0:T(8,128)(2,1)} %refs_4_.1), channel_id=1, source_target_pairs={{0,2},{1,3},{2,0},{3,1},{4,6},{5,7},{6,4},{7,5},{8,10},{9,11},{10,... | collective-permute-start | bytes 73736 | tf_op jit(solution)/shard_map/ppermute | solution.py:213
  24.4 2.8 %collective-permute-start.2 = (bf16[1,2,1,16,384]{4,3,2,1,0:T(8,128)(2,1)S(1)}, bf16[1,2,1,16,384]{4,3,2,1,0:T(8,128)(2,1)S(1)}, u32[]{:S(2)}, u32[]{:S(2)}) collective-permute-start(bf16[1,2,1,16,384]{4,3,2,1,0:T(8,128)(2,1)S(1)} %collective-permute-done.1.refs_2_), channel_id=1, source_target_pairs={{0,1},{1,0},{2,3},{3,2},{4,5},{5,4},{6,7},{7,6},{8,9},{9,8},{10,11... | collective-permute-start | bytes 73736 | tf_op jit(solution)/shard_map/ppermute | solution.py:213
  26.6 2.0 %collective-permute-start.6 = (bf16[1,2,2,32,192]{4,3,2,1,0:T(8,128)(2,1)}, bf16[1,2,2,32,192]{4,3,2,1,0:T(8,128)(2,1)S(1)}, u32[]{:S(2)}, u32[]{:S(2)}) collective-permute-start(bf16[1,2,2,32,192]{4,3,2,1,0:T(8,128)(2,1)} %refs_8_.1), channel_id=1, source_target_pairs={{0,1},{1,0},{2,3},{3,2},{4,5},{5,4},{6,7},{7,6},{8,9},{9,8},{10,11... | collective-permute-start | bytes 147464 | tf_op jit(solution)/shard_map/ppermute | solution.py:213
  26.6 2.0 %collective-permute-start.8 = (bf16[1,2,2,32,192]{4,3,2,1,0:T(8,128)(2,1)S(1)}, bf16[1,2,2,32,192]{4,3,2,1,0:T(8,128)(2,1)S(1)}, u32[]{:S(2)}, u32[]{:S(2)}) collective-permute-start(bf16[1,2,2,32,192]{4,3,2,1,0:T(8,128)(2,1)S(1)} %collective-permute-done.7.refs_10_), channel_id=1, source_target_pairs={{0,1},{1,0},{2,3},{3,2},{4,5},{5,4},{6,7},{7,6},{8,9},{9,8},{10,11... | collective-permute-start | bytes 147464 | tf_op jit(solution)/shard_map/ppermute | solution.py:213
  27.2 1.5 %collective-permute-start.5 = (bf16[1,2,1,16,384]{4,3,2,1,0:T(8,128)(2,1)S(1)}, bf16[1,2,1,16,384]{4,3,2,1,0:T(8,128)(2,1)S(1)}, u32[]{:S(2)}, u32[]{:S(2)}) collective-permute-start(bf16[1,2,1,16,384]{4,3,2,1,0:T(8,128)(2,1)S(1)} %collective-permute-done.4.refs_6_), channel_id=1, source_target_pairs={{0,1},{1,0},{2,3},{3,2},{4,5},{5,4},{6,7},{7,6},{8,9},{9,8},{10,11... | collective-permute-start | bytes 73736 | tf_op jit(solution)/shard_map/ppermute | solution.py:213
  28.7 20.7 %copy-start.11 = (s32[11]{0:T(128)}, s32[11]{0:T(128)S(1)}, u32[]{:S(2)}) copy-start(s32[11]{0:T(128)S(1)} %concatenate.3.meta) | copy-start | bytes 136
  28.7 2.1 %copy-start = (bf16[3,3,3,384,192]{3,4,2,1,0:T(8,128)(2,1)S(1)}, bf16[3,3,3,384,192]{3,4,2,1,0:T(8,128)(2,1)}, u32[]{:S(2)}) copy-start(bf16[3,3,3,384,192]{3,4,2,1,0:T(8,128)(2,1)} %param.14) | copy-start | bytes 11943940
  30.8 0.8 %copy-start.7 = (bf16[1,2,2,32,192]{4,3,2,1,0:T(8,128)(2,1)S(1)}, bf16[1,2,2,32,192]{4,3,2,1,0:T(8,128)(2,1)}, u32[]{:S(2)}) copy-start(bf16[1,2,2,32,192]{4,3,2,1,0:T(8,128)(2,1)} %refs_8_.1) | copy-start | bytes 147460
  31.7 0.7 %copy-start.9 = (bf16[1,2,1,16,384]{4,3,2,1,0:T(8,128)(2,1)S(1)}, bf16[1,2,1,16,384]{4,3,2,1,0:T(8,128)(2,1)}, u32[]{:S(2)}) copy-start(bf16[1,2,1,16,384]{4,3,2,1,0:T(8,128)(2,1)} %refs_0_.1) | copy-start | bytes 73732
  32.4 0.7 %copy-start.10 = (bf16[1,2,1,16,384]{4,3,2,1,0:T(8,128)(2,1)S(1)}, bf16[1,2,1,16,384]{4,3,2,1,0:T(8,128)(2,1)}, u32[]{:S(2)}) copy-start(bf16[1,2,1,16,384]{4,3,2,1,0:T(8,128)(2,1)} %refs_4_.1) | copy-start | bytes 73732
  33.1 24.1 %copy-start.1 = (bf16[3,3,3,192,48]{3,4,2,1,0:T(8,128)(2,1)S(1)}, bf16[3,3,3,192,48]{3,4,2,1,0:T(8,128)(2,1)}, u32[]{:S(2)}) copy-start(bf16[3,3,3,192,48]{3,4,2,1,0:T(8,128)(2,1)} %param.15) | copy-start | bytes 1492996
  35.4 0.7 %copy-start.6 = (f32[128,384]{1,0:T(8,128)}, f32[128,384]{1,0:T(8,128)S(1)}, u32[]{:S(2)}) copy-start(f32[128,384]{1,0:T(8,128)S(1)} %get-tuple-element.12.own) | copy-start | bytes 589828
  36.1 13.3 %collective-permute-start.9 = (bf16[160,384]{1,0:T(8,128)(2,1)S(1)}, bf16[160,384]{1,0:T(8,128)(2,1)S(1)}, u32[]{:S(2)}, u32[]{:S(2)}) collective-permute-start(bf16[160,384]{1,0:T(8,128)(2,1)S(1)} %get-tuple-element.13), channel_id=1, source_target_pairs={{2,6},{3,7},{4,0},{5,1},{6,10},{7,11},{8,4},{9,5},{10,14},{11,15},... | collective-permute-start | bytes 368648 | tf_op jit(solution)/shard_map/ppermute | solution.py:222
  37.4 12.0 %collective-permute-start.10 = (bf16[96,384]{1,0:T(8,128)(2,1)S(1)}, bf16[96,384]{1,0:T(8,128)(2,1)S(1)}, u32[]{:S(2)}, u32[]{:S(2)}) collective-permute-start(bf16[96,384]{1,0:T(8,128)(2,1)S(1)} %get-tuple-element.14), channel_id=1, source_target_pairs={{0,4},{1,5},{4,8},{5,9},{6,2},{7,3},{8,12},{9,13},{10,6},{11,7},{1... | collective-permute-start | bytes 221192 | tf_op jit(solution)/shard_map/ppermute | solution.py:222
  41.9 7.4 %collective-permute-start.11 = (bf16[64,384]{1,0:T(8,128)(2,1)S(1)}, bf16[64,384]{1,0:T(8,128)(2,1)S(1)}, u32[]{:S(2)}, u32[]{:S(2)}) collective-permute-start(bf16[64,384]{1,0:T(8,128)(2,1)S(1)} %get-tuple-element.15), channel_id=1, source_target_pairs={{2,10},{3,11},{6,14},{7,15},{8,0},{9,1},{12,4},{13,5},{18,26},{19,... | collective-permute-start | bytes 147464 | tf_op jit(solution)/shard_map/ppermute | solution.py:222
  49.3 0.6 copy-start.14
  49.3 0.6 copy-start.4
  49.4 0.7 %copy-start.2 = (bf16[160,384]{1,0:T(8,128)(2,1)}, bf16[160,384]{1,0:T(8,128)(2,1)S(1)}, u32[]{:S(2)}) copy-start(bf16[160,384]{1,0:T(8,128)(2,1)S(1)} %collective-permute-done.9.far.refs_5_) | copy-start | bytes 368644
  51.7 4.3 %collective-permute-start.13 = (bf16[64,384]{1,0:T(8,128)(2,1)}, bf16[64,384]{1,0:T(8,128)(2,1)S(1)}, u32[]{:S(2)}, u32[]{:S(2)}) collective-permute-start(bf16[64,384]{1,0:T(8,128)(2,1)} %get-tuple-element.17), channel_id=1, source_target_pairs={{0,2},{1,3},{2,0},{3,1},{4,6},{5,7},{6,4},{7,5},{8,10},{9,11},{10,... | collective-permute-start | bytes 147464 | tf_op jit(solution)/shard_map/ppermute | solution.py:213
  52.3 3.7 %collective-permute-start.12 = (bf16[64,384]{1,0:T(8,128)(2,1)}, bf16[64,384]{1,0:T(8,128)(2,1)S(1)}, u32[]{:S(2)}, u32[]{:S(2)}) collective-permute-start(bf16[64,384]{1,0:T(8,128)(2,1)} %get-tuple-element.16.refs_0_), channel_id=1, source_target_pairs={{0,1},{1,0},{2,3},{3,2},{4,5},{5,4},{6,7},{7,6},{8,9},{9,8},{10,11... | collective-permute-start | bytes 147464 | tf_op jit(solution)/shard_map/ppermute | solution.py:213
  56.0 1.2 %collective-permute-start.14 = (bf16[64,384]{1,0:T(8,128)(2,1)S(1)}, bf16[64,384]{1,0:T(8,128)(2,1)S(1)}, u32[]{:S(2)}, u32[]{:S(2)}) collective-permute-start(bf16[64,384]{1,0:T(8,128)(2,1)S(1)} %collective-permute-done.13.refs_2_), channel_id=1, source_target_pairs={{0,1},{1,0},{2,3},{3,2},{4,5},{5,4},{6,7},{7,6},{8,9},{9,8},{10,11... | collective-permute-start | bytes 147464 | tf_op jit(solution)/shard_map/ppermute | solution.py:213
  57.3 0.9 %copy-start.3 = (bf16[160,384]{1,0:T(8,128)(2,1)S(1)}, bf16[160,384]{1,0:T(8,128)(2,1)}, u32[]{:S(2)}) copy-start(bf16[160,384]{1,0:T(8,128)(2,1)} %copy-done.2) | copy-start | bytes 368644
  58.2 0.9 %copy-start.5 = (bf16[96,384]{1,0:T(8,128)(2,1)S(1)}, bf16[96,384]{1,0:T(8,128)(2,1)}, u32[]{:S(2)}) copy-start(bf16[96,384]{1,0:T(8,128)(2,1)} %copy-done.4) | copy-start | bytes 221188
  59.1 0.8 %copy-start.8 = (bf16[64,384]{1,0:T(8,128)(2,1)S(1)}, bf16[64,384]{1,0:T(8,128)(2,1)}, u32[]{:S(2)}) copy-start(bf16[64,384]{1,0:T(8,128)(2,1)} %get-tuple-element.16.refs_0_) | copy-start | bytes 147460
  59.9 0.6 copy-start.12

commit v2 on v1

--- a/solution.py
+++ b/solution.py
@@ -30,26 +30,42 @@
     return left, values, right
 
 
-def first_kernel(frames, columns, meta, *refs):
+def first_kernel(frames, columns, *refs):
     latents, firsts, seconds = refs[0:4], refs[4:8], refs[8:12]
-    gain, weight = refs[12:14]
-    far, near, two, own, mid = refs[14:19]
-    slot_first, slot_second = refs[19:21]
-    me = meta[8]
+    gain_there, weight_there, slots_there, blocks_there = refs[12:16]
+    far, near, two, own, mid = refs[16:21]
+    slot_first, slot_second, latent_here, weight, gain, slots, blocks, sems = refs[21:29]
+    me = lax.axis_index("strm")
     upper = me // 2 == 0
     channels = latents[0].shape[-1]
     outputs = weight.shape[-2]
-    for d in range(4):
+    loads = [
+        pltpu.make_async_copy(latents[0], latent_here, sems.at[0]),
+        pltpu.make_async_copy(firsts[0].at[0, :, 0], slot_first.at[me], sems.at[1]),
+        pltpu.make_async_copy(seconds[0].at[0], slot_second.at[me], sems.at[2]),
+        pltpu.make_async_copy(gain_there, gain, sems.at[3]),
+        pltpu.make_async_copy(slots_there, slots, sems.at[4]),
+        pltpu.make_async_copy(blocks_there, blocks, sems.at[5]),
+    ]
+    for load in loads:
+        load.start()
+    weight_loads = [pltpu.make_async_copy(weight_there.at[i], weight.at[i], sems.at[6 + i]) for i in range(3)]
+    for load in weight_loads:
+        load.start()
+    for d in range(1, 4):
         slot_first[me ^ d] = firsts[d][...].reshape(2, columns, channels)
         slot_second[me ^ d] = seconds[d][0]
+    for load in loads:
+        load.wait()
 
     parts = []
     for d in range(4):
         stream = me ^ d
-        chosen = slot_first[meta[stream]].astype(f32)
-        chosen = jnp.where(meta[4 + stream] > 0, chosen, 0.0)
-        fresh = latents[d][...].reshape(frames * columns, channels).astype(f32)
-        parts += [chosen.reshape(2 * columns, channels), norm_silu(fresh, gain[...])]
+        chosen = slot_first[slots[stream]].astype(f32)
+        chosen = jnp.where(blocks[stream] > 0, chosen, 0.0)
+        source = latents[d] if d else latent_here
+        fresh = source[...].reshape(frames * columns, channels).astype(f32)
+        parts += [chosen.reshape(2 * columns, channels), norm_silu(fresh, gain[...][None, :])]
     views = [
         view.astype(bf16).reshape(4, frames + 2, columns, channels)
         for view in shifted(jnp.concatenate(parts, axis=0), columns)
@@ -58,6 +74,7 @@
     sums = [jnp.zeros((rows, outputs), f32) for _ in range(3)]
     taps = [jnp.where(upper, 2, 0), 1, jnp.where(upper, 0, 2)]
     for i in range(3):
+        weight_loads[i].wait()
         for l in range(3):
             window = views[l][:, i : i + frames].reshape(rows, channels)
             for j in range(3):
@@ -82,8 +99,8 @@
         own[at, :] = v[p]
         own[after, :] = w[p]
 
-    chosen = slot_second[meta[me]].astype(f32)
-    chosen = jnp.where(meta[4 + me] > 0, chosen, 0.0)
+    chosen = slot_second[slots[me]].astype(f32)
+    chosen = jnp.where(blocks[me] > 0, chosen, 0.0)
     mid[...] = chosen.astype(bf16)
     edges = [jnp.concatenate([chosen[0, r], chosen[1, r]], axis=-1) for r in range(2)]
     width = 2 * columns
@@ -91,8 +108,8 @@
     near[pl.ds(2 * half, width), :] = jnp.where(upper, edges[1], edges[0]).astype(bf16)
 
 
-def sum_kernel(half, meta, own, far, near, two, first_pair, second_pair):
-    me, place, bands = meta[8], meta[9], meta[10]
+def sum_kernel(half, own, far, near, two, first_pair, second_pair):
+    me, place, bands = lax.axis_index("strm"), lax.axis_index("band"), lax.axis_size("band")
     outside = jnp.where(me // 2 == 0, place == bands - 1, place == 0)
     for p, pair in enumerate((first_pair, second_pair)):
         at = pl.ds(p * half, half)
@@ -103,11 +120,11 @@
         pair[pl.ds(half, half), :] = jnp.where(outside, 0.0, extra).astype(bf16)
 
 
-def second_kernel(frames, columns, meta, *refs):
+def second_kernel(frames, columns, *refs):
     pairs, mid, far, near = refs[0:4], refs[4], refs[5], refs[6]
     weights, gain, out = refs[7:11], refs[11], refs[12]
     taps, quarters, sems = refs[13:16]
-    me = meta[8]
+    me = lax.axis_index("strm")
     upper = me // 2 == 0
     channels = out.shape[-1]
     group = channels // 4
@@ -130,7 +147,7 @@
     upsampled = jnp.stack(
         [jnp.stack([jnp.stack([fields[2 * a + b][c, t] for b in range(2)]) for a, c in row_of]) for t in range(frames)]
     )
-    act = norm_silu(upsampled.reshape(-1, channels), gain[...])
+    act = norm_silu(upsampled.reshape(-1, channels), gain[...][None, :])
     left, same, right = [
         v.astype(bf16).reshape(frames, 4, 2, columns, channels) for v in shifted(act, columns)
     ]
@@ -194,7 +211,11 @@
     return [pl.BlockSpec(memory_space=pltpu.VMEM)] * count
 
 
-SMEM = pl.BlockSpec(memory_space=pltpu.SMEM)
+THERE = pl.BlockSpec(memory_space=pltpu.HBM)
+
+
+def there(value):
+    return pltpu.with_memory_space_constraint(value, pltpu.HBM)
 
 
 def body(latents, cache_first, cache_second, gain_first, gain_second, w_first, w_second, cache_slot, block_index):
@@ -205,9 +226,6 @@
     assert streams == 4 and latents.shape[2] == 1 and frames == 2
     half = frames * columns
     width = 2 * columns
-    me = lax.axis_index("strm")
-    place = lax.axis_index("band")
-    meta = jnp.concatenate([cache_slot, block_index, jnp.stack([me, place, jnp.int32(bands)]).astype(jnp.int32)])
 
     def swapped(value, distance):
         return lax.ppermute(value, "strm", [(i, i ^ distance) for i in range(streams)])
@@ -227,7 +245,10 @@
 
     turned_first = jnp.swapaxes(w_first, 3, 4)
     turned_second = jnp.swapaxes(w_second, 3, 4)
-    args = everyone(latents) + everyone(cache_first) + everyone(cache_second)
+    firsts = everyone(cache_first)
+    args = everyone(latents) + firsts + everyone(cache_second)
+    turned_second, *_ = lax.optimization_barrier((turned_second, args[2], args[6], args[10]))
+    weights = [turned_second, swapped(turned_second, 1), swapped(turned_second, 2)]
     pair = jax.ShapeDtypeStruct((2 * half, 2 * outputs), bf16)
     far, near, two, own, mid = pl.pallas_call(
         functools.partial(first_kernel, frames, columns),
@@ -238,30 +259,44 @@
             jax.ShapeDtypeStruct((4 * half, 2 * outputs), f32),
             jax.ShapeDtypeStruct(cache_second.shape[1:], bf16),
         ],
-        in_specs=[SMEM] + whole(14),
+        in_specs=([THERE] + whole(3)) * 3 + [THERE] * 4,
         out_specs=whole(5),
         scratch_shapes=[
             pltpu.VMEM((4,) + (2, columns, channels), bf16),
             pltpu.VMEM((4,) + cache_second.shape[1:], bf16),
+            pltpu.VMEM(latents.shape, bf16),
+            pltpu.VMEM(turned_first.shape, bf16),
+            pltpu.VMEM(gain_first.shape, f32),
+            pltpu.SMEM(cache_slot.shape, jnp.int32),
+            pltpu.SMEM(block_index.shape, jnp.int32),
+            pltpu.SemaphoreType.DMA((9,)),
         ],
         compiler_params=pltpu.CompilerParams(vmem_limit_bytes=24 * 2**20),
         name="first_conv",
-    )(meta, *args, gain_first.reshape(1, -1), turned_first)
-    weights = everyone(turned_second)
+    )(
+        *[there(v) if n % 4 == 0 else v for n, v in enumerate(args)],
+        there(gain_first),
+        there(turned_first),
+        there(cache_slot),
+        there(block_index),
+    )
     far, near, two = along(far, 1), along(near, -1), along(two, 2)
     first_pair, second_pair = pl.pallas_call(
         functools.partial(sum_kernel, half),
         out_shape=[pair, pair],
-        in_specs=[SMEM] + whole(4),
+        in_specs=whole(4),
         out_specs=whole(2),
+        compiler_params=pltpu.CompilerParams(vmem_limit_bytes=8 * 2**20),
         name="row_sums",
-    )(meta, own, far, near, two)
+    )(own, far, near, two)
+    second_pair, weight_across = lax.optimization_barrier((second_pair, weights[2]))
+    weights.append(swapped(weight_across, 1))
     across = swapped(second_pair, 2)
     pairs = [first_pair, swapped(first_pair, 1), across, swapped(across, 1)]
     decoded = pl.pallas_call(
         functools.partial(second_kernel, frames, columns),
         out_shape=jax.ShapeDtypeStruct((1, frames, 2, width, outputs), bf16),
-        in_specs=[SMEM] + whole(7) + [pl.BlockSpec(memory_space=pl.ANY)] * 4 + whole(1),
+        in_specs=whole(7) + [pl.BlockSpec(memory_space=pl.ANY)] * 4 + whole(1),
         out_specs=pl.BlockSpec(memory_space=pltpu.VMEM),
         scratch_shapes=[
             pltpu.VMEM((3, 3, 3, outputs, outputs), bf16),
@@ -270,7 +305,7 @@
         ],
         compiler_params=pltpu.CompilerParams(vmem_limit_bytes=24 * 2**20),
         name="second_conv",
-    )(meta, *pairs, mid, far, near, *weights, gain_second.reshape(1, -1))
+    )(*pairs, mid, far, near, *weights, gain_second)
     return decoded
 
 

time: 64.9 us -> 37.9 us (0.58)
  waiting for transfers between devices: 30.5 us -> 14.3 us
  local copies, waits for them, and re-layouts: 10.4 us -> 0.01 us
    ppermute x15, waiting for transfers between devices: 24.4 us -> 8.4 us  [swapped(): lax.ppermute(value, 'strm', [(i, i ^ distance) for i in range(streams)])]
    unnamed x30 -> x4, local copies, waits for them, and re-layouts: 8.98 us -> 0.01 us
    pallas_call x1, Pallas kernels: 1.7 us -> 0.05 us  [body(): pl.pallas_call(functools.partial(sum_kernel, half), out_shape=[pair, pair...]
    pallas_call x1, Pallas kernels: 2.26 us -> 3.92 us  [body(): pl.pallas_call(functools.partial(first_kernel, frames, columns), out_shap...]
    concatenate x1 -> x0, local copies, waits for them, and re-layouts: 0.75 us -> none  [body(): jnp.concatenate([cache_slot, block_index, jnp.stack([me, place, jnp.int32...]
    reshape x1 -> x0, local copies, waits for them, and re-layouts: 0.68 us -> none  [body(): gain_first.reshape(1, -1)]
  transfers between devices with their start and end apart: 18 -> 18, of which waited for: 6 -> 8; matrix products, arithmetic and copies ran while one was open for 2% -> 0% of each run, Pallas kernels for 6% -> 11%
where the time goes in v2:
time: 37.9 us; the launch traced here: 37.7 us
  starting transfers between devices  16 us (42%)
  waiting for transfers between devices  14.3 us (38%)
  Pallas kernels  7.28 us (19%)
    ppermute x15, starting transfers between devices, swapped(): lax.ppermute(value, 'strm', [(i, i ^ distance) for i in range(streams)])  8.9 us
    ppermute x15, waiting for transfers between devices, swapped(): lax.ppermute(value, 'strm', [(i, i ^ distance) for i in range(streams)])  8.4 us
    ppermute x3, starting transfers between devices, along(): return lax.ppermute(value, ('band', 'strm'), pairs)  7.13 us
    ppermute x3, waiting for transfers between devices, along(): return lax.ppermute(value, ('band', 'strm'), pairs)  5.85 us
    pallas_call x1, Pallas kernels, body(): pl.pallas_call(functools.partial(first_kernel, frames, columns), out_shap...  3.92 us
    pallas_call x1, Pallas kernels, body(): pl.pallas_call(functools.partial(second_kernel, frames, columns), out_sha...  3.31 us
  transfers between devices with their start and end apart: 18, of which 8 were waited for; matrix products, arithmetic and copies ran while one was open for 0% of the time, Pallas kernels for 11%

profile of v2, /device:TPU:0, one launch (start us, length us, event | category | flops | bytes accessed | tf_op | source)
XLA Modules:
  0.0 37.7 jit_solution(10177480220447018273)
XLA Ops:
  0.0 0.0 copy-start
  0.0 0.0 copy-start.1
  0.0 2.9 %collective-permute-start.7 = (bf16[1,2,2,32,192]{4,3,2,1,0:T(8,128)(2,1)}, bf16[1,2,2,32,192]{4,3,2,1,0:T(8,128)(2,1)S(1)}, u32[]{:S(2)}, u32[]{:S(2)}) collective-permute-start(bf16[1,2,2,32,192]{4,3,2,1,0:T(8,128)(2,1)} %refs_8_.1), channel_id=1, source_target_pairs={{0,2},{1,3},{2,0},{3,1},{4,6},{5,7},{6,4},{7,5},{8,10},{9,11},{10,... | collective-permute-start | bytes 147464 | tf_op jit(solution)/shard_map/ppermute | solution.py:231
  2.9 0.1 collective-permute-start.1
  3.0 2.0 %collective-permute-start.4 = (bf16[1,2,1,16,384]{4,3,2,1,0:T(8,128)(2,1)}, bf16[1,2,1,16,384]{4,3,2,1,0:T(8,128)(2,1)S(1)}, u32[]{:S(2)}, u32[]{:S(2)}) collective-permute-start(bf16[1,2,1,16,384]{4,3,2,1,0:T(8,128)(2,1)} %refs_4_.1), channel_id=1, source_target_pairs={{0,2},{1,3},{2,0},{3,1},{4,6},{5,7},{6,4},{7,5},{8,10},{9,11},{10,... | collective-permute-start | bytes 73736 | tf_op jit(solution)/shard_map/ppermute | solution.py:231
  5.0 2.0 %collective-permute-done.1.refs_2_ = bf16[1,2,1,16,384]{4,3,2,1,0:T(8,128)(2,1)S(1)} collective-permute-done((bf16[1,2,1,16,384]{4,3,2,1,0:T(8,128)(2,1)}, bf16[1,2,1,16,384]{4,3,2,1,0:T(8,128)(2,1)S(1)}, u32[]{:S(2)}, u32[]{:S(2)}) %collective-permute-start.1) | collective-permute-done | bytes 24608 | tf_op jit(solution)/shard_map/ppermute | solution.py:231
  7.0 0.3 collective-permute-done.4.refs_6_
  7.2 0.0 collective-permute-done.7.refs_10_
  7.2 1.8 %collective-permute-start.13 = (bf16[3,3,3,48,192]{4,3,2,1,0:T(8,128)(2,1)}, bf16[3,3,3,48,192]{4,3,2,1,0:T(8,128)(2,1)S(1)}, u32[]{:S(2)}, u32[]{:S(2)}) collective-permute-start(bf16[3,3,3,48,192]{4,3,2,1,0:T(8,128)(2,1)} %bitcast.2), channel_id=1, source_target_pairs={{0,2},{1,3},{2,0},{3,1},{4,6},{5,7},{6,4},{7,5},{8,10},{9,11},{10,... | collective-permute-start | bytes 1493000 | tf_op jit(solution)/shard_map/ppermute | solution.py:231
  9.0 0.0 collective-permute-start
  9.0 0.5 %collective-permute-start.3 = (bf16[1,2,1,16,384]{4,3,2,1,0:T(8,128)(2,1)}, bf16[1,2,1,16,384]{4,3,2,1,0:T(8,128)(2,1)S(1)}, u32[]{:S(2)}, u32[]{:S(2)}) collective-permute-start(bf16[1,2,1,16,384]{4,3,2,1,0:T(8,128)(2,1)} %refs_4_.1), channel_id=1, source_target_pairs={{0,1},{1,0},{2,3},{3,2},{4,5},{5,4},{6,7},{7,6},{8,9},{9,8},{10,11... | collective-permute-start | bytes 73736 | tf_op jit(solution)/shard_map/ppermute | solution.py:231
  9.5 0.0 collective-permute-start.6
  9.5 0.5 %collective-permute-start.8 = (bf16[1,2,2,32,192]{4,3,2,1,0:T(8,128)(2,1)S(1)}, bf16[1,2,2,32,192]{4,3,2,1,0:T(8,128)(2,1)S(1)}, u32[]{:S(2)}, u32[]{:S(2)}) collective-permute-start(bf16[1,2,2,32,192]{4,3,2,1,0:T(8,128)(2,1)S(1)} %collective-permute-done.7.refs_10_), channel_id=1, source_target_pairs={{0,1},{1,0},{2,3},{3,2},{4,5},{5,4},{6,7},{7,6},{8,9},{9,8},{10,11... | collective-permute-start | bytes 147464 | tf_op jit(solution)/shard_map/ppermute | solution.py:231
  10.0 0.4 %collective-permute-done.refs_1_ = bf16[1,2,1,16,384]{4,3,2,1,0:T(8,128)(2,1)S(1)} collective-permute-done((bf16[1,2,1,16,384]{4,3,2,1,0:T(8,128)(2,1)}, bf16[1,2,1,16,384]{4,3,2,1,0:T(8,128)(2,1)S(1)}, u32[]{:S(2)}, u32[]{:S(2)}) %collective-permute-start) | collective-permute-done | bytes 24608 | tf_op jit(solution)/shard_map/ppermute | solution.py:231
  10.4 0.2 collective-permute-start.2
  10.6 0.0 collective-permute-done.3.refs_5_
  10.6 0.3 collective-permute-start.5
  10.9 0.7 %collective-permute-done.2.refs_3_ = bf16[1,2,1,16,384]{4,3,2,1,0:T(8,128)(2,1)S(1)} collective-permute-done((bf16[1,2,1,16,384]{4,3,2,1,0:T(8,128)(2,1)S(1)}, bf16[1,2,1,16,384]{4,3,2,1,0:T(8,128)(2,1)S(1)}, u32[]{:S(2)}, u32[]{:S(2)}) %collective-permute-start.2) | collective-permute-done | bytes 24608 | tf_op jit(solution)/shard_map/ppermute | solution.py:231
  11.6 0.2 collective-permute-done.5.refs_7_
  11.8 0.0 collective-permute-done.6.refs_9_
  11.8 0.0 collective-permute-done.8.refs_11_
  11.8 3.9 %first_conv.1 = (bf16[160,384]{1,0:T(8,128)(2,1)S(1)}, bf16[96,384]{1,0:T(8,128)(2,1)S(1)}, bf16[64,384]{1,0:T(8,128)(2,1)S(1)}, f32[128,384]{1,0:T(8,128)S(1)}, bf16[2,2,32,192]{3,2,1,0:T(8,128)(2,1)S(1)}) custom-call(bf16[1,2,1,16,384]{4,3,2,1,0:T(8,128)(2,1)} %refs_0_.1, bf16[1,2,1,16,384]{4,3,2,1,0:T(8,128)(2,1)S(1)} %collective-permute-done.refs_1_, ...), custom_call_target="tpu_custom_call" | custom-call | tf_op jit(solution)/shard_map/first_conv/pallas_call | solution.py:253
  15.7 1.3 %collective-permute-start.9 = (bf16[160,384]{1,0:T(8,128)(2,1)S(1)}, bf16[160,384]{1,0:T(8,128)(2,1)S(1)}, u32[]{:S(2)}, u32[]{:S(2)}) collective-permute-start(bf16[160,384]{1,0:T(8,128)(2,1)S(1)} %get-tuple-element.16), channel_id=1, source_target_pairs={{2,6},{3,7},{4,0},{5,1},{6,10},{7,11},{8,4},{9,5},{10,14},{11,15},... | collective-permute-start | bytes 368648 | tf_op jit(solution)/shard_map/ppermute | solution.py:240
  17.0 4.5 %collective-permute-start.10 = (bf16[96,384]{1,0:T(8,128)(2,1)S(1)}, bf16[96,384]{1,0:T(8,128)(2,1)S(1)}, u32[]{:S(2)}, u32[]{:S(2)}) collective-permute-start(bf16[96,384]{1,0:T(8,128)(2,1)S(1)} %get-tuple-element.17), channel_id=1, source_target_pairs={{0,4},{1,5},{4,8},{5,9},{6,2},{7,3},{8,12},{9,13},{10,6},{11,7},{1... | collective-permute-start | bytes 221192 | tf_op jit(solution)/shard_map/ppermute | solution.py:240
  21.6 1.3 %collective-permute-start.11 = (bf16[64,384]{1,0:T(8,128)(2,1)S(1)}, bf16[64,384]{1,0:T(8,128)(2,1)S(1)}, u32[]{:S(2)}, u32[]{:S(2)}) collective-permute-start(bf16[64,384]{1,0:T(8,128)(2,1)S(1)} %get-tuple-element.18), channel_id=1, source_target_pairs={{2,10},{3,11},{6,14},{7,15},{8,0},{9,1},{12,4},{13,5},{18,26},{19,... | collective-permute-start | bytes 147464 | tf_op jit(solution)/shard_map/ppermute | solution.py:240
  22.9 0.0 copy-done
  22.9 0.1 collective-permute-start.16
  23.0 5.8 %collective-permute-done.11.two = bf16[64,384]{1,0:T(8,128)(2,1)S(1)} collective-permute-done((bf16[64,384]{1,0:T(8,128)(2,1)S(1)}, bf16[64,384]{1,0:T(8,128)(2,1)S(1)}, u32[]{:S(2)}, u32[]{:S(2)}) %collective-permute-start.11) | collective-permute-done | bytes 49184 | tf_op jit(solution)/shard_map/ppermute | solution.py:240
  28.8 0.0 collective-permute-done.10.near.refs_6_
  28.8 0.0 collective-permute-done.9.far.refs_5_
  28.9 0.0 collective-permute-done.13.refs_9_
  28.9 0.1 collective-permute-start.17
  29.0 0.1 collective-permute-start.14
  29.0 0.4 %collective-permute-start.12 = (bf16[64,384]{1,0:T(8,128)(2,1)S(1)}, bf16[64,384]{1,0:T(8,128)(2,1)S(1)}, u32[]{:S(2)}, u32[]{:S(2)}) collective-permute-start(bf16[64,384]{1,0:T(8,128)(2,1)S(1)} %get-tuple-element.19.refs_0_), channel_id=1, source_target_pairs={{0,1},{1,0},{2,3},{3,2},{4,5},{5,4},{6,7},{7,6},{8,9},{9,8},{10,11... | collective-permute-start | bytes 147464 | tf_op jit(solution)/shard_map/ppermute | solution.py:231
  29.5 3.7 %collective-permute-done.14.refs_2_ = bf16[64,384]{1,0:T(8,128)(2,1)S(1)} collective-permute-done((bf16[64,384]{1,0:T(8,128)(2,1)S(1)}, bf16[64,384]{1,0:T(8,128)(2,1)S(1)}, u32[]{:S(2)}, u32[]{:S(2)}) %collective-permute-start.14) | collective-permute-done | bytes 49184 | tf_op jit(solution)/shard_map/ppermute | solution.py:231
  33.1 0.0 collective-permute-start.15
  33.1 0.0 collective-permute-done.12.refs_1_
  33.1 0.0 collective-permute-done.16.refs_8_
  33.1 1.2 %collective-permute-done.15.refs_3_ = bf16[64,384]{1,0:T(8,128)(2,1)S(1)} collective-permute-done((bf16[64,384]{1,0:T(8,128)(2,1)S(1)}, bf16[64,384]{1,0:T(8,128)(2,1)S(1)}, u32[]{:S(2)}, u32[]{:S(2)}) %collective-permute-start.15) | collective-permute-done | bytes 49184 | tf_op jit(solution)/shard_map/ppermute | solution.py:231
  34.3 0.0 collective-permute-done.17.refs_10_
  34.3 0.0 copy-done.1
  34.4 3.3 %second_conv.1 = bf16[1,2,2,32,192]{4,3,2,1,0:T(8,128)(2,1)} custom-call(bf16[64,384]{1,0:T(8,128)(2,1)S(1)} %get-tuple-element.19.refs_0_, bf16[64,384]{1,0:T(8,128)(2,1)S(1)} %collective-permute-done.12.refs_1_, bf16[64,384]{1,0:T(8,128)(2,1)S(1)} %collective-permute-done.14.refs_2_, bf16[64,384]{1,0:T(8,128)(2,1)S(1)} %collective-permute-done.15.refs_3_, ...), custom_call_target="tpu_custom_call" | custom-call | tf_op jit(solution)/shard_map/second_conv/pallas_call | solution.py:296
  (1 shorter events, 0.0 us)
Async XLA Ops:
  0.0 22.9 %copy-start = (bf16[3,3,3,192,48]{3,4,2,1,0:T(8,128)(2,1)S(1)}, bf16[3,3,3,192,48]{3,4,2,1,0:T(8,128)(2,1)}, u32[]{:S(2)}) copy-start(bf16[3,3,3,192,48]{3,4,2,1,0:T(8,128)(2,1)} %param.15) | copy-start | bytes 1492996
  0.0 34.3 %copy-start.1 = (f32[192]{0:T(256)S(1)}, f32[192]{0:T(256)}, u32[]{:S(2)}) copy-start(f32[192]{0:T(256)} %refs_11_.1) | copy-start | bytes 2308
  0.0 7.2 %collective-permute-start.7 = (bf16[1,2,2,32,192]{4,3,2,1,0:T(8,128)(2,1)}, bf16[1,2,2,32,192]{4,3,2,1,0:T(8,128)(2,1)S(1)}, u32[]{:S(2)}, u32[]{:S(2)}) collective-permute-start(bf16[1,2,2,32,192]{4,3,2,1,0:T(8,128)(2,1)} %refs_8_.1), channel_id=1, source_target_pairs={{0,2},{1,3},{2,0},{3,1},{4,6},{5,7},{6,4},{7,5},{8,10},{9,11},{10,... | collective-permute-start | bytes 147464 | tf_op jit(solution)/shard_map/ppermute | solution.py:231
  2.9 4.0 %collective-permute-start.1 = (bf16[1,2,1,16,384]{4,3,2,1,0:T(8,128)(2,1)}, bf16[1,2,1,16,384]{4,3,2,1,0:T(8,128)(2,1)S(1)}, u32[]{:S(2)}, u32[]{:S(2)}) collective-permute-start(bf16[1,2,1,16,384]{4,3,2,1,0:T(8,128)(2,1)} %refs_0_.1), channel_id=1, source_target_pairs={{0,2},{1,3},{2,0},{3,1},{4,6},{5,7},{6,4},{7,5},{8,10},{9,11},{10,... | collective-permute-start | bytes 73736 | tf_op jit(solution)/shard_map/ppermute | solution.py:231
  3.0 4.2 %collective-permute-start.4 = (bf16[1,2,1,16,384]{4,3,2,1,0:T(8,128)(2,1)}, bf16[1,2,1,16,384]{4,3,2,1,0:T(8,128)(2,1)S(1)}, u32[]{:S(2)}, u32[]{:S(2)}) collective-permute-start(bf16[1,2,1,16,384]{4,3,2,1,0:T(8,128)(2,1)} %refs_4_.1), channel_id=1, source_target_pairs={{0,2},{1,3},{2,0},{3,1},{4,6},{5,7},{6,4},{7,5},{8,10},{9,11},{10,... | collective-permute-start | bytes 73736 | tf_op jit(solution)/shard_map/ppermute | solution.py:231
  7.2 21.6 %collective-permute-start.13 = (bf16[3,3,3,48,192]{4,3,2,1,0:T(8,128)(2,1)}, bf16[3,3,3,48,192]{4,3,2,1,0:T(8,128)(2,1)S(1)}, u32[]{:S(2)}, u32[]{:S(2)}) collective-permute-start(bf16[3,3,3,48,192]{4,3,2,1,0:T(8,128)(2,1)} %bitcast.2), channel_id=1, source_target_pairs={{0,2},{1,3},{2,0},{3,1},{4,6},{5,7},{6,4},{7,5},{8,10},{9,11},{10,... | collective-permute-start | bytes 1493000 | tf_op jit(solution)/shard_map/ppermute | solution.py:231
  9.0 1.4 %collective-permute-start = (bf16[1,2,1,16,384]{4,3,2,1,0:T(8,128)(2,1)}, bf16[1,2,1,16,384]{4,3,2,1,0:T(8,128)(2,1)S(1)}, u32[]{:S(2)}, u32[]{:S(2)}) collective-permute-start(bf16[1,2,1,16,384]{4,3,2,1,0:T(8,128)(2,1)} %refs_0_.1), channel_id=1, source_target_pairs={{0,1},{1,0},{2,3},{3,2},{4,5},{5,4},{6,7},{7,6},{8,9},{9,8},{10,11... | collective-permute-start | bytes 73736 | tf_op jit(solution)/shard_map/ppermute | solution.py:231
  9.0 1.6 %collective-permute-start.3 = (bf16[1,2,1,16,384]{4,3,2,1,0:T(8,128)(2,1)}, bf16[1,2,1,16,384]{4,3,2,1,0:T(8,128)(2,1)S(1)}, u32[]{:S(2)}, u32[]{:S(2)}) collective-permute-start(bf16[1,2,1,16,384]{4,3,2,1,0:T(8,128)(2,1)} %refs_4_.1), channel_id=1, source_target_pairs={{0,1},{1,0},{2,3},{3,2},{4,5},{5,4},{6,7},{7,6},{8,9},{9,8},{10,11... | collective-permute-start | bytes 73736 | tf_op jit(solution)/shard_map/ppermute | solution.py:231
  9.5 2.3 %collective-permute-start.6 = (bf16[1,2,2,32,192]{4,3,2,1,0:T(8,128)(2,1)}, bf16[1,2,2,32,192]{4,3,2,1,0:T(8,128)(2,1)S(1)}, u32[]{:S(2)}, u32[]{:S(2)}) collective-permute-start(bf16[1,2,2,32,192]{4,3,2,1,0:T(8,128)(2,1)} %refs_8_.1), channel_id=1, source_target_pairs={{0,1},{1,0},{2,3},{3,2},{4,5},{5,4},{6,7},{7,6},{8,9},{9,8},{10,11... | collective-permute-start | bytes 147464 | tf_op jit(solution)/shard_map/ppermute | solution.py:231
  9.5 2.3 %collective-permute-start.8 = (bf16[1,2,2,32,192]{4,3,2,1,0:T(8,128)(2,1)S(1)}, bf16[1,2,2,32,192]{4,3,2,1,0:T(8,128)(2,1)S(1)}, u32[]{:S(2)}, u32[]{:S(2)}) collective-permute-start(bf16[1,2,2,32,192]{4,3,2,1,0:T(8,128)(2,1)S(1)} %collective-permute-done.7.refs_10_), channel_id=1, source_target_pairs={{0,1},{1,0},{2,3},{3,2},{4,5},{5,4},{6,7},{7,6},{8,9},{9,8},{10,11... | collective-permute-start | bytes 147464 | tf_op jit(solution)/shard_map/ppermute | solution.py:231
  10.4 1.2 %collective-permute-start.2 = (bf16[1,2,1,16,384]{4,3,2,1,0:T(8,128)(2,1)S(1)}, bf16[1,2,1,16,384]{4,3,2,1,0:T(8,128)(2,1)S(1)}, u32[]{:S(2)}, u32[]{:S(2)}) collective-permute-start(bf16[1,2,1,16,384]{4,3,2,1,0:T(8,128)(2,1)S(1)} %collective-permute-done.1.refs_2_), channel_id=1, source_target_pairs={{0,1},{1,0},{2,3},{3,2},{4,5},{5,4},{6,7},{7,6},{8,9},{9,8},{10,11... | collective-permute-start | bytes 73736 | tf_op jit(solution)/shard_map/ppermute | solution.py:231
  10.6 1.2 %collective-permute-start.5 = (bf16[1,2,1,16,384]{4,3,2,1,0:T(8,128)(2,1)S(1)}, bf16[1,2,1,16,384]{4,3,2,1,0:T(8,128)(2,1)S(1)}, u32[]{:S(2)}, u32[]{:S(2)}) collective-permute-start(bf16[1,2,1,16,384]{4,3,2,1,0:T(8,128)(2,1)S(1)} %collective-permute-done.4.refs_6_), channel_id=1, source_target_pairs={{0,1},{1,0},{2,3},{3,2},{4,5},{5,4},{6,7},{7,6},{8,9},{9,8},{10,11... | collective-permute-start | bytes 73736 | tf_op jit(solution)/shard_map/ppermute | solution.py:231
  15.7 13.1 %collective-permute-start.9 = (bf16[160,384]{1,0:T(8,128)(2,1)S(1)}, bf16[160,384]{1,0:T(8,128)(2,1)S(1)}, u32[]{:S(2)}, u32[]{:S(2)}) collective-permute-start(bf16[160,384]{1,0:T(8,128)(2,1)S(1)} %get-tuple-element.16), channel_id=1, source_target_pairs={{2,6},{3,7},{4,0},{5,1},{6,10},{7,11},{8,4},{9,5},{10,14},{11,15},... | collective-permute-start | bytes 368648 | tf_op jit(solution)/shard_map/ppermute | solution.py:240
  17.0 11.8 %collective-permute-start.10 = (bf16[96,384]{1,0:T(8,128)(2,1)S(1)}, bf16[96,384]{1,0:T(8,128)(2,1)S(1)}, u32[]{:S(2)}, u32[]{:S(2)}) collective-permute-start(bf16[96,384]{1,0:T(8,128)(2,1)S(1)} %get-tuple-element.17), channel_id=1, source_target_pairs={{0,4},{1,5},{4,8},{5,9},{6,2},{7,3},{8,12},{9,13},{10,6},{11,7},{1... | collective-permute-start | bytes 221192 | tf_op jit(solution)/shard_map/ppermute | solution.py:240
  21.6 7.2 %collective-permute-start.11 = (bf16[64,384]{1,0:T(8,128)(2,1)S(1)}, bf16[64,384]{1,0:T(8,128)(2,1)S(1)}, u32[]{:S(2)}, u32[]{:S(2)}) collective-permute-start(bf16[64,384]{1,0:T(8,128)(2,1)S(1)} %get-tuple-element.18), channel_id=1, source_target_pairs={{2,10},{3,11},{6,14},{7,15},{8,0},{9,1},{12,4},{13,5},{18,26},{19,... | collective-permute-start | bytes 147464 | tf_op jit(solution)/shard_map/ppermute | solution.py:240
  22.9 10.2 %collective-permute-start.16 = (bf16[3,3,3,48,192]{4,3,2,1,0:T(8,128)(2,1)S(1)}, bf16[3,3,3,48,192]{4,3,2,1,0:T(8,128)(2,1)S(1)}, u32[]{:S(2)}, u32[]{:S(2)}) collective-permute-start(bf16[3,3,3,48,192]{4,3,2,1,0:T(8,128)(2,1)S(1)} %bitcast.3), channel_id=1, source_target_pairs={{0,1},{1,0},{2,3},{3,2},{4,5},{5,4},{6,7},{7,6},{8,9},{9,8},{10,11... | collective-permute-start | bytes 1493000 | tf_op jit(solution)/shard_map/ppermute | solution.py:231
  28.9 5.5 %collective-permute-start.17 = (bf16[3,3,3,48,192]{4,3,2,1,0:T(8,128)(2,1)S(1)}, bf16[3,3,3,48,192]{4,3,2,1,0:T(8,128)(2,1)S(1)}, u32[]{:S(2)}, u32[]{:S(2)}) collective-permute-start(bf16[3,3,3,48,192]{4,3,2,1,0:T(8,128)(2,1)S(1)} %collective-permute-done.13.refs_9_), channel_id=1, source_target_pairs={{0,1},{1,0},{2,3},{3,2},{4,5},{5,4},{6,7},{7,6},{8,9},{9,8},{10,11... | collective-permute-start | bytes 1493000 | tf_op jit(solution)/shard_map/ppermute | solution.py:231
  29.0 4.2 %collective-permute-start.14 = (bf16[64,384]{1,0:T(8,128)(2,1)S(1)}, bf16[64,384]{1,0:T(8,128)(2,1)S(1)}, u32[]{:S(2)}, u32[]{:S(2)}) collective-permute-start(bf16[64,384]{1,0:T(8,128)(2,1)S(1)} %get-tuple-element.22), channel_id=1, source_target_pairs={{0,2},{1,3},{2,0},{3,1},{4,6},{5,7},{6,4},{7,5},{8,10},{9,11},{10,... | collective-permute-start | bytes 147464 | tf_op jit(solution)/shard_map/ppermute | solution.py:231
  29.0 4.1 %collective-permute-start.12 = (bf16[64,384]{1,0:T(8,128)(2,1)S(1)}, bf16[64,384]{1,0:T(8,128)(2,1)S(1)}, u32[]{:S(2)}, u32[]{:S(2)}) collective-permute-start(bf16[64,384]{1,0:T(8,128)(2,1)S(1)} %get-tuple-element.19.refs_0_), channel_id=1, source_target_pairs={{0,1},{1,0},{2,3},{3,2},{4,5},{5,4},{6,7},{7,6},{8,9},{9,8},{10,11... | collective-permute-start | bytes 147464 | tf_op jit(solution)/shard_map/ppermute | solution.py:231
  33.1 1.2 %collective-permute-start.15 = (bf16[64,384]{1,0:T(8,128)(2,1)S(1)}, bf16[64,384]{1,0:T(8,128)(2,1)S(1)}, u32[]{:S(2)}, u32[]{:S(2)}) collective-permute-start(bf16[64,384]{1,0:T(8,128)(2,1)S(1)} %collective-permute-done.14.refs_2_), channel_id=1, source_target_pairs={{0,1},{1,0},{2,3},{3,2},{4,5},{5,4},{6,7},{7,6},{8,9},{9,8},{10,11... | collective-permute-start | bytes 147464 | tf_op jit(solution)/shard_map/ppermute | solution.py:231

commit v3 on v1

v3 whole, which is shorter than its diff:
```python
import functools

import jax
import jax.numpy as jnp
from jax import lax
from jax.experimental import pallas as pl
from jax.experimental.pallas import tpu as pltpu
from jax.sharding import PartitionSpec as P

epsilon = 1e-06
f32 = jnp.float32
bf16 = jnp.bfloat16


def norm_silu(values, gain):
    mean_square = jnp.mean(values * values, axis=-1, keepdims=True)
    return jax.nn.silu(values * lax.rsqrt(mean_square + epsilon) * gain)


def dot(lhs, rhs, transposed=False):
    dims = (((1,), (1,)), ((), ())) if transposed else (((1,), (0,)), ((), ()))
    return lax.dot_general(lhs, rhs, dims, preferred_element_type=f32)


def shifted(values, width):
    count = values.shape[0]
    place = lax.broadcasted_iota(jnp.int32, values.shape, 0) % width
    left = jnp.where(place == 0, 0.0, pltpu.roll(values, 1, 0))
    right = jnp.where(place == width - 1, 0.0, pltpu.roll(values, count - 1, 0))
    return left, values, right


def halves(values):
    count = values.shape[0] // 2
    return jnp.concatenate([values[:count], values[count:]], axis=1)


def pack_kernel(latents, first, second, gain_there, out, latent_here, first_here, second_here, gain, sems):
    loads = [
        pltpu.make_async_copy(*pair, sems.at[n])
        for n, pair in enumerate(((gain_there, gain), (latents, latent_here), (first, first_here), (second, second_here)))
    ]
    for load in loads:
        load.start()
    rows, channels = latent_here.shape[1] * latent_here.shape[3], latent_here.shape[-1]
    width = second_here.shape[3]
    for load in loads:
        load.wait()
    out[pl.ds(0, rows), :] = first_here[...].reshape(rows, channels)
    act = norm_silu(latent_here[...].reshape(rows, channels).astype(f32), gain[...][None, :])
    out[pl.ds(rows, rows), :] = act.astype(bf16)
    for r in range(2):
        out[pl.ds(2 * rows + r * width, width), :] = jnp.concatenate([second_here[0, f, r] for f in range(2)], axis=1)


def fetch_kernel(packed, first_there, second_there, first, second, second_here, sems):
    del packed
    loads = [
        pltpu.make_async_copy(second_there, second_here, sems.at[0]),
        pltpu.make_async_copy(first_there, first, sems.at[1]),
    ]
    for load in loads:
        load.start()
    loads[0].wait()
    taps, group, channels = 27, second_here.shape[-2], second_here.shape[-1]
    values = second_here[...].reshape(taps * group, channels)
    most = (taps + 1) // 2 * group
    rest = taps * group - most
    second[pl.ds(0, rest), :] = jnp.concatenate([values[:rest], values[most:]], axis=1)
    last = values[rest:most]
    second[pl.ds(rest, group), :] = jnp.concatenate([last, last], axis=1)
    loads[1].wait()


def first_kernel(frames, columns, *refs):
    packs, weight, slots_there, blocks_there = refs[0:4], refs[4], refs[5], refs[6]
    one, other, two, own, mid = refs[7:12]
    held, slots, blocks, sems = refs[12:16]
    loads = [
        pltpu.make_async_copy(slots_there, slots, sems.at[0]),
        pltpu.make_async_copy(blocks_there, blocks, sems.at[1]),
    ]
    for load in loads:
        load.start()
    me = lax.axis_index("strm")
    upper = me // 2 == 0
    channels = held.shape[-1]
    outputs = weight.shape[-2]
    half = frames * columns
    width = 2 * columns
    for d in range(4):
        held[me ^ d] = packs[d][...]
    for load in loads:
        load.wait()

    parts = []
    for d in range(4):
        stream = me ^ d
        chosen = held[slots[stream], pl.ds(0, half)].astype(f32)
        parts.append(jnp.where(blocks[stream] > 0, chosen, 0.0))
        parts.append(packs[d][pl.ds(half, half), :].astype(f32))
    views = [
        view.astype(bf16).reshape(4, frames + 2, columns, channels)
        for view in shifted(jnp.concatenate(parts, axis=0), columns)
    ]
    rows = 4 * half
    sums = [jnp.zeros((rows, outputs), f32) for _ in range(3)]
    taps = [jnp.where(upper, 2, 0), 1, jnp.where(upper, 0, 2)]
    for i in range(3):
        for l in range(3):
            window = views[l][:, i : i + frames].reshape(rows, channels)
            for j in range(3):
                sums[j] = sums[j] + dot(window, weight[i, taps[j], l], True)

    u, v, w = [[halves(values[: 2 * half]), halves(values[2 * half :])] for values in sums]
    far_first = sends_far_first()
    cached = held[slots[me], pl.ds(2 * half, 2 * width)].astype(f32)
    cached = jnp.where(blocks[me] > 0, cached, 0.0)
    mid[...] = cached.astype(bf16)
    edges = [cached[:width], cached[width:]]
    far = u + v + [jnp.where(upper, edges[0], edges[1])]
    near = w + [jnp.zeros_like(w[0])] * 2 + [jnp.where(upper, edges[1], edges[0])]
    for n in range(5):
        at = pl.ds(n * half, half)
        one[at, :] = jnp.where(far_first, far[n], near[n]).astype(bf16)
        other[at, :] = jnp.where(far_first, near[n], far[n]).astype(bf16)
    for p in range(2):
        two[pl.ds(p * half, half), :] = u[p].astype(bf16)
        own[pl.ds(p * half, half), :] = v[p]
        own[pl.ds((2 + p) * half, half), :] = w[p]


def sends_far_first():
    return (lax.axis_index("strm") // 2 == 0) == (lax.axis_index("band") % 2 == 1)


def far_comes_first():
    return (lax.axis_index("strm") // 2 == 0) == (lax.axis_index("band") % 2 == 0)


def at_end():
    place = lax.axis_index("band")
    return (place == 0) | (place == lax.axis_size("band") - 1)


def sum_kernel(half, own, one, other, two, first_pair, second_pair):
    me, place, bands = lax.axis_index("strm"), lax.axis_index("band"), lax.axis_size("band")
    upper = me // 2 == 0
    outside = jnp.where(upper, place == bands - 1, place == 0)
    beyond = jnp.where(upper, place >= bands - 2, place <= 1)
    far_first = far_comes_first()
    alone = at_end()
    for p, pair in enumerate((first_pair, second_pair)):
        at = pl.ds(p * half, half)
        after = pl.ds((2 + p) * half, half)
        centre = own[at, :] + one[at, :].astype(f32) + jnp.where(alone, 0.0, other[at, :].astype(f32))
        extra = jnp.where(far_first, one[after, :].astype(f32), jnp.where(alone, 0.0, other[after, :].astype(f32)))
        extra = own[after, :] + extra + jnp.where(beyond, 0.0, two[at, :].astype(f32))
        pair[pl.ds(0, half), :] = centre.astype(bf16)
        pair[pl.ds(half, half), :] = jnp.where(outside, 0.0, extra).astype(bf16)


def cache_kernel(columns, mid, one, other, w0, w1, w2, w3, sums, weights, first_taps):
    me = lax.axis_index("strm")
    upper = me // 2 == 0
    far_first = far_comes_first()
    channels = sums.shape[-1]
    group = channels // 4
    width = 2 * columns
    area = 2 * width
    for d, quarter in enumerate((w0, w1, w2, w3)):
        at = pl.ds(pl.multiple_of((me ^ d) * group, 16), group)
        values = quarter[...].reshape(14, group, 2 * channels)
        left, right = values[:, :, :channels], values[:13, :, channels:]
        first_taps[:, at, :] = left[:9]
        weights[pl.ds(0, 5), at, :] = left[9:]
        weights[pl.ds(5, 13), at, :] = right

    first_edge = one[pl.ds(4 * width, width), :].astype(f32)
    second_edge = jnp.where(at_end(), 0.0, other[pl.ds(4 * width, width), :].astype(f32))
    far = jnp.where(far_first, first_edge, second_edge)
    near = jnp.where(far_first, second_edge, first_edge)
    top = jnp.where(upper, near, far).astype(bf16)
    bottom = jnp.where(upper, far, near).astype(bf16)
    stored = jnp.concatenate([top, mid[...], bottom], axis=0)
    size = stored.shape[0]
    row = lax.broadcasted_iota(jnp.int32, (size, size), 0)
    column = lax.broadcasted_iota(jnp.int32, (size, size), 1)
    inside = row % width
    natural = 2 * (inside % columns) + inside // columns
    early = jnp.zeros((area, channels), f32)
    late = jnp.zeros((area, channels), f32)
    for l in range(3):
        source = natural + (l - 1)
        keep = (source >= 0) & (source < width) & (column == row - inside + source)
        view = dot(jnp.where(keep, 1.0, 0.0).astype(bf16), stored).astype(bf16)
        c0, c1 = view[:, :channels], view[:, channels:]
        for j in range(3):
            at = slice(j * width, j * width + area)
            tap = 3 * j + l
            early = early + dot(c0[at], first_taps[tap], True) + dot(c1[at], weights[tap], True)
            late = late + dot(c1[at], first_taps[tap], True)
    sums[0] = early
    sums[1] = late


def second_kernel(frames, columns, p0, p1, p2, p3, sums, weights, gain, out, quarters):
    me = lax.axis_index("strm")
    channels = out.shape[-1]
    width = 2 * columns
    for e, pair in enumerate((p0, p1, p2, p3)):
        quarters[me ^ e] = pair[:, (e % 2) * channels : (e % 2 + 1) * channels]

    fields = [quarters[q].astype(f32).reshape(2, frames, columns, channels) for q in range(4)]
    row_of = ((1, 1), (0, 0), (1, 0), (0, 1))
    upsampled = jnp.stack(
        [jnp.stack([jnp.stack([fields[2 * a + b][c, t] for b in range(2)]) for a, c in row_of]) for t in range(frames)]
    )
    act = norm_silu(upsampled.reshape(-1, channels), gain[...][None, :])
    left, same, right = [
        v.astype(bf16).reshape(frames, 4, 2, columns, channels) for v in shifted(act, columns)
    ]

    def split(first, second):
        return jnp.stack([first, second], axis=2)

    views = [
        split(left[:, :, 1], same[:, :, 0]),
        same,
        split(same[:, :, 1], right[:, :, 0]),
    ]
    area = 2 * width
    early, late = sums[0], sums[1]
    for j in range(3):
        for l in range(3):
            a0, a1 = [views[l][f, j : j + 2].reshape(area, channels) for f in range(2)]
            tap = 3 * j + l
            early = early + dot(a0, weights[9 + tap], True)
            late = late + dot(a0, weights[tap], True) + dot(a1, weights[9 + tap], True)

    row = lax.broadcasted_iota(jnp.int32, (area, area), 0)
    column = lax.broadcasted_iota(jnp.int32, (area, area), 1)
    inside = row % width
    keep = column == row - inside + (inside % 2) * columns + inside // 2
    order = jnp.where(keep, 1.0, 0.0).astype(bf16)
    for t, branch in enumerate((early, late)):
        base = upsampled[t, 1:3].reshape(area, channels)
        decoded = (base + branch.astype(bf16).astype(f32)).astype(bf16)
        out[0, t] = dot(order, decoded).astype(bf16).reshape(2, width, channels)


def whole(count):
    return [pl.BlockSpec(memory_space=pltpu.VMEM)] * count


THERE = pl.BlockSpec(memory_space=pltpu.HBM)


def there(value):
    return pltpu.with_memory_space_constraint(value, pltpu.HBM)


def call(kernel, name, megabytes, **settings):
    return pl.pallas_call(
        kernel, name=name, compiler_params=pltpu.CompilerParams(vmem_limit_bytes=megabytes * 2**20), **settings
    )


def struct(shape, dtype=bf16):
    return jax.ShapeDtypeStruct(shape, dtype)


def body(latents, cache_first, cache_second, gain_first, gain_second, w_first, w_second, cache_slot, block_index):
    frames, columns, channels = latents.shape[1], latents.shape[3], latents.shape[4]
    outputs = w_first.shape[-1]
    bands = lax.axis_size("band")
    streams = lax.axis_size("strm")
    assert streams == 4 and bands % 2 == 0 and latents.shape[2] == 1 and frames == 2
    half = frames * columns
    width = 2 * columns

    def swapped(value, distance):
        return lax.ppermute(value, "strm", [(i, i ^ distance) for i in range(streams)])

    def along(value, target):
        pairs = []
        for band in range(bands):
            for k in range(streams):
                to, there = target(band, k)
                if 0 <= to < bands:
                    pairs.append((band * streams + k, to * streams + there))
        return lax.ppermute(value, ("band", "strm"), pairs)

    def first_way(band, k):
        return band ^ 1, k

    def second_way(band, k):
        if band in (0, bands - 1):
            return band, k ^ 1
        return ((band + 1) ^ 1) - 1, k

    def third_way(band, k):
        if bands == 4:
            return band ^ 2, k
        return (band - 2 if k // 2 == 0 else band + 2), k

    turned_first = jnp.swapaxes(w_first, 3, 4)
    turned_second = jnp.swapaxes(w_second, 3, 4)
    group = turned_second.shape[3]
    packed = call(
        pack_kernel,
        "pack",
        4,
        out_shape=struct((2 * half + 2 * width, channels)),
        in_specs=[THERE] * 4,
        out_specs=whole(1)[0],
        scratch_shapes=[
            pltpu.VMEM(latents.shape, bf16),
            pltpu.VMEM(cache_first.shape, bf16),
            pltpu.VMEM(cache_second.shape, bf16),
            pltpu.VMEM(gain_first.shape, f32),
            pltpu.SemaphoreType.DMA((4,)),
        ],
    )(*map(there, (latents, cache_first, cache_second, gain_first)))
    across = swapped(packed, 2)
    weight_first, weight_own = call(
        fetch_kernel,
        "fetch",
        16,
        out_shape=[struct(turned_first.shape), struct((14 * group, 2 * outputs))],
        in_specs=whole(1) + [THERE] * 2,
        out_specs=whole(2),
        scratch_shapes=[pltpu.VMEM(turned_second.shape, bf16), pltpu.SemaphoreType.DMA((2,))],
    )(packed, there(turned_first), there(turned_second))
    weight_own, across = lax.optimization_barrier((weight_own, across))
    packs = [packed, swapped(packed, 1), across, swapped(across, 1)]
    weights = [weight_own, swapped(weight_own, 1), swapped(weight_own, 2)]
    pair = struct((2 * half, 2 * outputs))
    payload = struct((4 * half + width, 2 * outputs))
    one, other, two, own, mid = call(
        functools.partial(first_kernel, frames, columns),
        "first_conv",
        16,
        out_shape=[payload, payload, pair, struct((4 * half, 2 * outputs), f32), struct((2 * width, 2 * outputs))],
        in_specs=whole(5) + [THERE] * 2,
        out_specs=whole(5),
        scratch_shapes=[
            pltpu.VMEM((4,) + packed.shape, bf16),
            pltpu.SMEM(cache_slot.shape, jnp.int32),
            pltpu.SMEM(block_index.shape, jnp.int32),
            pltpu.SemaphoreType.DMA((2,)),
        ],
    )(*packs, weight_first, there(cache_slot), there(block_index))
    one, other, two = along(one, first_way), along(other, second_way), along(two, third_way)
    first_pair, second_pair = call(
        functools.partial(sum_kernel, half),
        "row_sums",
        4,
        out_shape=[pair, pair],
        in_specs=whole(4),
        out_specs=whole(2),
    )(own, one, other, two)
    weight_across, _ = lax.optimization_barrier((weights[2], first_pair))
    weights.append(swapped(weight_across, 1))
    across = swapped(second_pair, 2)
    sums, taps = call(
        functools.partial(cache_kernel, columns),
        "cached_conv",
        16,
        out_shape=[struct((2, 2 * width, outputs), f32), struct((18, outputs, outputs))],
        in_specs=whole(7),
        out_specs=whole(2),
        scratch_shapes=[pltpu.VMEM((9, outputs, outputs), bf16)],
    )(mid, one, other, *weights)
    across, sums = lax.optimization_barrier((across, sums))
    pairs = [first_pair, swapped(first_pair, 1), across, swapped(across, 1)]
    return call(
        functools.partial(second_kernel, frames, columns),
        "second_conv",
        16,
        out_shape=struct((1, frames, 2, width, outputs)),
        in_specs=whole(7),
        out_specs=whole(1)[0],
        scratch_shapes=[pltpu.VMEM((4, 2 * half, outputs), bf16)],
    )(*pairs, sums, taps, gain_second)


def solution(mesh):
    in_specs = (
        P(("grp", "strm"), None, "band", None, None),
        P(("grp", "strm"), None, "band", None, None),
        P(("grp", "strm"), None, "band", None, None),
        P(),
        P(),
        P(None, None, None, None, "strm"),
        P(None, None, None, None, "strm"),
        P("grp"),
        P("grp"),
    )
    out_specs = P(("grp", "strm"), None, "band", None, None)
    return jax.shard_map(body, mesh=mesh, in_specs=in_specs, out_specs=out_specs, check_vma=False)
```

time: 64.9 us -> 30.2 us (0.47)
  waiting for transfers between devices: 30.5 us -> 9.45 us
  local copies, waits for them, and re-layouts: 10.4 us -> 0.01 us
  starting transfers between devices: 15.5 us -> 10.5 us
  Pallas kernels: 7.83 us -> 10 us
    ppermute x15 -> x9, waiting for transfers between devices: 24.4 us -> 3.8 us  [swapped(): lax.ppermute(value, 'strm', [(i, i ^ distance) for i in range(streams)])]
    unnamed x30 -> x2, local copies, waits for them, and re-layouts: 8.98 us -> 0.01 us
    ppermute x3, starting transfers between devices: 7.12 us -> 4.24 us  [along(): return lax.ppermute(value, ('band', 'strm'), pairs)]
    pallas_call x3 -> x6, Pallas kernels: 7.83 us -> 10 us  [the longest x1 2.63 us: body(): call(functools.partial(first_kernel, frames, columns), 'first_conv', 16,...]
    ppermute x15 -> x9, starting transfers between devices: 8.38 us -> 6.24 us  [swapped(): lax.ppermute(value, 'strm', [(i, i ^ distance) for i in range(streams)])]
    concatenate x1 -> x0, local copies, waits for them, and re-layouts: 0.75 us -> none  [body(): jnp.concatenate([cache_slot, block_index, jnp.stack([me, place, jnp.int32...]
    reshape x1 -> x0, local copies, waits for them, and re-layouts: 0.68 us -> none  [body(): gain_first.reshape(1, -1)]
  transfers between devices with their start and end apart: 18 -> 12, of which waited for: 6 -> 7; matrix products, arithmetic and copies ran while one was open for 2% -> 0% of each run, Pallas kernels for 6% -> 24%
where the time goes in v3:
time: 30.2 us; the launch traced here: 30.1 us
  starting transfers between devices  10.5 us (35%)
  Pallas kernels  10 us (33%)
  waiting for transfers between devices  9.45 us (31%)
    ppermute x9, starting transfers between devices, swapped(): lax.ppermute(value, 'strm', [(i, i ^ distance) for i in range(streams)])  6.24 us
    ppermute x3, waiting for transfers between devices, along(): return lax.ppermute(value, ('band', 'strm'), pairs)  5.65 us
    ppermute x3, starting transfers between devices, along(): return lax.ppermute(value, ('band', 'strm'), pairs)  4.24 us
    ppermute x9, waiting for transfers between devices, swapped(): lax.ppermute(value, 'strm', [(i, i ^ distance) for i in range(streams)])  3.8 us
    pallas_call x1, Pallas kernels, body(): call(functools.partial(first_kernel, frames, columns), 'first_conv', 16,...  2.63 us
    pallas_call x1, Pallas kernels, body(): call(fetch_kernel, 'fetch', 16, out_shape=[struct(turned_first.shape), st...  2.35 us
    pallas_call x1, Pallas kernels, body(): call(functools.partial(cache_kernel, columns), 'cached_conv', 16, out_sha...  2.11 us
    pallas_call x1, Pallas kernels, body(): call(functools.partial(second_kernel, frames, columns), 'second_conv', 16...  1.85 us
  transfers between devices with their start and end apart: 12, of which 7 were waited for; matrix products, arithmetic and copies ran while one was open for 0% of the time, Pallas kernels for 24%

profile of v3, /device:TPU:0, one launch (start us, length us, event | category | flops | bytes accessed | tf_op | source)
XLA Modules:
  0.0 30.1 jit_solution(12892499916219023857)
XLA Ops:
  0.0 1.0 %pack.1.packed.refs_0_ = bf16[128,384]{1,0:T(8,128)(2,1)S(1)} custom-call(bf16[1,2,1,16,384]{4,3,2,1,0:T(8,128)(2,1)} %latents.1, bf16[1,2,1,16,384]{4,3,2,1,0:T(8,128)(2,1)} %first.1, bf16[1,2,2,32,192]{4,3,2,1,0:T(8,128)(2,1)} %second.1, f32[384]{0:T(512)} %gain_there.1), custom_call_target="tpu_custom_call" | custom-call | tf_op jit(solution)/shard_map/pack/pallas_call | solution.py:310
  1.0 3.0 %collective-permute-start.1 = (bf16[128,384]{1,0:T(8,128)(2,1)S(1)}, bf16[128,384]{1,0:T(8,128)(2,1)S(1)}, u32[]{:S(2)}, u32[]{:S(2)}) collective-permute-start(bf16[128,384]{1,0:T(8,128)(2,1)S(1)} %pack.1.packed.refs_0_), channel_id=1, source_target_pairs={{0,2},{1,3},{2,0},{3,1},{4,6},{5,7},{6,4},{7,5},{8,10},{9,11},{10,... | collective-permute-start | bytes 294920 | tf_op jit(solution)/shard_map/ppermute | solution.py:283
  4.0 2.4 %fetch.1 = (bf16[3,3,3,192,384]{4,3,2,1,0:T(8,128)(2,1)S(1)}, bf16[672,384]{1,0:T(8,128)(2,1)S(1)}) custom-call(bf16[128,384]{1,0:T(8,128)(2,1)S(1)} %pack.1.packed.refs_0_, bf16[3,3,3,192,384]{4,3,2,1,0:T(8,128)(2,1)} %bitcast.2, bf16[3,3,3,48,192]{4,3,2,1,0:T(8,128)(2,1)} %bitcast.3), custom_call_target="tpu_custom_call" | custom-call | tf_op jit(solution)/shard_map/fetch/pallas_call | solution.py:326
  6.4 0.0 copy-start
  6.4 0.4 %collective-permute-done.1.refs_2_ = bf16[128,384]{1,0:T(8,128)(2,1)S(1)} collective-permute-done((bf16[128,384]{1,0:T(8,128)(2,1)S(1)}, bf16[128,384]{1,0:T(8,128)(2,1)S(1)}, u32[]{:S(2)}, u32[]{:S(2)}) %collective-permute-start.1) | collective-permute-done | bytes 98336 | tf_op jit(solution)/shard_map/ppermute | solution.py:283
  6.8 1.8 %collective-permute-start.9 = (bf16[672,384]{1,0:T(8,128)(2,1)S(1)}, bf16[672,384]{1,0:T(8,128)(2,1)S(1)}, u32[]{:S(2)}, u32[]{:S(2)}) collective-permute-start(bf16[672,384]{1,0:T(8,128)(2,1)S(1)} %get-tuple-element.31.w0), channel_id=1, source_target_pairs={{0,2},{1,3},{2,0},{3,1},{4,6},{5,7},{6,4},{7,5},{8,10},{9,11},{10,... | collective-permute-start | bytes 1548296 | tf_op jit(solution)/shard_map/ppermute | solution.py:283
  8.7 0.0 collective-permute-start
  8.7 0.5 %collective-permute-start.2 = (bf16[128,384]{1,0:T(8,128)(2,1)S(1)}, bf16[128,384]{1,0:T(8,128)(2,1)S(1)}, u32[]{:S(2)}, u32[]{:S(2)}) collective-permute-start(bf16[128,384]{1,0:T(8,128)(2,1)S(1)} %collective-permute-done.1.refs_2_), channel_id=1, source_target_pairs={{0,1},{1,0},{2,3},{3,2},{4,5},{5,4},{6,7},{7,6},{8,9},{9,8},{10,11... | collective-permute-start | bytes 294920 | tf_op jit(solution)/shard_map/ppermute | solution.py:283
  9.2 0.8 %collective-permute-done.refs_1_ = bf16[128,384]{1,0:T(8,128)(2,1)S(1)} collective-permute-done((bf16[128,384]{1,0:T(8,128)(2,1)S(1)}, bf16[128,384]{1,0:T(8,128)(2,1)S(1)}, u32[]{:S(2)}, u32[]{:S(2)}) %collective-permute-start) | collective-permute-done | bytes 98336 | tf_op jit(solution)/shard_map/ppermute | solution.py:283
  10.0 0.2 collective-permute-done.2.refs_3_
  10.1 2.6 %first_conv.1 = (bf16[160,384]{1,0:T(8,128)(2,1)S(1)}, bf16[160,384]{1,0:T(8,128)(2,1)S(1)}, bf16[64,384]{1,0:T(8,128)(2,1)S(1)}, f32[128,384]{1,0:T(8,128)S(1)}, bf16[64,384]{1,0:T(8,128)(2,1)S(1)}) custom-call(bf16[128,384]{1,0:T(8,128)(2,1)S(1)} %pack.1.packed.refs_0_, bf16[128,384]{1,0:T(8,128)(2,1)S(1)} %collective-permute-done.refs_1_, ...), custom_call_target="tpu_custom_call" | custom-call | tf_op jit(solution)/shard_map/first_conv/pallas_call | solution.py:340
  12.8 1.6 %collective-permute-start.3 = (bf16[160,384]{1,0:T(8,128)(2,1)S(1)}, bf16[160,384]{1,0:T(8,128)(2,1)S(1)}, u32[]{:S(2)}, u32[]{:S(2)}) collective-permute-start(bf16[160,384]{1,0:T(8,128)(2,1)S(1)} %get-tuple-element.25), channel_id=1, source_target_pairs={{0,4},{1,5},{2,6},{3,7},{4,0},{5,1},{6,2},{7,3},{8,12},{9,13},{10,... | collective-permute-start | bytes 368648 | tf_op jit(solution)/shard_map/ppermute | solution.py:292
  14.4 0.1 collective-permute-start.4
  14.5 2.5 %collective-permute-start.5 = (bf16[64,384]{1,0:T(8,128)(2,1)S(1)}, bf16[64,384]{1,0:T(8,128)(2,1)S(1)}, u32[]{:S(2)}, u32[]{:S(2)}) collective-permute-start(bf16[64,384]{1,0:T(8,128)(2,1)S(1)} %get-tuple-element.27), channel_id=1, source_target_pairs={{0,8},{1,9},{2,10},{3,11},{4,12},{5,13},{6,14},{7,15},{8,0},{9,1},... | collective-permute-start | bytes 147464 | tf_op jit(solution)/shard_map/ppermute | solution.py:292
  17.0 0.0 collective-permute-start.8
  17.0 5.6 %collective-permute-done.5.two = bf16[64,384]{1,0:T(8,128)(2,1)S(1)} collective-permute-done((bf16[64,384]{1,0:T(8,128)(2,1)S(1)}, bf16[64,384]{1,0:T(8,128)(2,1)S(1)}, u32[]{:S(2)}, u32[]{:S(2)}) %collective-permute-start.5) | collective-permute-done | bytes 49184 | tf_op jit(solution)/shard_map/ppermute | solution.py:292
  22.6 0.0 collective-permute-done.3.one
  22.7 0.0 collective-permute-done.4.other
  22.7 0.1 row_sums.1
  22.7 0.0 collective-permute-done.9.w2
  22.7 0.1 collective-permute-start.10
  22.8 0.6 %collective-permute-start.7 = (bf16[64,384]{1,0:T(8,128)(2,1)S(1)}, bf16[64,384]{1,0:T(8,128)(2,1)S(1)}, u32[]{:S(2)}, u32[]{:S(2)}) collective-permute-start(bf16[64,384]{1,0:T(8,128)(2,1)S(1)} %get-tuple-element.29), channel_id=1, source_target_pairs={{0,2},{1,3},{2,0},{3,1},{4,6},{5,7},{6,4},{7,5},{8,10},{9,11},{10,... | collective-permute-start | bytes 147464 | tf_op jit(solution)/shard_map/ppermute | solution.py:283
  23.4 0.2 collective-permute-start.6
  23.6 0.0 collective-permute-done.8.w1
  23.6 1.1 %collective-permute-done.10.w3 = bf16[672,384]{1,0:T(8,128)(2,1)S(1)} collective-permute-done((bf16[672,384]{1,0:T(8,128)(2,1)S(1)}, bf16[672,384]{1,0:T(8,128)(2,1)S(1)}, u32[]{:S(2)}, u32[]{:S(2)}) %collective-permute-start.10) | collective-permute-done | bytes 516128 | tf_op jit(solution)/shard_map/ppermute | solution.py:283
  24.7 2.1 %cached_conv.1 = (f32[2,64,192]{2,1,0:T(8,128)S(1)}, bf16[18,192,192]{2,1,0:T(8,128)(2,1)S(1)}) custom-call(bf16[64,384]{1,0:T(8,128)(2,1)S(1)} %get-tuple-element.30.mid, bf16[160,384]{1,0:T(8,128)(2,1)S(1)} %collective-permute-done.3.one, bf16[160,384]{1,0:T(8,128)(2,1)S(1)} %collective-permute-done.4.other, bf16[672,384]{1,0:T(8,128)(2,1)S(1)} %get-tuple-element.31.w0, ...), custom_call_target="tpu_custom_call" | custom-call | tf_op jit(solution)/shard_map/cached_conv/pallas_call | solution.py:366
  26.8 0.2 collective-permute-done.7.p2
  27.0 0.1 collective-permute-start.11
  27.0 0.0 collective-permute-done.6.p1
  27.0 1.2 %collective-permute-done.11.p3 = bf16[64,384]{1,0:T(8,128)(2,1)S(1)} collective-permute-done((bf16[64,384]{1,0:T(8,128)(2,1)S(1)}, bf16[64,384]{1,0:T(8,128)(2,1)S(1)}, u32[]{:S(2)}, u32[]{:S(2)}) %collective-permute-start.11) | collective-permute-done | bytes 49184 | tf_op jit(solution)/shard_map/ppermute | solution.py:283
  28.2 0.0 copy-done
  28.2 1.9 %second_conv.1 = bf16[1,2,2,32,192]{4,3,2,1,0:T(8,128)(2,1)} custom-call(bf16[64,384]{1,0:T(8,128)(2,1)S(1)} %get-tuple-element.28.p0, bf16[64,384]{1,0:T(8,128)(2,1)S(1)} %collective-permute-done.6.p1, bf16[64,384]{1,0:T(8,128)(2,1)S(1)} %collective-permute-done.7.p2, bf16[64,384]{1,0:T(8,128)(2,1)S(1)} %collective-permute-done.11.p3, ...), custom_call_target="tpu_custom_call" | custom-call | tf_op jit(solution)/shard_map/second_conv/pallas_call | solution.py:377
Async XLA Ops:
  1.0 5.8 %collective-permute-start.1 = (bf16[128,384]{1,0:T(8,128)(2,1)S(1)}, bf16[128,384]{1,0:T(8,128)(2,1)S(1)}, u32[]{:S(2)}, u32[]{:S(2)}) collective-permute-start(bf16[128,384]{1,0:T(8,128)(2,1)S(1)} %pack.1.packed.refs_0_), channel_id=1, source_target_pairs={{0,2},{1,3},{2,0},{3,1},{4,6},{5,7},{6,4},{7,5},{8,10},{9,11},{10,... | collective-permute-start | bytes 294920 | tf_op jit(solution)/shard_map/ppermute | solution.py:283
  6.4 21.8 %copy-start = (f32[192]{0:T(256)S(1)}, f32[192]{0:T(256)}, u32[]{:S(2)}) copy-start(f32[192]{0:T(256)} %gain.1) | copy-start | bytes 2308
  6.8 15.9 %collective-permute-start.9 = (bf16[672,384]{1,0:T(8,128)(2,1)S(1)}, bf16[672,384]{1,0:T(8,128)(2,1)S(1)}, u32[]{:S(2)}, u32[]{:S(2)}) collective-permute-start(bf16[672,384]{1,0:T(8,128)(2,1)S(1)} %get-tuple-element.31.w0), channel_id=1, source_target_pairs={{0,2},{1,3},{2,0},{3,1},{4,6},{5,7},{6,4},{7,5},{8,10},{9,11},{10,... | collective-permute-start | bytes 1548296 | tf_op jit(solution)/shard_map/ppermute | solution.py:283
  8.7 1.3 %collective-permute-start = (bf16[128,384]{1,0:T(8,128)(2,1)S(1)}, bf16[128,384]{1,0:T(8,128)(2,1)S(1)}, u32[]{:S(2)}, u32[]{:S(2)}) collective-permute-start(bf16[128,384]{1,0:T(8,128)(2,1)S(1)} %pack.1.packed.refs_0_), channel_id=1, source_target_pairs={{0,1},{1,0},{2,3},{3,2},{4,5},{5,4},{6,7},{7,6},{8,9},{9,8},{10,11... | collective-permute-start | bytes 294920 | tf_op jit(solution)/shard_map/ppermute | solution.py:283
  8.7 1.5 %collective-permute-start.2 = (bf16[128,384]{1,0:T(8,128)(2,1)S(1)}, bf16[128,384]{1,0:T(8,128)(2,1)S(1)}, u32[]{:S(2)}, u32[]{:S(2)}) collective-permute-start(bf16[128,384]{1,0:T(8,128)(2,1)S(1)} %collective-permute-done.1.refs_2_), channel_id=1, source_target_pairs={{0,1},{1,0},{2,3},{3,2},{4,5},{5,4},{6,7},{7,6},{8,9},{9,8},{10,11... | collective-permute-start | bytes 294920 | tf_op jit(solution)/shard_map/ppermute | solution.py:283
  12.8 9.9 %collective-permute-start.3 = (bf16[160,384]{1,0:T(8,128)(2,1)S(1)}, bf16[160,384]{1,0:T(8,128)(2,1)S(1)}, u32[]{:S(2)}, u32[]{:S(2)}) collective-permute-start(bf16[160,384]{1,0:T(8,128)(2,1)S(1)} %get-tuple-element.25), channel_id=1, source_target_pairs={{0,4},{1,5},{2,6},{3,7},{4,0},{5,1},{6,2},{7,3},{8,12},{9,13},{10,... | collective-permute-start | bytes 368648 | tf_op jit(solution)/shard_map/ppermute | solution.py:292
  14.4 8.3 %collective-permute-start.4 = (bf16[160,384]{1,0:T(8,128)(2,1)S(1)}, bf16[160,384]{1,0:T(8,128)(2,1)S(1)}, u32[]{:S(2)}, u32[]{:S(2)}) collective-permute-start(bf16[160,384]{1,0:T(8,128)(2,1)S(1)} %get-tuple-element.26), channel_id=1, source_target_pairs={{0,1},{1,0},{2,3},{3,2},{4,8},{5,9},{6,10},{7,11},{8,4},{9,5},{10,... | collective-permute-start | bytes 368648 | tf_op jit(solution)/shard_map/ppermute | solution.py:292
  14.5 8.2 %collective-permute-start.5 = (bf16[64,384]{1,0:T(8,128)(2,1)S(1)}, bf16[64,384]{1,0:T(8,128)(2,1)S(1)}, u32[]{:S(2)}, u32[]{:S(2)}) collective-permute-start(bf16[64,384]{1,0:T(8,128)(2,1)S(1)} %get-tuple-element.27), channel_id=1, source_target_pairs={{0,8},{1,9},{2,10},{3,11},{4,12},{5,13},{6,14},{7,15},{8,0},{9,1},... | collective-permute-start | bytes 147464 | tf_op jit(solution)/shard_map/ppermute | solution.py:292
  17.0 6.6 %collective-permute-start.8 = (bf16[672,384]{1,0:T(8,128)(2,1)S(1)}, bf16[672,384]{1,0:T(8,128)(2,1)S(1)}, u32[]{:S(2)}, u32[]{:S(2)}) collective-permute-start(bf16[672,384]{1,0:T(8,128)(2,1)S(1)} %get-tuple-element.31.w0), channel_id=1, source_target_pairs={{0,1},{1,0},{2,3},{3,2},{4,5},{5,4},{6,7},{7,6},{8,9},{9,8},{10,11... | collective-permute-start | bytes 1548296 | tf_op jit(solution)/shard_map/ppermute | solution.py:283
  22.7 2.0 %collective-permute-start.10 = (bf16[672,384]{1,0:T(8,128)(2,1)S(1)}, bf16[672,384]{1,0:T(8,128)(2,1)S(1)}, u32[]{:S(2)}, u32[]{:S(2)}) collective-permute-start(bf16[672,384]{1,0:T(8,128)(2,1)S(1)} %collective-permute-done.9.w2), channel_id=1, source_target_pairs={{0,1},{1,0},{2,3},{3,2},{4,5},{5,4},{6,7},{7,6},{8,9},{9,8},{10,11... | collective-permute-start | bytes 1548296 | tf_op jit(solution)/shard_map/ppermute | solution.py:283
  22.8 4.2 %collective-permute-start.7 = (bf16[64,384]{1,0:T(8,128)(2,1)S(1)}, bf16[64,384]{1,0:T(8,128)(2,1)S(1)}, u32[]{:S(2)}, u32[]{:S(2)}) collective-permute-start(bf16[64,384]{1,0:T(8,128)(2,1)S(1)} %get-tuple-element.29), channel_id=1, source_target_pairs={{0,2},{1,3},{2,0},{3,1},{4,6},{5,7},{6,4},{7,5},{8,10},{9,11},{10,... | collective-permute-start | bytes 147464 | tf_op jit(solution)/shard_map/ppermute | solution.py:283
  23.4 3.6 %collective-permute-start.6 = (bf16[64,384]{1,0:T(8,128)(2,1)S(1)}, bf16[64,384]{1,0:T(8,128)(2,1)S(1)}, u32[]{:S(2)}, u32[]{:S(2)}) collective-permute-start(bf16[64,384]{1,0:T(8,128)(2,1)S(1)} %get-tuple-element.28.p0), channel_id=1, source_target_pairs={{0,1},{1,0},{2,3},{3,2},{4,5},{5,4},{6,7},{7,6},{8,9},{9,8},{10,11... | collective-permute-start | bytes 147464 | tf_op jit(solution)/shard_map/ppermute | solution.py:283
  27.0 1.2 %collective-permute-start.11 = (bf16[64,384]{1,0:T(8,128)(2,1)S(1)}, bf16[64,384]{1,0:T(8,128)(2,1)S(1)}, u32[]{:S(2)}, u32[]{:S(2)}) collective-permute-start(bf16[64,384]{1,0:T(8,128)(2,1)S(1)} %collective-permute-done.7.p2), channel_id=1, source_target_pairs={{0,1},{1,0},{2,3},{3,2},{4,5},{5,4},{6,7},{7,6},{8,9},{9,8},{10,11... | collective-permute-start | bytes 147464 | tf_op jit(solution)/shard_map/ppermute | solution.py:283

commit v4 on v3

--- a/solution.py
+++ b/solution.py
@@ -53,15 +53,25 @@
         out[pl.ds(2 * rows + r * width, width), :] = jnp.concatenate([second_here[0, f, r] for f in range(2)], axis=1)
 
 
-def fetch_kernel(packed, first_there, second_there, first, second, second_here, sems):
+def fetch_kernel(
+    packed, first_there, second_there, slots_there, blocks_there, first, second, masks, second_here, slots, blocks, sems
+):
     del packed
     loads = [
         pltpu.make_async_copy(second_there, second_here, sems.at[0]),
-        pltpu.make_async_copy(first_there, first, sems.at[1]),
+        pltpu.make_async_copy(slots_there, slots, sems.at[1]),
+        pltpu.make_async_copy(blocks_there, blocks, sems.at[2]),
+        pltpu.make_async_copy(first_there, first, sems.at[3]),
     ]
     for load in loads:
         load.start()
-    loads[0].wait()
+    for load in loads[:3]:
+        load.wait()
+    me = lax.axis_index("strm")
+    for d in range(4):
+        for e in range(4):
+            chosen = (slots[me ^ d] == me ^ e) & (blocks[me ^ d] > 0)
+            masks[d, e] = jnp.full(masks.shape[2:], jnp.where(chosen, 1.0, 0.0), f32)
     taps, group, channels = 27, second_here.shape[-2], second_here.shape[-1]
     values = second_here[...].reshape(taps * group, channels)
     most = (taps + 1) // 2 * group
@@ -69,35 +79,23 @@
     second[pl.ds(0, rest), :] = jnp.concatenate([values[:rest], values[most:]], axis=1)
     last = values[rest:most]
     second[pl.ds(rest, group), :] = jnp.concatenate([last, last], axis=1)
-    loads[1].wait()
-
-
-def first_kernel(frames, columns, *refs):
-    packs, weight, slots_there, blocks_there = refs[0:4], refs[4], refs[5], refs[6]
-    one, other, two, own, mid = refs[7:12]
-    held, slots, blocks, sems = refs[12:16]
-    loads = [
-        pltpu.make_async_copy(slots_there, slots, sems.at[0]),
-        pltpu.make_async_copy(blocks_there, blocks, sems.at[1]),
-    ]
-    for load in loads:
-        load.start()
-    me = lax.axis_index("strm")
-    upper = me // 2 == 0
-    channels = held.shape[-1]
+    loads[3].wait()
+
+
+def first_kernel(frames, columns, p0, p1, p2, p3, weight, masks, one, other, two, own, mid):
+    packs = (p0, p1, p2, p3)
+    upper = lax.axis_index("strm") // 2 == 0
+    channels = p0.shape[-1]
     outputs = weight.shape[-2]
     half = frames * columns
     width = 2 * columns
-    for d in range(4):
-        held[me ^ d] = packs[d][...]
-    for load in loads:
-        load.wait()
+
+    def chosen(d, at):
+        return sum(jnp.where(masks[d, e] > 0.5, packs[e][at, :].astype(f32), 0.0) for e in range(4))
 
     parts = []
     for d in range(4):
-        stream = me ^ d
-        chosen = held[slots[stream], pl.ds(0, half)].astype(f32)
-        parts.append(jnp.where(blocks[stream] > 0, chosen, 0.0))
+        parts.append(chosen(d, pl.ds(0, half)))
         parts.append(packs[d][pl.ds(half, half), :].astype(f32))
     views = [
         view.astype(bf16).reshape(4, frames + 2, columns, channels)
@@ -114,8 +112,7 @@
 
     u, v, w = [[halves(values[: 2 * half]), halves(values[2 * half :])] for values in sums]
     far_first = sends_far_first()
-    cached = held[slots[me], pl.ds(2 * half, 2 * width)].astype(f32)
-    cached = jnp.where(blocks[me] > 0, cached, 0.0)
+    cached = chosen(0, pl.ds(2 * half, 2 * width))
     mid[...] = cached.astype(bf16)
     edges = [cached[:width], cached[width:]]
     far = u + v + [jnp.where(upper, edges[0], edges[1])]
@@ -143,21 +140,25 @@
     return (place == 0) | (place == lax.axis_size("band") - 1)
 
 
-def sum_kernel(half, own, one, other, two, first_pair, second_pair):
+def sum_kernel(half, own, one, other, two, *pieces):
     me, place, bands = lax.axis_index("strm"), lax.axis_index("band"), lax.axis_size("band")
     upper = me // 2 == 0
     outside = jnp.where(upper, place == bands - 1, place == 0)
     beyond = jnp.where(upper, place >= bands - 2, place <= 1)
     far_first = far_comes_first()
     alone = at_end()
-    for p, pair in enumerate((first_pair, second_pair)):
+    channels = pieces[0].shape[-1]
+    for p in range(2):
         at = pl.ds(p * half, half)
         after = pl.ds((2 + p) * half, half)
         centre = own[at, :] + one[at, :].astype(f32) + jnp.where(alone, 0.0, other[at, :].astype(f32))
         extra = jnp.where(far_first, one[after, :].astype(f32), jnp.where(alone, 0.0, other[after, :].astype(f32)))
         extra = own[after, :] + extra + jnp.where(beyond, 0.0, two[at, :].astype(f32))
-        pair[pl.ds(0, half), :] = centre.astype(bf16)
-        pair[pl.ds(half, half), :] = jnp.where(outside, 0.0, extra).astype(bf16)
+        extra = jnp.where(outside, 0.0, extra)
+        for side in range(2):
+            lanes = slice(side * channels, (side + 1) * channels)
+            pieces[2 * p + side][pl.ds(0, half), :] = centre[:, lanes].astype(bf16)
+            pieces[2 * p + side][pl.ds(half, half), :] = extra[:, lanes].astype(bf16)
 
 
 def cache_kernel(columns, mid, one, other, w0, w1, w2, w3, sums, weights, first_taps):
@@ -188,8 +189,8 @@
     column = lax.broadcasted_iota(jnp.int32, (size, size), 1)
     inside = row % width
     natural = 2 * (inside % columns) + inside // columns
+    both = jnp.zeros((2 * area, channels), f32)
     early = jnp.zeros((area, channels), f32)
-    late = jnp.zeros((area, channels), f32)
     for l in range(3):
         source = natural + (l - 1)
         keep = (source >= 0) & (source < width) & (column == row - inside + source)
@@ -198,18 +199,18 @@
         for j in range(3):
             at = slice(j * width, j * width + area)
             tap = 3 * j + l
-            early = early + dot(c0[at], first_taps[tap], True) + dot(c1[at], weights[tap], True)
-            late = late + dot(c1[at], first_taps[tap], True)
-    sums[0] = early
-    sums[1] = late
+            both = both + dot(jnp.concatenate([c0[at], c1[at]], axis=0), first_taps[tap], True)
+            early = early + dot(c1[at], weights[tap], True)
+    sums[0] = both[:area] + early
+    sums[1] = both[area:]
 
 
 def second_kernel(frames, columns, p0, p1, p2, p3, sums, weights, gain, out, quarters):
     me = lax.axis_index("strm")
     channels = out.shape[-1]
     width = 2 * columns
-    for e, pair in enumerate((p0, p1, p2, p3)):
-        quarters[me ^ e] = pair[:, (e % 2) * channels : (e % 2 + 1) * channels]
+    for e, piece in enumerate((p0, p1, p2, p3)):
+        quarters[me ^ e] = piece[...]
 
     fields = [quarters[q].astype(f32).reshape(2, frames, columns, channels) for q in range(4)]
     row_of = ((1, 1), (0, 0), (1, 0), (0, 1))
@@ -230,20 +231,21 @@
         split(same[:, :, 1], right[:, :, 0]),
     ]
     area = 2 * width
-    early, late = sums[0], sums[1]
+    both = sums[...].reshape(2 * area, channels)
+    late = jnp.zeros((area, channels), f32)
     for j in range(3):
         for l in range(3):
-            a0, a1 = [views[l][f, j : j + 2].reshape(area, channels) for f in range(2)]
+            window = views[l][:, j : j + 2].reshape(2 * area, channels)
             tap = 3 * j + l
-            early = early + dot(a0, weights[9 + tap], True)
-            late = late + dot(a0, weights[tap], True) + dot(a1, weights[9 + tap], True)
+            both = both + dot(window, weights[9 + tap], True)
+            late = late + dot(window[:area], weights[tap], True)
 
     row = lax.broadcasted_iota(jnp.int32, (area, area), 0)
     column = lax.broadcasted_iota(jnp.int32, (area, area), 1)
     inside = row % width
     keep = column == row - inside + (inside % 2) * columns + inside // 2
     order = jnp.where(keep, 1.0, 0.0).astype(bf16)
-    for t, branch in enumerate((early, late)):
+    for t, branch in enumerate((both[:area], both[area:] + late)):
         base = upsampled[t, 1:3].reshape(area, channels)
         decoded = (base + branch.astype(bf16).astype(f32)).astype(bf16)
         out[0, t] = dot(order, decoded).astype(bf16).reshape(2, width, channels)
@@ -323,15 +325,20 @@
         ],
     )(*map(there, (latents, cache_first, cache_second, gain_first)))
     across = swapped(packed, 2)
-    weight_first, weight_own = call(
+    weight_first, weight_own, masks = call(
         fetch_kernel,
         "fetch",
         16,
-        out_shape=[struct(turned_first.shape), struct((14 * group, 2 * outputs))],
-        in_specs=whole(1) + [THERE] * 2,
-        out_specs=whole(2),
-        scratch_shapes=[pltpu.VMEM(turned_second.shape, bf16), pltpu.SemaphoreType.DMA((2,))],
-    )(packed, there(turned_first), there(turned_second))
+        out_shape=[struct(turned_first.shape), struct((14 * group, 2 * outputs)), struct((4, 4, 1, channels), f32)],
+        in_specs=whole(1) + [THERE] * 4,
+        out_specs=whole(3),
+        scratch_shapes=[
+            pltpu.VMEM(turned_second.shape, bf16),
+            pltpu.SMEM(cache_slot.shape, jnp.int32),
+            pltpu.SMEM(block_index.shape, jnp.int32),
+            pltpu.SemaphoreType.DMA((4,)),
+        ],
+    )(packed, *map(there, (turned_first, turned_second, cache_slot, block_index)))
     weight_own, across = lax.optimization_barrier((weight_own, across))
     packs = [packed, swapped(packed, 1), across, swapped(across, 1)]
     weights = [weight_own, swapped(weight_own, 1), swapped(weight_own, 2)]
@@ -342,27 +349,21 @@
         "first_conv",
         16,
         out_shape=[payload, payload, pair, struct((4 * half, 2 * outputs), f32), struct((2 * width, 2 * outputs))],
-        in_specs=whole(5) + [THERE] * 2,
+        in_specs=whole(6),
         out_specs=whole(5),
-        scratch_shapes=[
-            pltpu.VMEM((4,) + packed.shape, bf16),
-            pltpu.SMEM(cache_slot.shape, jnp.int32),
-            pltpu.SMEM(block_index.shape, jnp.int32),
-            pltpu.SemaphoreType.DMA((2,)),
-        ],
-    )(*packs, weight_first, there(cache_slot), there(block_index))
+    )(*packs, weight_first, masks)
     one, other, two = along(one, first_way), along(other, second_way), along(two, third_way)
-    first_pair, second_pair = call(
+    pieces = call(
         functools.partial(sum_kernel, half),
         "row_sums",
         4,
-        out_shape=[pair, pair],
+        out_shape=[struct((2 * half, outputs))] * 4,
         in_specs=whole(4),
-        out_specs=whole(2),
+        out_specs=whole(4),
     )(own, one, other, two)
-    weight_across, _ = lax.optimization_barrier((weights[2], first_pair))
+    weight_across, _ = lax.optimization_barrier((weights[2], pieces[0]))
     weights.append(swapped(weight_across, 1))
-    across = swapped(second_pair, 2)
+    pieces = [pieces[0]] + [swapped(pieces[d], d) for d in (1, 2, 3)]
     sums, taps = call(
         functools.partial(cache_kernel, columns),
         "cached_conv",
@@ -372,8 +373,6 @@
         out_specs=whole(2),
         scratch_shapes=[pltpu.VMEM((9, outputs, outputs), bf16)],
     )(mid, one, other, *weights)
-    across, sums = lax.optimization_barrier((across, sums))
-    pairs = [first_pair, swapped(first_pair, 1), across, swapped(across, 1)]
     return call(
         functools.partial(second_kernel, frames, columns),
         "second_conv",
@@ -382,7 +381,7 @@
         in_specs=whole(7),
         out_specs=whole(1)[0],
         scratch_shapes=[pltpu.VMEM((4, 2 * half, outputs), bf16)],
-    )(*pairs, sums, taps, gain_second)
+    )(*pieces, sums, taps, gain_second)
 
 
 def solution(mesh):

time: 30.2 us -> 28.5 us (0.944)
  waiting for transfers between devices: 9.45 us -> 7.88 us
  Pallas kernels: 10 us -> 8.8 us
  starting transfers between devices: 10.5 us -> 11.6 us
    ppermute x9, waiting for transfers between devices: 3.8 us -> 2.22 us  [swapped(): lax.ppermute(value, 'strm', [(i, i ^ distance) for i in range(streams)])]
    ppermute x9, starting transfers between devices: 6.24 us -> 7.34 us  [swapped(): lax.ppermute(value, 'strm', [(i, i ^ distance) for i in range(streams)])]
    pallas_call x1, Pallas kernels: 2.63 us -> 1.88 us  [body(): call(functools.partial(first_kernel, frames, columns), 'first_conv', 16,...]
    pallas_call x1, Pallas kernels: 1.85 us -> 1.48 us  [body(): call(functools.partial(second_kernel, frames, columns), 'second_conv', 16...]
  transfers between devices with their start and end apart: 12 -> 12, of which waited for: 7 -> 5; matrix products, arithmetic and copies ran while one was open for 0% -> 0% of each run, Pallas kernels for 24% -> 22%
where the time goes in v4:
time: 28.5 us; the launch traced here: 28.3 us
  starting transfers between devices  11.6 us (41%)
  Pallas kernels  8.8 us (31%)
  waiting for transfers between devices  7.88 us (28%)
    ppermute x9, starting transfers between devices, swapped(): lax.ppermute(value, 'strm', [(i, i ^ distance) for i in range(streams)])  7.34 us
    ppermute x3, waiting for transfers between devices, along(): return lax.ppermute(value, ('band', 'strm'), pairs)  5.66 us
    ppermute x3, starting transfers between devices, along(): return lax.ppermute(value, ('band', 'strm'), pairs)  4.23 us
    pallas_call x1, Pallas kernels, body(): call(fetch_kernel, 'fetch', 16, out_shape=[struct(turned_first.shape), st...  2.37 us
    ppermute x9, waiting for transfers between devices, swapped(): lax.ppermute(value, 'strm', [(i, i ^ distance) for i in range(streams)])  2.22 us
    pallas_call x1, Pallas kernels, body(): call(functools.partial(cache_kernel, columns), 'cached_conv', 16, out_sha...  1.91 us
    pallas_call x1, Pallas kernels, body(): call(functools.partial(first_kernel, frames, columns), 'first_conv', 16,...  1.88 us
    pallas_call x1, Pallas kernels, body(): call(functools.partial(second_kernel, frames, columns), 'second_conv', 16...  1.48 us
  transfers between devices with their start and end apart: 12, of which 5 were waited for; matrix products, arithmetic and copies ran while one was open for 0% of the time, Pallas kernels for 22%

profile of v4, /device:TPU:0, one launch (start us, length us, event | category | flops | bytes accessed | tf_op | source)
XLA Modules:
  0.0 28.3 jit_solution(172494973922384723)
XLA Ops:
  0.0 1.0 %pack.1.packed.p0 = bf16[128,384]{1,0:T(8,128)(2,1)S(1)} custom-call(bf16[1,2,1,16,384]{4,3,2,1,0:T(8,128)(2,1)} %latents.1, bf16[1,2,1,16,384]{4,3,2,1,0:T(8,128)(2,1)} %first.1, bf16[1,2,2,32,192]{4,3,2,1,0:T(8,128)(2,1)} %second.1, f32[384]{0:T(512)} %gain_there.1), custom_call_target="tpu_custom_call" | custom-call | tf_op jit(solution)/shard_map/pack/pallas_call | solution.py:312
  1.0 3.0 %collective-permute-start.1 = (bf16[128,384]{1,0:T(8,128)(2,1)S(1)}, bf16[128,384]{1,0:T(8,128)(2,1)S(1)}, u32[]{:S(2)}, u32[]{:S(2)}) collective-permute-start(bf16[128,384]{1,0:T(8,128)(2,1)S(1)} %pack.1.packed.p0), channel_id=1, source_target_pairs={{0,2},{1,3},{2,0},{3,1},{4,6},{5,7},{6,4},{7,5},{8,10},{9,11},{10,... | collective-permute-start | bytes 294920 | tf_op jit(solution)/shard_map/ppermute | solution.py:285
  4.0 2.4 %fetch.1 = (bf16[3,3,3,192,384]{4,3,2,1,0:T(8,128)(2,1)S(1)}, bf16[672,384]{1,0:T(8,128)(2,1)S(1)}, f32[4,4,1,384]{3,2,1,0:T(1,128)S(1)}) custom-call(bf16[128,384]{1,0:T(8,128)(2,1)S(1)} %pack.1.packed.p0, bf16[3,3,3,192,384]{4,3,2,1,0:T(8,128)(2,1)} %bitcast.2, bf16[3,3,3,48,192]{4,3,2,1,0:T(8,128)(2,1)} %bitcast.3, s32[4]{0:T(128)} %slots_there.1, ...), custom_call_target="tpu_custom_call" | custom-call | tf_op jit(solution)/shard_map/fetch/pallas_call | solution.py:328
  6.4 0.0 copy-start
  6.4 0.4 %collective-permute-done.1.p2 = bf16[128,384]{1,0:T(8,128)(2,1)S(1)} collective-permute-done((bf16[128,384]{1,0:T(8,128)(2,1)S(1)}, bf16[128,384]{1,0:T(8,128)(2,1)S(1)}, u32[]{:S(2)}, u32[]{:S(2)}) %collective-permute-start.1) | collective-permute-done | bytes 98336 | tf_op jit(solution)/shard_map/ppermute | solution.py:285
  6.8 1.8 %collective-permute-start.10 = (bf16[672,384]{1,0:T(8,128)(2,1)S(1)}, bf16[672,384]{1,0:T(8,128)(2,1)S(1)}, u32[]{:S(2)}, u32[]{:S(2)}) collective-permute-start(bf16[672,384]{1,0:T(8,128)(2,1)S(1)} %get-tuple-element.35.w0), channel_id=1, source_target_pairs={{0,2},{1,3},{2,0},{3,1},{4,6},{5,7},{6,4},{7,5},{8,10},{9,11},{10,... | collective-permute-start | bytes 1548296 | tf_op jit(solution)/shard_map/ppermute | solution.py:285
  8.7 0.0 collective-permute-start
  8.7 0.5 %collective-permute-start.2 = (bf16[128,384]{1,0:T(8,128)(2,1)S(1)}, bf16[128,384]{1,0:T(8,128)(2,1)S(1)}, u32[]{:S(2)}, u32[]{:S(2)}) collective-permute-start(bf16[128,384]{1,0:T(8,128)(2,1)S(1)} %collective-permute-done.1.p2), channel_id=1, source_target_pairs={{0,1},{1,0},{2,3},{3,2},{4,5},{5,4},{6,7},{7,6},{8,9},{9,8},{10,11... | collective-permute-start | bytes 294920 | tf_op jit(solution)/shard_map/ppermute | solution.py:285
  9.2 0.8 %collective-permute-done.p1 = bf16[128,384]{1,0:T(8,128)(2,1)S(1)} collective-permute-done((bf16[128,384]{1,0:T(8,128)(2,1)S(1)}, bf16[128,384]{1,0:T(8,128)(2,1)S(1)}, u32[]{:S(2)}, u32[]{:S(2)}) %collective-permute-start) | collective-permute-done | bytes 98336 | tf_op jit(solution)/shard_map/ppermute | solution.py:285
  10.0 0.2 collective-permute-done.2.p3
  10.1 1.9 %first_conv.1 = (bf16[160,384]{1,0:T(8,128)(2,1)S(1)}, bf16[160,384]{1,0:T(8,128)(2,1)S(1)}, bf16[64,384]{1,0:T(8,128)(2,1)S(1)}, f32[128,384]{1,0:T(8,128)S(1)}, bf16[64,384]{1,0:T(8,128)(2,1)S(1)}) custom-call(bf16[128,384]{1,0:T(8,128)(2,1)S(1)} %pack.1.packed.p0, bf16[128,384]{1,0:T(8,128)(2,1)S(1)} %collective-permute-done.p1, ...), custom_call_target="tpu_custom_call" | custom-call | tf_op jit(solution)/shard_map/first_conv/pallas_call | solution.py:347
  12.0 1.7 %collective-permute-start.3 = (bf16[160,384]{1,0:T(8,128)(2,1)S(1)}, bf16[160,384]{1,0:T(8,128)(2,1)S(1)}, u32[]{:S(2)}, u32[]{:S(2)}) collective-permute-start(bf16[160,384]{1,0:T(8,128)(2,1)S(1)} %get-tuple-element.27), channel_id=1, source_target_pairs={{0,4},{1,5},{2,6},{3,7},{4,0},{5,1},{6,2},{7,3},{8,12},{9,13},{10,... | collective-permute-start | bytes 368648 | tf_op jit(solution)/shard_map/ppermute | solution.py:294
  13.7 0.1 collective-permute-start.4
  13.7 2.5 %collective-permute-start.5 = (bf16[64,384]{1,0:T(8,128)(2,1)S(1)}, bf16[64,384]{1,0:T(8,128)(2,1)S(1)}, u32[]{:S(2)}, u32[]{:S(2)}) collective-permute-start(bf16[64,384]{1,0:T(8,128)(2,1)S(1)} %get-tuple-element.29), channel_id=1, source_target_pairs={{0,8},{1,9},{2,10},{3,11},{4,12},{5,13},{6,14},{7,15},{8,0},{9,1},... | collective-permute-start | bytes 147464 | tf_op jit(solution)/shard_map/ppermute | solution.py:294
  16.2 0.0 collective-permute-start.9
  16.2 5.7 %collective-permute-done.5.two = bf16[64,384]{1,0:T(8,128)(2,1)S(1)} collective-permute-done((bf16[64,384]{1,0:T(8,128)(2,1)S(1)}, bf16[64,384]{1,0:T(8,128)(2,1)S(1)}, u32[]{:S(2)}, u32[]{:S(2)}) %collective-permute-start.5) | collective-permute-done | bytes 49184 | tf_op jit(solution)/shard_map/ppermute | solution.py:294
  21.9 0.0 collective-permute-done.3.one
  21.9 0.0 collective-permute-done.4.other
  21.9 0.1 row_sums.1
  22.0 0.0 collective-permute-done.10.w2
  22.0 0.1 collective-permute-start.11
  22.1 0.5 %collective-permute-start.6 = (bf16[64,192]{1,0:T(8,128)(2,1)S(1)}, bf16[64,192]{1,0:T(8,128)(2,1)S(1)}, u32[]{:S(2)}, u32[]{:S(2)}) collective-permute-start(bf16[64,192]{1,0:T(8,128)(2,1)S(1)} %get-tuple-element.31), channel_id=1, source_target_pairs={{0,1},{1,0},{2,3},{3,2},{4,5},{5,4},{6,7},{7,6},{8,9},{9,8},{10,11... | collective-permute-start | bytes 73736 | tf_op jit(solution)/shard_map/ppermute | solution.py:285
  22.6 0.5 %collective-permute-start.7 = (bf16[64,192]{1,0:T(8,128)(2,1)S(1)}, bf16[64,192]{1,0:T(8,128)(2,1)S(1)}, u32[]{:S(2)}, u32[]{:S(2)}) collective-permute-start(bf16[64,192]{1,0:T(8,128)(2,1)S(1)} %get-tuple-element.32), channel_id=1, source_target_pairs={{0,2},{1,3},{2,0},{3,1},{4,6},{5,7},{6,4},{7,5},{8,10},{9,11},{10,... | collective-permute-start | bytes 73736 | tf_op jit(solution)/shard_map/ppermute | solution.py:285
  23.1 0.9 %collective-permute-start.8 = (bf16[64,192]{1,0:T(8,128)(2,1)S(1)}, bf16[64,192]{1,0:T(8,128)(2,1)S(1)}, u32[]{:S(2)}, u32[]{:S(2)}) collective-permute-start(bf16[64,192]{1,0:T(8,128)(2,1)S(1)} %get-tuple-element.33), channel_id=1, source_target_pairs={{0,3},{1,2},{2,1},{3,0},{4,7},{5,6},{6,5},{7,4},{8,11},{9,10},{10,... | collective-permute-start | bytes 73736 | tf_op jit(solution)/shard_map/ppermute | solution.py:285
  24.0 0.0 collective-permute-done.9.w1
  24.1 0.0 collective-permute-done.11.w3
  24.1 1.9 %cached_conv.1 = (f32[2,64,192]{2,1,0:T(8,128)S(1)}, bf16[18,192,192]{2,1,0:T(8,128)(2,1)S(1)}) custom-call(bf16[64,384]{1,0:T(8,128)(2,1)S(1)} %get-tuple-element.34.mid, bf16[160,384]{1,0:T(8,128)(2,1)S(1)} %collective-permute-done.3.one, bf16[160,384]{1,0:T(8,128)(2,1)S(1)} %collective-permute-done.4.other, bf16[672,384]{1,0:T(8,128)(2,1)S(1)} %get-tuple-element.35.w0, ...), custom_call_target="tpu_custom_call" | custom-call | tf_op jit(solution)/shard_map/cached_conv/pallas_call | solution.py:367
  26.0 0.0 collective-permute-done.6.p1
  26.0 0.9 %collective-permute-done.7.p2 = bf16[64,192]{1,0:T(8,128)(2,1)S(1)} collective-permute-done((bf16[64,192]{1,0:T(8,128)(2,1)S(1)}, bf16[64,192]{1,0:T(8,128)(2,1)S(1)}, u32[]{:S(2)}, u32[]{:S(2)}) %collective-permute-start.7) | collective-permute-done | bytes 24608 | tf_op jit(solution)/shard_map/ppermute | solution.py:285
  26.8 0.0 collective-permute-done.8.p3
  26.8 0.0 copy-done
  26.8 1.5 %second_conv.1 = bf16[1,2,2,32,192]{4,3,2,1,0:T(8,128)(2,1)} custom-call(bf16[64,192]{1,0:T(8,128)(2,1)S(1)} %get-tuple-element.30.p0, bf16[64,192]{1,0:T(8,128)(2,1)S(1)} %collective-permute-done.6.p1, bf16[64,192]{1,0:T(8,128)(2,1)S(1)} %collective-permute-done.7.p2, bf16[64,192]{1,0:T(8,128)(2,1)S(1)} %collective-permute-done.8.p3, ...), custom_call_target="tpu_custom_call" | custom-call | tf_op jit(solution)/shard_map/second_conv/pallas_call | solution.py:376
Async XLA Ops:
  1.0 5.8 %collective-permute-start.1 = (bf16[128,384]{1,0:T(8,128)(2,1)S(1)}, bf16[128,384]{1,0:T(8,128)(2,1)S(1)}, u32[]{:S(2)}, u32[]{:S(2)}) collective-permute-start(bf16[128,384]{1,0:T(8,128)(2,1)S(1)} %pack.1.packed.p0), channel_id=1, source_target_pairs={{0,2},{1,3},{2,0},{3,1},{4,6},{5,7},{6,4},{7,5},{8,10},{9,11},{10,... | collective-permute-start | bytes 294920 | tf_op jit(solution)/shard_map/ppermute | solution.py:285
  6.4 20.4 %copy-start = (f32[192]{0:T(256)S(1)}, f32[192]{0:T(256)}, u32[]{:S(2)}) copy-start(f32[192]{0:T(256)} %gain.1) | copy-start | bytes 2308
  6.8 15.2 %collective-permute-start.10 = (bf16[672,384]{1,0:T(8,128)(2,1)S(1)}, bf16[672,384]{1,0:T(8,128)(2,1)S(1)}, u32[]{:S(2)}, u32[]{:S(2)}) collective-permute-start(bf16[672,384]{1,0:T(8,128)(2,1)S(1)} %get-tuple-element.35.w0), channel_id=1, source_target_pairs={{0,2},{1,3},{2,0},{3,1},{4,6},{5,7},{6,4},{7,5},{8,10},{9,11},{10,... | collective-permute-start | bytes 1548296 | tf_op jit(solution)/shard_map/ppermute | solution.py:285
  8.7 1.3 %collective-permute-start = (bf16[128,384]{1,0:T(8,128)(2,1)S(1)}, bf16[128,384]{1,0:T(8,128)(2,1)S(1)}, u32[]{:S(2)}, u32[]{:S(2)}) collective-permute-start(bf16[128,384]{1,0:T(8,128)(2,1)S(1)} %pack.1.packed.p0), channel_id=1, source_target_pairs={{0,1},{1,0},{2,3},{3,2},{4,5},{5,4},{6,7},{7,6},{8,9},{9,8},{10,11... | collective-permute-start | bytes 294920 | tf_op jit(solution)/shard_map/ppermute | solution.py:285
  8.7 1.5 %collective-permute-start.2 = (bf16[128,384]{1,0:T(8,128)(2,1)S(1)}, bf16[128,384]{1,0:T(8,128)(2,1)S(1)}, u32[]{:S(2)}, u32[]{:S(2)}) collective-permute-start(bf16[128,384]{1,0:T(8,128)(2,1)S(1)} %collective-permute-done.1.p2), channel_id=1, source_target_pairs={{0,1},{1,0},{2,3},{3,2},{4,5},{5,4},{6,7},{7,6},{8,9},{9,8},{10,11... | collective-permute-start | bytes 294920 | tf_op jit(solution)/shard_map/ppermute | solution.py:285
  12.0 9.9 %collective-permute-start.3 = (bf16[160,384]{1,0:T(8,128)(2,1)S(1)}, bf16[160,384]{1,0:T(8,128)(2,1)S(1)}, u32[]{:S(2)}, u32[]{:S(2)}) collective-permute-start(bf16[160,384]{1,0:T(8,128)(2,1)S(1)} %get-tuple-element.27), channel_id=1, source_target_pairs={{0,4},{1,5},{2,6},{3,7},{4,0},{5,1},{6,2},{7,3},{8,12},{9,13},{10,... | collective-permute-start | bytes 368648 | tf_op jit(solution)/shard_map/ppermute | solution.py:294
  13.7 8.2 %collective-permute-start.4 = (bf16[160,384]{1,0:T(8,128)(2,1)S(1)}, bf16[160,384]{1,0:T(8,128)(2,1)S(1)}, u32[]{:S(2)}, u32[]{:S(2)}) collective-permute-start(bf16[160,384]{1,0:T(8,128)(2,1)S(1)} %get-tuple-element.28), channel_id=1, source_target_pairs={{0,1},{1,0},{2,3},{3,2},{4,8},{5,9},{6,10},{7,11},{8,4},{9,5},{10,... | collective-permute-start | bytes 368648 | tf_op jit(solution)/shard_map/ppermute | solution.py:294
  13.7 8.2 %collective-permute-start.5 = (bf16[64,384]{1,0:T(8,128)(2,1)S(1)}, bf16[64,384]{1,0:T(8,128)(2,1)S(1)}, u32[]{:S(2)}, u32[]{:S(2)}) collective-permute-start(bf16[64,384]{1,0:T(8,128)(2,1)S(1)} %get-tuple-element.29), channel_id=1, source_target_pairs={{0,8},{1,9},{2,10},{3,11},{4,12},{5,13},{6,14},{7,15},{8,0},{9,1},... | collective-permute-start | bytes 147464 | tf_op jit(solution)/shard_map/ppermute | solution.py:294
  16.2 7.8 %collective-permute-start.9 = (bf16[672,384]{1,0:T(8,128)(2,1)S(1)}, bf16[672,384]{1,0:T(8,128)(2,1)S(1)}, u32[]{:S(2)}, u32[]{:S(2)}) collective-permute-start(bf16[672,384]{1,0:T(8,128)(2,1)S(1)} %get-tuple-element.35.w0), channel_id=1, source_target_pairs={{0,1},{1,0},{2,3},{3,2},{4,5},{5,4},{6,7},{7,6},{8,9},{9,8},{10,11... | collective-permute-start | bytes 1548296 | tf_op jit(solution)/shard_map/ppermute | solution.py:285
  22.0 2.0 %collective-permute-start.11 = (bf16[672,384]{1,0:T(8,128)(2,1)S(1)}, bf16[672,384]{1,0:T(8,128)(2,1)S(1)}, u32[]{:S(2)}, u32[]{:S(2)}) collective-permute-start(bf16[672,384]{1,0:T(8,128)(2,1)S(1)} %collective-permute-done.10.w2), channel_id=1, source_target_pairs={{0,1},{1,0},{2,3},{3,2},{4,5},{5,4},{6,7},{7,6},{8,9},{9,8},{10,11... | collective-permute-start | bytes 1548296 | tf_op jit(solution)/shard_map/ppermute | solution.py:285
  22.1 3.9 %collective-permute-start.6 = (bf16[64,192]{1,0:T(8,128)(2,1)S(1)}, bf16[64,192]{1,0:T(8,128)(2,1)S(1)}, u32[]{:S(2)}, u32[]{:S(2)}) collective-permute-start(bf16[64,192]{1,0:T(8,128)(2,1)S(1)} %get-tuple-element.31), channel_id=1, source_target_pairs={{0,1},{1,0},{2,3},{3,2},{4,5},{5,4},{6,7},{7,6},{8,9},{9,8},{10,11... | collective-permute-start | bytes 73736 | tf_op jit(solution)/shard_map/ppermute | solution.py:285
  22.6 4.2 %collective-permute-start.7 = (bf16[64,192]{1,0:T(8,128)(2,1)S(1)}, bf16[64,192]{1,0:T(8,128)(2,1)S(1)}, u32[]{:S(2)}, u32[]{:S(2)}) collective-permute-start(bf16[64,192]{1,0:T(8,128)(2,1)S(1)} %get-tuple-element.32), channel_id=1, source_target_pairs={{0,2},{1,3},{2,0},{3,1},{4,6},{5,7},{6,4},{7,5},{8,10},{9,11},{10,... | collective-permute-start | bytes 73736 | tf_op jit(solution)/shard_map/ppermute | solution.py:285
  23.1 3.7 %collective-permute-start.8 = (bf16[64,192]{1,0:T(8,128)(2,1)S(1)}, bf16[64,192]{1,0:T(8,128)(2,1)S(1)}, u32[]{:S(2)}, u32[]{:S(2)}) collective-permute-start(bf16[64,192]{1,0:T(8,128)(2,1)S(1)} %get-tuple-element.33), channel_id=1, source_target_pairs={{0,3},{1,2},{2,1},{3,0},{4,7},{5,6},{6,5},{7,4},{8,11},{9,10},{10,... | collective-permute-start | bytes 73736 | tf_op jit(solution)/shard_map/ppermute | solution.py:285

commit v5 on v4

--- a/solution.py
+++ b/solution.py
@@ -262,9 +262,10 @@
     return pltpu.with_memory_space_constraint(value, pltpu.HBM)
 
 
-def call(kernel, name, megabytes, **settings):
+def call(kernel, name, megabytes, microseconds=1, **settings):
+    cost = pl.CostEstimate(flops=int(microseconds * 1e9), bytes_accessed=0, transcendentals=0)
     return pl.pallas_call(
-        kernel, name=name, compiler_params=pltpu.CompilerParams(vmem_limit_bytes=megabytes * 2**20), **settings
+        kernel, name=name, cost_estimate=cost, compiler_params=pltpu.CompilerParams(vmem_limit_bytes=megabytes * 2**20), **settings
     )
 
 
@@ -329,6 +330,7 @@
         fetch_kernel,
         "fetch",
         16,
+        0.05,
         out_shape=[struct(turned_first.shape), struct((14 * group, 2 * outputs)), struct((4, 4, 1, channels), f32)],
         in_specs=whole(1) + [THERE] * 4,
         out_specs=whole(3),
@@ -339,7 +341,7 @@
             pltpu.SemaphoreType.DMA((4,)),
         ],
     )(packed, *map(there, (turned_first, turned_second, cache_slot, block_index)))
-    weight_own, across = lax.optimization_barrier((weight_own, across))
+    weight_first, across = lax.optimization_barrier((weight_first, across))
     packs = [packed, swapped(packed, 1), across, swapped(across, 1)]
     weights = [weight_own, swapped(weight_own, 1), swapped(weight_own, 2)]
     pair = struct((2 * half, 2 * outputs))
@@ -348,6 +350,7 @@
         functools.partial(first_kernel, frames, columns),
         "first_conv",
         16,
+        2,
         out_shape=[payload, payload, pair, struct((4 * half, 2 * outputs), f32), struct((2 * width, 2 * outputs))],
         in_specs=whole(6),
         out_specs=whole(5),
@@ -357,22 +360,26 @@
         functools.partial(sum_kernel, half),
         "row_sums",
         4,
+        1,
         out_shape=[struct((2 * half, outputs))] * 4,
         in_specs=whole(4),
         out_specs=whole(4),
     )(own, one, other, two)
     weight_across, _ = lax.optimization_barrier((weights[2], pieces[0]))
     weights.append(swapped(weight_across, 1))
-    pieces = [pieces[0]] + [swapped(pieces[d], d) for d in (1, 2, 3)]
+    across, beyond = swapped(pieces[2], 2), swapped(pieces[3], 3)
     sums, taps = call(
         functools.partial(cache_kernel, columns),
         "cached_conv",
         16,
+        1,
         out_shape=[struct((2, 2 * width, outputs), f32), struct((18, outputs, outputs))],
         in_specs=whole(7),
         out_specs=whole(2),
         scratch_shapes=[pltpu.VMEM((9, outputs, outputs), bf16)],
     )(mid, one, other, *weights)
+    beside, sums = lax.optimization_barrier((pieces[1], sums))
+    pieces = [pieces[0], swapped(beside, 1), across, beyond]
     return call(
         functools.partial(second_kernel, frames, columns),
         "second_conv",

time: 28.5 us -> 27.2 us (0.954)
  starting transfers between devices: 11.6 us -> 10.3 us
    ppermute x9, starting transfers between devices: 7.34 us -> 5.73 us  [swapped(): lax.ppermute(value, 'strm', [(i, i ^ distance) for i in range(streams)])]
    ppermute x3, starting transfers between devices: 4.23 us -> 4.58 us  [along(): return lax.ppermute(value, ('band', 'strm'), pairs)]
  transfers between devices with their start and end apart: 12 -> 12, of which waited for: 5 -> 6; matrix products, arithmetic and copies ran while one was open for 0% -> 0% of each run, Pallas kernels for 22% -> 23%
where the time goes in v5:
time: 27.2 us; the launch traced here: 27 us
  starting transfers between devices  10.3 us (38%)
  Pallas kernels  8.78 us (32%)
  waiting for transfers between devices  7.87 us (29%)
    ppermute x9, starting transfers between devices, swapped(): lax.ppermute(value, 'strm', [(i, i ^ distance) for i in range(streams)])  5.73 us
    ppermute x3, waiting for transfers between devices, along(): return lax.ppermute(value, ('band', 'strm'), pairs)  5.66 us
    ppermute x3, starting transfers between devices, along(): return lax.ppermute(value, ('band', 'strm'), pairs)  4.58 us
    pallas_call x1, Pallas kernels, body(): call(fetch_kernel, 'fetch', 16, 0.05, out_shape=[struct(turned_first.shap...  2.37 us
    ppermute x9, waiting for transfers between devices, swapped(): lax.ppermute(value, 'strm', [(i, i ^ distance) for i in range(streams)])  2.21 us
    pallas_call x1, Pallas kernels, body(): call(functools.partial(cache_kernel, columns), 'cached_conv', 16, 1, out_...  1.9 us
    pallas_call x1, Pallas kernels, body(): call(functools.partial(first_kernel, frames, columns), 'first_conv', 16,...  1.87 us
    pallas_call x1, Pallas kernels, body(): call(functools.partial(second_kernel, frames, columns), 'second_conv', 16...  1.48 us
  transfers between devices with their start and end apart: 12, of which 6 were waited for; matrix products, arithmetic and copies ran while one was open for 0% of the time, Pallas kernels for 23%

profile of v5, /device:TPU:0, one launch (start us, length us, event | category | flops | bytes accessed | tf_op | source)
XLA Modules:
  0.0 27.0 jit_solution(10364358301542396062)
XLA Ops:
  0.0 1.0 %pack.1.packed.p0 = bf16[128,384]{1,0:T(8,128)(2,1)S(1)} custom-call(bf16[1,2,1,16,384]{4,3,2,1,0:T(8,128)(2,1)} %latents.1, bf16[1,2,1,16,384]{4,3,2,1,0:T(8,128)(2,1)} %first.1, bf16[1,2,2,32,192]{4,3,2,1,0:T(8,128)(2,1)} %second.1, f32[384]{0:T(512)} %gain_there.1), custom_call_target="tpu_custom_call" | custom-call | flops 1000000000 | tf_op jit(solution)/shard_map/pack/pallas_call | solution.py:313
  1.0 3.0 %collective-permute-start.1 = (bf16[128,384]{1,0:T(8,128)(2,1)S(1)}, bf16[128,384]{1,0:T(8,128)(2,1)S(1)}, u32[]{:S(2)}, u32[]{:S(2)}) collective-permute-start(bf16[128,384]{1,0:T(8,128)(2,1)S(1)} %pack.1.packed.p0), channel_id=1, source_target_pairs={{0,2},{1,3},{2,0},{3,1},{4,6},{5,7},{6,4},{7,5},{8,10},{9,11},{10,... | collective-permute-start | bytes 294920 | tf_op jit(solution)/shard_map/ppermute | solution.py:286
  4.0 2.4 %fetch.1 = (bf16[3,3,3,192,384]{4,3,2,1,0:T(8,128)(2,1)S(1)}, bf16[672,384]{1,0:T(8,128)(2,1)S(1)}, f32[4,4,1,384]{3,2,1,0:T(1,128)S(1)}) custom-call(bf16[128,384]{1,0:T(8,128)(2,1)S(1)} %pack.1.packed.p0, bf16[3,3,3,192,384]{4,3,2,1,0:T(8,128)(2,1)} %bitcast.2, bf16[3,3,3,48,192]{4,3,2,1,0:T(8,128)(2,1)} %bitcast.3, s32[4]{0:T(128)} %slots_there.1, ...), custom_call_target="tpu_custom_call" | custom-call | flops 50000000 | tf_op jit(solution)/shard_map/fetch/pallas_call | solution.py:329
  6.4 0.1 collective-permute-start.7
  6.5 0.1 collective-permute-start
  6.6 0.3 collective-permute-done.1.p2
  6.8 0.2 collective-permute-start.2
  7.1 0.8 %collective-permute-done.p1 = bf16[128,384]{1,0:T(8,128)(2,1)S(1)} collective-permute-done((bf16[128,384]{1,0:T(8,128)(2,1)S(1)}, bf16[128,384]{1,0:T(8,128)(2,1)S(1)}, u32[]{:S(2)}, u32[]{:S(2)}) %collective-permute-start) | collective-permute-done | bytes 98336 | tf_op jit(solution)/shard_map/ppermute | solution.py:286
  7.9 0.3 %collective-permute-done.2.p3 = bf16[128,384]{1,0:T(8,128)(2,1)S(1)} collective-permute-done((bf16[128,384]{1,0:T(8,128)(2,1)S(1)}, bf16[128,384]{1,0:T(8,128)(2,1)S(1)}, u32[]{:S(2)}, u32[]{:S(2)}) %collective-permute-start.2) | collective-permute-done | bytes 98336 | tf_op jit(solution)/shard_map/ppermute | solution.py:286
  8.1 1.9 %first_conv.1 = (bf16[160,384]{1,0:T(8,128)(2,1)S(1)}, bf16[160,384]{1,0:T(8,128)(2,1)S(1)}, bf16[64,384]{1,0:T(8,128)(2,1)S(1)}, f32[128,384]{1,0:T(8,128)S(1)}, bf16[64,384]{1,0:T(8,128)(2,1)S(1)}) custom-call(bf16[128,384]{1,0:T(8,128)(2,1)S(1)} %pack.1.packed.p0, bf16[128,384]{1,0:T(8,128)(2,1)S(1)} %collective-permute-done.p1, ...), custom_call_target="tpu_custom_call" | custom-call | flops 2000000000 | tf_op jit(solution)/shard_map/first_conv/pallas_call | solution.py:349
  10.0 0.0 copy-start
  10.0 2.0 %collective-permute-start.3 = (bf16[160,384]{1,0:T(8,128)(2,1)S(1)}, bf16[160,384]{1,0:T(8,128)(2,1)S(1)}, u32[]{:S(2)}, u32[]{:S(2)}) collective-permute-start(bf16[160,384]{1,0:T(8,128)(2,1)S(1)} %get-tuple-element.29), channel_id=1, source_target_pairs={{0,4},{1,5},{2,6},{3,7},{4,0},{5,1},{6,2},{7,3},{8,12},{9,13},{10,... | collective-permute-start | bytes 368648 | tf_op jit(solution)/shard_map/ppermute | solution.py:295
  12.0 0.1 collective-permute-start.4
  12.1 2.5 %collective-permute-start.5 = (bf16[64,384]{1,0:T(8,128)(2,1)S(1)}, bf16[64,384]{1,0:T(8,128)(2,1)S(1)}, u32[]{:S(2)}, u32[]{:S(2)}) collective-permute-start(bf16[64,384]{1,0:T(8,128)(2,1)S(1)} %get-tuple-element.31), channel_id=1, source_target_pairs={{0,8},{1,9},{2,10},{3,11},{4,12},{5,13},{6,14},{7,15},{8,0},{9,1},... | collective-permute-start | bytes 147464 | tf_op jit(solution)/shard_map/ppermute | solution.py:295
  14.6 0.0 collective-permute-start.6
  14.6 5.7 %collective-permute-done.5.two = bf16[64,384]{1,0:T(8,128)(2,1)S(1)} collective-permute-done((bf16[64,384]{1,0:T(8,128)(2,1)S(1)}, bf16[64,384]{1,0:T(8,128)(2,1)S(1)}, u32[]{:S(2)}, u32[]{:S(2)}) %collective-permute-start.5) | collective-permute-done | bytes 49184 | tf_op jit(solution)/shard_map/ppermute | solution.py:295
  20.3 0.0 collective-permute-done.3.one
  20.3 0.0 collective-permute-done.4.other
  20.3 0.1 row_sums.1
  20.4 0.0 collective-permute-done.7.w2
  20.4 0.1 collective-permute-start.8
  20.5 1.6 %collective-permute-start.10 = (bf16[64,192]{1,0:T(8,128)(2,1)S(1)}, bf16[64,192]{1,0:T(8,128)(2,1)S(1)}, u32[]{:S(2)}, u32[]{:S(2)}) collective-permute-start(bf16[64,192]{1,0:T(8,128)(2,1)S(1)} %get-tuple-element.39), channel_id=1, source_target_pairs={{0,2},{1,3},{2,0},{3,1},{4,6},{5,7},{6,4},{7,5},{8,10},{9,11},{10,... | collective-permute-start | bytes 73736 | tf_op jit(solution)/shard_map/ppermute | solution.py:286
  22.1 0.3 %collective-permute-start.11 = (bf16[64,192]{1,0:T(8,128)(2,1)S(1)}, bf16[64,192]{1,0:T(8,128)(2,1)S(1)}, u32[]{:S(2)}, u32[]{:S(2)}) collective-permute-start(bf16[64,192]{1,0:T(8,128)(2,1)S(1)} %get-tuple-element.40), channel_id=1, source_target_pairs={{0,3},{1,2},{2,1},{3,0},{4,7},{5,6},{6,5},{7,4},{8,11},{9,10},{10,... | collective-permute-start | bytes 73736 | tf_op jit(solution)/shard_map/ppermute | solution.py:286
  22.4 0.0 collective-permute-done.6.w1
  22.4 0.0 collective-permute-done.8.w3
  22.4 1.9 %cached_conv.1 = (f32[2,64,192]{2,1,0:T(8,128)S(1)}, bf16[18,192,192]{2,1,0:T(8,128)(2,1)S(1)}) custom-call(bf16[64,384]{1,0:T(8,128)(2,1)S(1)} %get-tuple-element.34.mid, bf16[160,384]{1,0:T(8,128)(2,1)S(1)} %collective-permute-done.3.one, bf16[160,384]{1,0:T(8,128)(2,1)S(1)} %collective-permute-done.4.other, bf16[672,384]{1,0:T(8,128)(2,1)S(1)} %get-tuple-element.35.w0, ...), custom_call_target="tpu_custom_call" | custom-call | flops 1000000000 | tf_op jit(solution)/shard_map/cached_conv/pallas_call | solution.py:371
  24.3 0.4 %collective-permute-start.9 = (bf16[64,192]{1,0:T(8,128)(2,1)S(1)}, bf16[64,192]{1,0:T(8,128)(2,1)S(1)}, u32[]{:S(2)}, u32[]{:S(2)}) collective-permute-start(bf16[64,192]{1,0:T(8,128)(2,1)S(1)} %get-tuple-element.38), channel_id=1, source_target_pairs={{0,1},{1,0},{2,3},{3,2},{4,5},{5,4},{6,7},{7,6},{8,9},{9,8},{10,11... | collective-permute-start | bytes 73736 | tf_op jit(solution)/shard_map/ppermute | solution.py:286
  24.7 0.0 collective-permute-done.10.p2
  24.7 0.7 %collective-permute-done.11.p3 = bf16[64,192]{1,0:T(8,128)(2,1)S(1)} collective-permute-done((bf16[64,192]{1,0:T(8,128)(2,1)S(1)}, bf16[64,192]{1,0:T(8,128)(2,1)S(1)}, u32[]{:S(2)}, u32[]{:S(2)}) %collective-permute-start.11) | collective-permute-done | bytes 24608 | tf_op jit(solution)/shard_map/ppermute | solution.py:286
  25.4 0.2 collective-permute-done.9.p1
  25.6 0.0 copy-done
  25.6 1.5 %second_conv.1 = bf16[1,2,2,32,192]{4,3,2,1,0:T(8,128)(2,1)} custom-call(bf16[64,192]{1,0:T(8,128)(2,1)S(1)} %get-tuple-element.32.p0, bf16[64,192]{1,0:T(8,128)(2,1)S(1)} %collective-permute-done.9.p1, bf16[64,192]{1,0:T(8,128)(2,1)S(1)} %collective-permute-done.10.p2, bf16[64,192]{1,0:T(8,128)(2,1)S(1)} %collective-permute-done.11.p3, ...), custom_call_target="tpu_custom_call" | custom-call | flops 1000000000 | tf_op jit(solution)/shard_map/second_conv/pallas_call | solution.py:383
Async XLA Ops:
  1.0 5.8 %collective-permute-start.1 = (bf16[128,384]{1,0:T(8,128)(2,1)S(1)}, bf16[128,384]{1,0:T(8,128)(2,1)S(1)}, u32[]{:S(2)}, u32[]{:S(2)}) collective-permute-start(bf16[128,384]{1,0:T(8,128)(2,1)S(1)} %pack.1.packed.p0), channel_id=1, source_target_pairs={{0,2},{1,3},{2,0},{3,1},{4,6},{5,7},{6,4},{7,5},{8,10},{9,11},{10,... | collective-permute-start | bytes 294920 | tf_op jit(solution)/shard_map/ppermute | solution.py:286
  6.4 14.0 %collective-permute-start.7 = (bf16[672,384]{1,0:T(8,128)(2,1)S(1)}, bf16[672,384]{1,0:T(8,128)(2,1)S(1)}, u32[]{:S(2)}, u32[]{:S(2)}) collective-permute-start(bf16[672,384]{1,0:T(8,128)(2,1)S(1)} %get-tuple-element.35.w0), channel_id=1, source_target_pairs={{0,2},{1,3},{2,0},{3,1},{4,6},{5,7},{6,4},{7,5},{8,10},{9,11},{10,... | collective-permute-start | bytes 1548296 | tf_op jit(solution)/shard_map/ppermute | solution.py:286
  6.5 1.4 %collective-permute-start = (bf16[128,384]{1,0:T(8,128)(2,1)S(1)}, bf16[128,384]{1,0:T(8,128)(2,1)S(1)}, u32[]{:S(2)}, u32[]{:S(2)}) collective-permute-start(bf16[128,384]{1,0:T(8,128)(2,1)S(1)} %pack.1.packed.p0), channel_id=1, source_target_pairs={{0,1},{1,0},{2,3},{3,2},{4,5},{5,4},{6,7},{7,6},{8,9},{9,8},{10,11... | collective-permute-start | bytes 294920 | tf_op jit(solution)/shard_map/ppermute | solution.py:286
  6.8 1.3 %collective-permute-start.2 = (bf16[128,384]{1,0:T(8,128)(2,1)S(1)}, bf16[128,384]{1,0:T(8,128)(2,1)S(1)}, u32[]{:S(2)}, u32[]{:S(2)}) collective-permute-start(bf16[128,384]{1,0:T(8,128)(2,1)S(1)} %collective-permute-done.1.p2), channel_id=1, source_target_pairs={{0,1},{1,0},{2,3},{3,2},{4,5},{5,4},{6,7},{7,6},{8,9},{9,8},{10,11... | collective-permute-start | bytes 294920 | tf_op jit(solution)/shard_map/ppermute | solution.py:286
  10.0 15.5 %copy-start = (f32[192]{0:T(256)S(1)}, f32[192]{0:T(256)}, u32[]{:S(2)}) copy-start(f32[192]{0:T(256)} %gain.1) | copy-start | bytes 2308
  10.0 10.2 %collective-permute-start.3 = (bf16[160,384]{1,0:T(8,128)(2,1)S(1)}, bf16[160,384]{1,0:T(8,128)(2,1)S(1)}, u32[]{:S(2)}, u32[]{:S(2)}) collective-permute-start(bf16[160,384]{1,0:T(8,128)(2,1)S(1)} %get-tuple-element.29), channel_id=1, source_target_pairs={{0,4},{1,5},{2,6},{3,7},{4,0},{5,1},{6,2},{7,3},{8,12},{9,13},{10,... | collective-permute-start | bytes 368648 | tf_op jit(solution)/shard_map/ppermute | solution.py:295
  12.0 8.2 %collective-permute-start.4 = (bf16[160,384]{1,0:T(8,128)(2,1)S(1)}, bf16[160,384]{1,0:T(8,128)(2,1)S(1)}, u32[]{:S(2)}, u32[]{:S(2)}) collective-permute-start(bf16[160,384]{1,0:T(8,128)(2,1)S(1)} %get-tuple-element.30), channel_id=1, source_target_pairs={{0,1},{1,0},{2,3},{3,2},{4,8},{5,9},{6,10},{7,11},{8,4},{9,5},{10,... | collective-permute-start | bytes 368648 | tf_op jit(solution)/shard_map/ppermute | solution.py:295
  12.1 8.2 %collective-permute-start.5 = (bf16[64,384]{1,0:T(8,128)(2,1)S(1)}, bf16[64,384]{1,0:T(8,128)(2,1)S(1)}, u32[]{:S(2)}, u32[]{:S(2)}) collective-permute-start(bf16[64,384]{1,0:T(8,128)(2,1)S(1)} %get-tuple-element.31), channel_id=1, source_target_pairs={{0,8},{1,9},{2,10},{3,11},{4,12},{5,13},{6,14},{7,15},{8,0},{9,1},... | collective-permute-start | bytes 147464 | tf_op jit(solution)/shard_map/ppermute | solution.py:295
  14.6 7.7 %collective-permute-start.6 = (bf16[672,384]{1,0:T(8,128)(2,1)S(1)}, bf16[672,384]{1,0:T(8,128)(2,1)S(1)}, u32[]{:S(2)}, u32[]{:S(2)}) collective-permute-start(bf16[672,384]{1,0:T(8,128)(2,1)S(1)} %get-tuple-element.35.w0), channel_id=1, source_target_pairs={{0,1},{1,0},{2,3},{3,2},{4,5},{5,4},{6,7},{7,6},{8,9},{9,8},{10,11... | collective-permute-start | bytes 1548296 | tf_op jit(solution)/shard_map/ppermute | solution.py:286
  20.4 2.0 %collective-permute-start.8 = (bf16[672,384]{1,0:T(8,128)(2,1)S(1)}, bf16[672,384]{1,0:T(8,128)(2,1)S(1)}, u32[]{:S(2)}, u32[]{:S(2)}) collective-permute-start(bf16[672,384]{1,0:T(8,128)(2,1)S(1)} %collective-permute-done.7.w2), channel_id=1, source_target_pairs={{0,1},{1,0},{2,3},{3,2},{4,5},{5,4},{6,7},{7,6},{8,9},{9,8},{10,11... | collective-permute-start | bytes 1548296 | tf_op jit(solution)/shard_map/ppermute | solution.py:286
  20.5 4.2 %collective-permute-start.10 = (bf16[64,192]{1,0:T(8,128)(2,1)S(1)}, bf16[64,192]{1,0:T(8,128)(2,1)S(1)}, u32[]{:S(2)}, u32[]{:S(2)}) collective-permute-start(bf16[64,192]{1,0:T(8,128)(2,1)S(1)} %get-tuple-element.39), channel_id=1, source_target_pairs={{0,2},{1,3},{2,0},{3,1},{4,6},{5,7},{6,4},{7,5},{8,10},{9,11},{10,... | collective-permute-start | bytes 73736 | tf_op jit(solution)/shard_map/ppermute | solution.py:286
  22.1 3.3 %collective-permute-start.11 = (bf16[64,192]{1,0:T(8,128)(2,1)S(1)}, bf16[64,192]{1,0:T(8,128)(2,1)S(1)}, u32[]{:S(2)}, u32[]{:S(2)}) collective-permute-start(bf16[64,192]{1,0:T(8,128)(2,1)S(1)} %get-tuple-element.40), channel_id=1, source_target_pairs={{0,3},{1,2},{2,1},{3,0},{4,7},{5,6},{6,5},{7,4},{8,11},{9,10},{10,... | collective-permute-start | bytes 73736 | tf_op jit(solution)/shard_map/ppermute | solution.py:286
  24.3 1.3 %collective-permute-start.9 = (bf16[64,192]{1,0:T(8,128)(2,1)S(1)}, bf16[64,192]{1,0:T(8,128)(2,1)S(1)}, u32[]{:S(2)}, u32[]{:S(2)}) collective-permute-start(bf16[64,192]{1,0:T(8,128)(2,1)S(1)} %get-tuple-element.38), channel_id=1, source_target_pairs={{0,1},{1,0},{2,3},{3,2},{4,5},{5,4},{6,7},{7,6},{8,9},{9,8},{10,11... | collective-permute-start | bytes 73736 | tf_op jit(solution)/shard_map/ppermute | solution.py:286

commit v6 on v5

--- a/solution.py
+++ b/solution.py
@@ -75,10 +75,9 @@
     taps, group, channels = 27, second_here.shape[-2], second_here.shape[-1]
     values = second_here[...].reshape(taps * group, channels)
     most = (taps + 1) // 2 * group
-    rest = taps * group - most
-    second[pl.ds(0, rest), :] = jnp.concatenate([values[:rest], values[most:]], axis=1)
-    last = values[rest:most]
-    second[pl.ds(rest, group), :] = jnp.concatenate([last, last], axis=1)
+    second[pl.ds(0, taps * group), :] = values[:, :128]
+    right = jnp.concatenate([values[most:, 128:], values[:group, 128:]], axis=0)
+    second[pl.ds(taps * group, most), :] = jnp.concatenate([values[:most, 128:], right], axis=1)
     loads[3].wait()
 
 
@@ -105,10 +104,10 @@
     sums = [jnp.zeros((rows, outputs), f32) for _ in range(3)]
     taps = [jnp.where(upper, 2, 0), 1, jnp.where(upper, 0, 2)]
     for i in range(3):
-        for l in range(3):
-            window = views[l][:, i : i + frames].reshape(rows, channels)
-            for j in range(3):
-                sums[j] = sums[j] + dot(window, weight[i, taps[j], l], True)
+        window = jnp.concatenate([view[:, i : i + frames].reshape(rows, channels) for view in views], axis=1)
+        for j in range(3):
+            kernel = jnp.concatenate([weight[i, taps[j], l] for l in range(3)], axis=1)
+            sums[j] = sums[j] + dot(window, kernel, True)
 
     u, v, w = [[halves(values[: 2 * half]), halves(values[2 * half :])] for values in sums]
     far_first = sends_far_first()
@@ -128,11 +127,11 @@
 
 
 def sends_far_first():
+    return (lax.axis_index("strm") // 2 == 0) == (lax.axis_index("band") % 2 == 0)
+
+
+def far_comes_first():
     return (lax.axis_index("strm") // 2 == 0) == (lax.axis_index("band") % 2 == 1)
-
-
-def far_comes_first():
-    return (lax.axis_index("strm") // 2 == 0) == (lax.axis_index("band") % 2 == 0)
 
 
 def at_end():
@@ -151,8 +150,8 @@
     for p in range(2):
         at = pl.ds(p * half, half)
         after = pl.ds((2 + p) * half, half)
-        centre = own[at, :] + one[at, :].astype(f32) + jnp.where(alone, 0.0, other[at, :].astype(f32))
-        extra = jnp.where(far_first, one[after, :].astype(f32), jnp.where(alone, 0.0, other[after, :].astype(f32)))
+        centre = own[at, :] + other[at, :].astype(f32) + jnp.where(alone, 0.0, one[at, :].astype(f32))
+        extra = jnp.where(far_first, jnp.where(alone, 0.0, one[after, :].astype(f32)), other[after, :].astype(f32))
         extra = own[after, :] + extra + jnp.where(beyond, 0.0, two[at, :].astype(f32))
         extra = jnp.where(outside, 0.0, extra)
         for side in range(2):
@@ -161,24 +160,12 @@
             pieces[2 * p + side][pl.ds(half, half), :] = extra[:, lanes].astype(bf16)
 
 
-def cache_kernel(columns, mid, one, other, w0, w1, w2, w3, sums, weights, first_taps):
-    me = lax.axis_index("strm")
-    upper = me // 2 == 0
+def view_kernel(columns, mid, one, other, views):
+    upper = lax.axis_index("strm") // 2 == 0
     far_first = far_comes_first()
-    channels = sums.shape[-1]
-    group = channels // 4
     width = 2 * columns
-    area = 2 * width
-    for d, quarter in enumerate((w0, w1, w2, w3)):
-        at = pl.ds(pl.multiple_of((me ^ d) * group, 16), group)
-        values = quarter[...].reshape(14, group, 2 * channels)
-        left, right = values[:, :, :channels], values[:13, :, channels:]
-        first_taps[:, at, :] = left[:9]
-        weights[pl.ds(0, 5), at, :] = left[9:]
-        weights[pl.ds(5, 13), at, :] = right
-
-    first_edge = one[pl.ds(4 * width, width), :].astype(f32)
-    second_edge = jnp.where(at_end(), 0.0, other[pl.ds(4 * width, width), :].astype(f32))
+    first_edge = jnp.where(at_end(), 0.0, one[pl.ds(4 * width, width), :].astype(f32))
+    second_edge = other[pl.ds(4 * width, width), :].astype(f32)
     far = jnp.where(far_first, first_edge, second_edge)
     near = jnp.where(far_first, second_edge, first_edge)
     top = jnp.where(upper, near, far).astype(bf16)
@@ -189,13 +176,31 @@
     column = lax.broadcasted_iota(jnp.int32, (size, size), 1)
     inside = row % width
     natural = 2 * (inside % columns) + inside // columns
+    for l in range(3):
+        source = natural + (l - 1)
+        keep = (source >= 0) & (source < width) & (column == row - inside + source)
+        views[l] = dot(jnp.where(keep, 1.0, 0.0).astype(bf16), stored).astype(bf16)
+
+
+def cache_kernel(columns, views, w0, w1, w2, w3, sums, weights, first_taps):
+    me = lax.axis_index("strm")
+    channels = sums.shape[-1]
+    group = channels // 4
+    width = 2 * columns
+    area = 2 * width
+    for d, quarter in enumerate((w0, w1, w2, w3)):
+        at = pl.ds(pl.multiple_of((me ^ d) * group, 16), group)
+        first_taps[:, at, pl.ds(0, 128)] = quarter[pl.ds(0, 9 * group), :].reshape(9, group, 128)
+        weights[:, at, pl.ds(0, 128)] = quarter[pl.ds(9 * group, 18 * group), :].reshape(18, group, 128)
+        others = quarter[pl.ds(27 * group, 14 * group), :].reshape(14, group, 128)
+        first_taps[:, at, pl.ds(128, 64)] = others[:9, :, :64]
+        weights[pl.ds(0, 5), at, pl.ds(128, 64)] = others[9:, :, :64]
+        weights[pl.ds(5, 13), at, pl.ds(128, 64)] = others[:13, :, 64:]
+
     both = jnp.zeros((2 * area, channels), f32)
     early = jnp.zeros((area, channels), f32)
     for l in range(3):
-        source = natural + (l - 1)
-        keep = (source >= 0) & (source < width) & (column == row - inside + source)
-        view = dot(jnp.where(keep, 1.0, 0.0).astype(bf16), stored).astype(bf16)
-        c0, c1 = view[:, :channels], view[:, channels:]
+        c0, c1 = views[l, :, :channels], views[l, :, channels:]
         for j in range(3):
             at = slice(j * width, j * width + area)
             tap = 3 * j + l
@@ -278,7 +283,7 @@
     outputs = w_first.shape[-1]
     bands = lax.axis_size("band")
     streams = lax.axis_size("strm")
-    assert streams == 4 and bands % 2 == 0 and latents.shape[2] == 1 and frames == 2
+    assert outputs == 192 and streams == 4 and bands % 2 == 0 and latents.shape[2] == 1 and frames == 2
     half = frames * columns
     width = 2 * columns
 
@@ -331,7 +336,7 @@
         "fetch",
         16,
         0.05,
-        out_shape=[struct(turned_first.shape), struct((14 * group, 2 * outputs)), struct((4, 4, 1, channels), f32)],
+        out_shape=[struct(turned_first.shape), struct((41 * group, 128)), struct((4, 4, 1, channels), f32)],
         in_specs=whole(1) + [THERE] * 4,
         out_specs=whole(3),
         scratch_shapes=[
@@ -350,12 +355,12 @@
         functools.partial(first_kernel, frames, columns),
         "first_conv",
         16,
-        2,
+        1.5,
         out_shape=[payload, payload, pair, struct((4 * half, 2 * outputs), f32), struct((2 * width, 2 * outputs))],
         in_specs=whole(6),
         out_specs=whole(5),
     )(*packs, weight_first, masks)
-    one, other, two = along(one, first_way), along(other, second_way), along(two, third_way)
+    one, other, two = along(one, second_way), along(other, first_way), along(two, third_way)
     pieces = call(
         functools.partial(sum_kernel, half),
         "row_sums",
@@ -365,19 +370,29 @@
         in_specs=whole(4),
         out_specs=whole(4),
     )(own, one, other, two)
-    weight_across, _ = lax.optimization_barrier((weights[2], pieces[0]))
+    across, beyond = swapped(pieces[2], 2), swapped(pieces[3], 3)
+    mid, one, other, _ = lax.optimization_barrier((mid, one, other, pieces[0]))
+    views = call(
+        functools.partial(view_kernel, columns),
+        "cached_views",
+        4,
+        0.1,
+        out_shape=struct((3, 4 * width, 2 * outputs)),
+        in_specs=whole(3),
+        out_specs=whole(1)[0],
+    )(mid, one, other)
+    weight_across, views = lax.optimization_barrier((weights[2], views))
     weights.append(swapped(weight_across, 1))
-    across, beyond = swapped(pieces[2], 2), swapped(pieces[3], 3)
     sums, taps = call(
         functools.partial(cache_kernel, columns),
         "cached_conv",
         16,
         1,
         out_shape=[struct((2, 2 * width, outputs), f32), struct((18, outputs, outputs))],
-        in_specs=whole(7),
+        in_specs=whole(5),
         out_specs=whole(2),
         scratch_shapes=[pltpu.VMEM((9, outputs, outputs), bf16)],
-    )(mid, one, other, *weights)
+    )(views, *weights)
     beside, sums = lax.optimization_barrier((pieces[1], sums))
     pieces = [pieces[0], swapped(beside, 1), across, beyond]
     return call(

time: 27.2 us -> 25.6 us (0.941)
  waiting for transfers between devices: 7.87 us -> 6.77 us
  Pallas kernels: 8.78 us -> 8.1 us
    ppermute x3, waiting for transfers between devices: 5.66 us -> 3.81 us  [along(): return lax.ppermute(value, ('band', 'strm'), pairs)]
    ppermute x9, waiting for transfers between devices: 2.21 us -> 2.96 us  [swapped(): lax.ppermute(value, 'strm', [(i, i ^ distance) for i in range(streams)])]
    pallas_call x1, Pallas kernels: 1.9 us -> 1.16 us  [body(): call(functools.partial(cache_kernel, columns), 'cached_conv', 16, 1, out_...]
    ppermute x3, starting transfers between devices: 4.58 us -> 4.93 us  [along(): return lax.ppermute(value, ('band', 'strm'), pairs)]
  transfers between devices with their start and end apart: 12 -> 12, of which waited for: 6 -> 7; matrix products, arithmetic and copies ran while one was open for 0% -> 0% of each run, Pallas kernels for 23% -> 22%
where the time goes in v6:
time: 25.6 us; the launch traced here: 25.5 us
  starting transfers between devices  10.5 us (41%)
  Pallas kernels  8.1 us (32%)
  waiting for transfers between devices  6.77 us (26%)
    ppermute x9, starting transfers between devices, swapped(): lax.ppermute(value, 'strm', [(i, i ^ distance) for i in range(streams)])  5.6 us
    ppermute x3, starting transfers between devices, along(): return lax.ppermute(value, ('band', 'strm'), pairs)  4.93 us
    ppermute x3, waiting for transfers between devices, along(): return lax.ppermute(value, ('band', 'strm'), pairs)  3.81 us
    ppermute x9, waiting for transfers between devices, swapped(): lax.ppermute(value, 'strm', [(i, i ^ distance) for i in range(streams)])  2.96 us
    pallas_call x1, Pallas kernels, body(): call(fetch_kernel, 'fetch', 16, 0.05, out_shape=[struct(turned_first.shap...  2.37 us
    pallas_call x1, Pallas kernels, body(): call(functools.partial(first_kernel, frames, columns), 'first_conv', 16,...  1.66 us
    pallas_call x1, Pallas kernels, body(): call(functools.partial(second_kernel, frames, columns), 'second_conv', 16...  1.48 us
    pallas_call x1, Pallas kernels, body(): call(functools.partial(cache_kernel, columns), 'cached_conv', 16, 1, out_...  1.16 us
  transfers between devices with their start and end apart: 12, of which 7 were waited for; matrix products, arithmetic and copies ran while one was open for 0% of the time, Pallas kernels for 22%

profile of v6, /device:TPU:0, one launch (start us, length us, event | category | flops | bytes accessed | tf_op | source)
XLA Modules:
  0.0 25.5 jit_solution(16449331193572968946)
XLA Ops:
  0.0 1.0 %pack.1.packed.p0 = bf16[128,384]{1,0:T(8,128)(2,1)S(1)} custom-call(bf16[1,2,1,16,384]{4,3,2,1,0:T(8,128)(2,1)} %latents.1, bf16[1,2,1,16,384]{4,3,2,1,0:T(8,128)(2,1)} %first.1, bf16[1,2,2,32,192]{4,3,2,1,0:T(8,128)(2,1)} %second.1, f32[384]{0:T(512)} %gain_there.1), custom_call_target="tpu_custom_call" | custom-call | flops 1000000000 | tf_op jit(solution)/shard_map/pack/pallas_call | solution.py:318
  1.0 3.0 %collective-permute-start.1 = (bf16[128,384]{1,0:T(8,128)(2,1)S(1)}, bf16[128,384]{1,0:T(8,128)(2,1)S(1)}, u32[]{:S(2)}, u32[]{:S(2)}) collective-permute-start(bf16[128,384]{1,0:T(8,128)(2,1)S(1)} %pack.1.packed.p0), channel_id=1, source_target_pairs={{0,2},{1,3},{2,0},{3,1},{4,6},{5,7},{6,4},{7,5},{8,10},{9,11},{10,... | collective-permute-start | bytes 294920 | tf_op jit(solution)/shard_map/ppermute | solution.py:291
  4.0 2.4 %fetch.1 = (bf16[3,3,3,192,384]{4,3,2,1,0:T(8,128)(2,1)S(1)}, bf16[1968,128]{1,0:T(8,128)(2,1)S(1)}, f32[4,4,1,384]{3,2,1,0:T(1,128)S(1)}) custom-call(bf16[128,384]{1,0:T(8,128)(2,1)S(1)} %pack.1.packed.p0, bf16[3,3,3,192,384]{4,3,2,1,0:T(8,128)(2,1)} %bitcast.2, bf16[3,3,3,48,192]{4,3,2,1,0:T(8,128)(2,1)} %bitcast.3, s32[4]{0:T(128)} %slots_there.1, ...), custom_call_target="tpu_custom_call" | custom-call | flops 50000000 | tf_op jit(solution)/shard_map/fetch/pallas_call | solution.py:334
  6.4 0.1 collective-permute-start.6
  6.5 0.1 collective-permute-start
  6.6 0.3 %collective-permute-done.1.p2 = bf16[128,384]{1,0:T(8,128)(2,1)S(1)} collective-permute-done((bf16[128,384]{1,0:T(8,128)(2,1)S(1)}, bf16[128,384]{1,0:T(8,128)(2,1)S(1)}, u32[]{:S(2)}, u32[]{:S(2)}) %collective-permute-start.1) | collective-permute-done | bytes 98336 | tf_op jit(solution)/shard_map/ppermute | solution.py:291
  6.8 0.2 collective-permute-start.2
  7.1 0.8 %collective-permute-done.p1 = bf16[128,384]{1,0:T(8,128)(2,1)S(1)} collective-permute-done((bf16[128,384]{1,0:T(8,128)(2,1)S(1)}, bf16[128,384]{1,0:T(8,128)(2,1)S(1)}, u32[]{:S(2)}, u32[]{:S(2)}) %collective-permute-start) | collective-permute-done | bytes 98336 | tf_op jit(solution)/shard_map/ppermute | solution.py:291
  7.9 0.3 %collective-permute-done.2.p3 = bf16[128,384]{1,0:T(8,128)(2,1)S(1)} collective-permute-done((bf16[128,384]{1,0:T(8,128)(2,1)S(1)}, bf16[128,384]{1,0:T(8,128)(2,1)S(1)}, u32[]{:S(2)}, u32[]{:S(2)}) %collective-permute-start.2) | collective-permute-done | bytes 98336 | tf_op jit(solution)/shard_map/ppermute | solution.py:291
  8.1 1.7 %first_conv.1 = (bf16[160,384]{1,0:T(8,128)(2,1)S(1)}, bf16[160,384]{1,0:T(8,128)(2,1)S(1)}, bf16[64,384]{1,0:T(8,128)(2,1)S(1)}, f32[128,384]{1,0:T(8,128)S(1)}, bf16[64,384]{1,0:T(8,128)(2,1)S(1)}) custom-call(bf16[128,384]{1,0:T(8,128)(2,1)S(1)} %pack.1.packed.p0, bf16[128,384]{1,0:T(8,128)(2,1)S(1)} %collective-permute-done.p1, ...), custom_call_target="tpu_custom_call" | custom-call | flops 1500000000 | tf_op jit(solution)/shard_map/first_conv/pallas_call | solution.py:354
  9.8 0.3 %collective-permute-start.3 = (bf16[160,384]{1,0:T(8,128)(2,1)S(1)}, bf16[160,384]{1,0:T(8,128)(2,1)S(1)}, u32[]{:S(2)}, u32[]{:S(2)}) collective-permute-start(bf16[160,384]{1,0:T(8,128)(2,1)S(1)} %get-tuple-element.33), channel_id=1, source_target_pairs={{0,1},{1,0},{2,3},{3,2},{4,8},{5,9},{6,10},{7,11},{8,4},{9,5},{10,... | collective-permute-start | bytes 368648 | tf_op jit(solution)/shard_map/ppermute | solution.py:300
  10.1 3.3 %collective-permute-start.4 = (bf16[160,384]{1,0:T(8,128)(2,1)S(1)}, bf16[160,384]{1,0:T(8,128)(2,1)S(1)}, u32[]{:S(2)}, u32[]{:S(2)}) collective-permute-start(bf16[160,384]{1,0:T(8,128)(2,1)S(1)} %get-tuple-element.34), channel_id=1, source_target_pairs={{0,4},{1,5},{2,6},{3,7},{4,0},{5,1},{6,2},{7,3},{8,12},{9,13},{10,... | collective-permute-start | bytes 368648 | tf_op jit(solution)/shard_map/ppermute | solution.py:300
  13.4 1.3 %collective-permute-start.5 = (bf16[64,384]{1,0:T(8,128)(2,1)S(1)}, bf16[64,384]{1,0:T(8,128)(2,1)S(1)}, u32[]{:S(2)}, u32[]{:S(2)}) collective-permute-start(bf16[64,384]{1,0:T(8,128)(2,1)S(1)} %get-tuple-element.35), channel_id=1, source_target_pairs={{0,8},{1,9},{2,10},{3,11},{4,12},{5,13},{6,14},{7,15},{8,0},{9,1},... | collective-permute-start | bytes 147464 | tf_op jit(solution)/shard_map/ppermute | solution.py:300
  14.7 0.0 collective-permute-start.7
  14.7 3.8 %collective-permute-done.5.two = bf16[64,384]{1,0:T(8,128)(2,1)S(1)} collective-permute-done((bf16[64,384]{1,0:T(8,128)(2,1)S(1)}, bf16[64,384]{1,0:T(8,128)(2,1)S(1)}, u32[]{:S(2)}, u32[]{:S(2)}) %collective-permute-start.5) | collective-permute-done | bytes 49184 | tf_op jit(solution)/shard_map/ppermute | solution.py:300
  18.5 0.0 collective-permute-done.3.one
  18.6 0.0 collective-permute-done.4.other
  18.6 0.0 copy-start
  18.6 0.1 row_sums.1
  18.7 0.3 %cached_views.1.views = bf16[3,128,384]{2,1,0:T(8,128)(2,1)S(1)} custom-call(bf16[64,384]{1,0:T(8,128)(2,1)S(1)} %get-tuple-element.40.mid, bf16[160,384]{1,0:T(8,128)(2,1)S(1)} %collective-permute-done.3.one, bf16[160,384]{1,0:T(8,128)(2,1)S(1)} %collective-permute-done.4.other), custom_call_target="tpu_custom_call" | custom-call | flops 100000000 | tf_op jit(solution)/shard_map/cached_views/pallas_call | solution.py:375
  19.0 0.5 %collective-permute-done.6.w2 = bf16[1968,128]{1,0:T(8,128)(2,1)S(1)} collective-permute-done((bf16[1968,128]{1,0:T(8,128)(2,1)S(1)}, bf16[1968,128]{1,0:T(8,128)(2,1)S(1)}, u32[]{:S(2)}, u32[]{:S(2)}) %collective-permute-start.6) | collective-permute-done | bytes 503840 | tf_op jit(solution)/shard_map/ppermute | solution.py:291
  19.4 0.0 collective-permute-start.8
  19.4 1.2 %collective-permute-start.10 = (bf16[64,192]{1,0:T(8,128)(2,1)S(1)}, bf16[64,192]{1,0:T(8,128)(2,1)S(1)}, u32[]{:S(2)}, u32[]{:S(2)}) collective-permute-start(bf16[64,192]{1,0:T(8,128)(2,1)S(1)} %get-tuple-element.47), channel_id=1, source_target_pairs={{0,2},{1,3},{2,0},{3,1},{4,6},{5,7},{6,4},{7,5},{8,10},{9,11},{10,... | collective-permute-start | bytes 73736 | tf_op jit(solution)/shard_map/ppermute | solution.py:291
  20.6 0.7 %collective-permute-start.11 = (bf16[64,192]{1,0:T(8,128)(2,1)S(1)}, bf16[64,192]{1,0:T(8,128)(2,1)S(1)}, u32[]{:S(2)}, u32[]{:S(2)}) collective-permute-start(bf16[64,192]{1,0:T(8,128)(2,1)S(1)} %get-tuple-element.48), channel_id=1, source_target_pairs={{0,3},{1,2},{2,1},{3,0},{4,7},{5,6},{6,5},{7,4},{8,11},{9,10},{10,... | collective-permute-start | bytes 73736 | tf_op jit(solution)/shard_map/ppermute | solution.py:291
  21.3 0.0 collective-permute-done.7.w1
  21.3 0.0 collective-permute-done.8.w3
  21.3 1.2 %cached_conv.1 = (f32[2,64,192]{2,1,0:T(8,128)S(1)}, bf16[18,192,192]{2,1,0:T(8,128)(2,1)S(1)}) custom-call(bf16[3,128,384]{2,1,0:T(8,128)(2,1)S(1)} %cached_views.1.views, bf16[1968,128]{1,0:T(8,128)(2,1)S(1)} %get-tuple-element.38.w0, bf16[1968,128]{1,0:T(8,128)(2,1)S(1)} %collective-permute-done.7.w1, bf16[1968,128]{1,0:T(8,128)(2,1)S(1)} %collective-permute-done.6.w2, ...), custom_call_target="tpu_custom_call" | custom-call | flops 1000000000 | tf_op jit(solution)/shard_map/cached_conv/pallas_call | solution.py:386
  22.5 0.3 %collective-permute-start.9 = (bf16[64,192]{1,0:T(8,128)(2,1)S(1)}, bf16[64,192]{1,0:T(8,128)(2,1)S(1)}, u32[]{:S(2)}, u32[]{:S(2)}) collective-permute-start(bf16[64,192]{1,0:T(8,128)(2,1)S(1)} %get-tuple-element.46), channel_id=1, source_target_pairs={{0,1},{1,0},{2,3},{3,2},{4,5},{5,4},{6,7},{7,6},{8,9},{9,8},{10,11... | collective-permute-start | bytes 73736 | tf_op jit(solution)/shard_map/ppermute | solution.py:291
  22.8 0.5 %collective-permute-done.10.p2 = bf16[64,192]{1,0:T(8,128)(2,1)S(1)} collective-permute-done((bf16[64,192]{1,0:T(8,128)(2,1)S(1)}, bf16[64,192]{1,0:T(8,128)(2,1)S(1)}, u32[]{:S(2)}, u32[]{:S(2)}) %collective-permute-start.10) | collective-permute-done | bytes 24608 | tf_op jit(solution)/shard_map/ppermute | solution.py:291
  23.4 0.6 %collective-permute-done.11.p3 = bf16[64,192]{1,0:T(8,128)(2,1)S(1)} collective-permute-done((bf16[64,192]{1,0:T(8,128)(2,1)S(1)}, bf16[64,192]{1,0:T(8,128)(2,1)S(1)}, u32[]{:S(2)}, u32[]{:S(2)}) %collective-permute-start.11) | collective-permute-done | bytes 24608 | tf_op jit(solution)/shard_map/ppermute | solution.py:291
  24.0 0.0 collective-permute-done.9.p1
  24.0 0.0 copy-done
  24.0 1.5 %second_conv.1 = bf16[1,2,2,32,192]{4,3,2,1,0:T(8,128)(2,1)} custom-call(bf16[64,192]{1,0:T(8,128)(2,1)S(1)} %get-tuple-element.36.p0, bf16[64,192]{1,0:T(8,128)(2,1)S(1)} %collective-permute-done.9.p1, bf16[64,192]{1,0:T(8,128)(2,1)S(1)} %collective-permute-done.10.p2, bf16[64,192]{1,0:T(8,128)(2,1)S(1)} %collective-permute-done.11.p3, ...), custom_call_target="tpu_custom_call" | custom-call | flops 1000000000 | tf_op jit(solution)/shard_map/second_conv/pallas_call | solution.py:398
Async XLA Ops:
  1.0 5.8 %collective-permute-start.1 = (bf16[128,384]{1,0:T(8,128)(2,1)S(1)}, bf16[128,384]{1,0:T(8,128)(2,1)S(1)}, u32[]{:S(2)}, u32[]{:S(2)}) collective-permute-start(bf16[128,384]{1,0:T(8,128)(2,1)S(1)} %pack.1.packed.p0), channel_id=1, source_target_pairs={{0,2},{1,3},{2,0},{3,1},{4,6},{5,7},{6,4},{7,5},{8,10},{9,11},{10,... | collective-permute-start | bytes 294920 | tf_op jit(solution)/shard_map/ppermute | solution.py:291
  6.4 13.0 %collective-permute-start.6 = (bf16[1968,128]{1,0:T(8,128)(2,1)S(1)}, bf16[1968,128]{1,0:T(8,128)(2,1)S(1)}, u32[]{:S(2)}, u32[]{:S(2)}) collective-permute-start(bf16[1968,128]{1,0:T(8,128)(2,1)S(1)} %get-tuple-element.38.w0), channel_id=1, source_target_pairs={{0,2},{1,3},{2,0},{3,1},{4,6},{5,7},{6,4},{7,5},{8,10},{9,11},{10,... | collective-permute-start | bytes 1511432 | tf_op jit(solution)/shard_map/ppermute | solution.py:291
  6.5 1.4 %collective-permute-start = (bf16[128,384]{1,0:T(8,128)(2,1)S(1)}, bf16[128,384]{1,0:T(8,128)(2,1)S(1)}, u32[]{:S(2)}, u32[]{:S(2)}) collective-permute-start(bf16[128,384]{1,0:T(8,128)(2,1)S(1)} %pack.1.packed.p0), channel_id=1, source_target_pairs={{0,1},{1,0},{2,3},{3,2},{4,5},{5,4},{6,7},{7,6},{8,9},{9,8},{10,11... | collective-permute-start | bytes 294920 | tf_op jit(solution)/shard_map/ppermute | solution.py:291
  6.8 1.3 %collective-permute-start.2 = (bf16[128,384]{1,0:T(8,128)(2,1)S(1)}, bf16[128,384]{1,0:T(8,128)(2,1)S(1)}, u32[]{:S(2)}, u32[]{:S(2)}) collective-permute-start(bf16[128,384]{1,0:T(8,128)(2,1)S(1)} %collective-permute-done.1.p2), channel_id=1, source_target_pairs={{0,1},{1,0},{2,3},{3,2},{4,5},{5,4},{6,7},{7,6},{8,9},{9,8},{10,11... | collective-permute-start | bytes 294920 | tf_op jit(solution)/shard_map/ppermute | solution.py:291
  9.8 8.7 %collective-permute-start.3 = (bf16[160,384]{1,0:T(8,128)(2,1)S(1)}, bf16[160,384]{1,0:T(8,128)(2,1)S(1)}, u32[]{:S(2)}, u32[]{:S(2)}) collective-permute-start(bf16[160,384]{1,0:T(8,128)(2,1)S(1)} %get-tuple-element.33), channel_id=1, source_target_pairs={{0,1},{1,0},{2,3},{3,2},{4,8},{5,9},{6,10},{7,11},{8,4},{9,5},{10,... | collective-permute-start | bytes 368648 | tf_op jit(solution)/shard_map/ppermute | solution.py:300
  10.1 8.4 %collective-permute-start.4 = (bf16[160,384]{1,0:T(8,128)(2,1)S(1)}, bf16[160,384]{1,0:T(8,128)(2,1)S(1)}, u32[]{:S(2)}, u32[]{:S(2)}) collective-permute-start(bf16[160,384]{1,0:T(8,128)(2,1)S(1)} %get-tuple-element.34), channel_id=1, source_target_pairs={{0,4},{1,5},{2,6},{3,7},{4,0},{5,1},{6,2},{7,3},{8,12},{9,13},{10,... | collective-permute-start | bytes 368648 | tf_op jit(solution)/shard_map/ppermute | solution.py:300
  13.4 5.2 %collective-permute-start.5 = (bf16[64,384]{1,0:T(8,128)(2,1)S(1)}, bf16[64,384]{1,0:T(8,128)(2,1)S(1)}, u32[]{:S(2)}, u32[]{:S(2)}) collective-permute-start(bf16[64,384]{1,0:T(8,128)(2,1)S(1)} %get-tuple-element.35), channel_id=1, source_target_pairs={{0,8},{1,9},{2,10},{3,11},{4,12},{5,13},{6,14},{7,15},{8,0},{9,1},... | collective-permute-start | bytes 147464 | tf_op jit(solution)/shard_map/ppermute | solution.py:300
  14.7 6.6 %collective-permute-start.7 = (bf16[1968,128]{1,0:T(8,128)(2,1)S(1)}, bf16[1968,128]{1,0:T(8,128)(2,1)S(1)}, u32[]{:S(2)}, u32[]{:S(2)}) collective-permute-start(bf16[1968,128]{1,0:T(8,128)(2,1)S(1)} %get-tuple-element.38.w0), channel_id=1, source_target_pairs={{0,1},{1,0},{2,3},{3,2},{4,5},{5,4},{6,7},{7,6},{8,9},{9,8},{10,11... | collective-permute-start | bytes 1511432 | tf_op jit(solution)/shard_map/ppermute | solution.py:291
  18.6 5.4 %copy-start = (f32[192]{0:T(256)S(1)}, f32[192]{0:T(256)}, u32[]{:S(2)}) copy-start(f32[192]{0:T(256)} %gain.1) | copy-start | bytes 2308
  19.4 1.9 %collective-permute-start.8 = (bf16[1968,128]{1,0:T(8,128)(2,1)S(1)}, bf16[1968,128]{1,0:T(8,128)(2,1)S(1)}, u32[]{:S(2)}, u32[]{:S(2)}) collective-permute-start(bf16[1968,128]{1,0:T(8,128)(2,1)S(1)} %collective-permute-done.6.w2), channel_id=1, source_target_pairs={{0,1},{1,0},{2,3},{3,2},{4,5},{5,4},{6,7},{7,6},{8,9},{9,8},{10,11... | collective-permute-start | bytes 1511432 | tf_op jit(solution)/shard_map/ppermute | solution.py:291
  19.4 3.9 %collective-permute-start.10 = (bf16[64,192]{1,0:T(8,128)(2,1)S(1)}, bf16[64,192]{1,0:T(8,128)(2,1)S(1)}, u32[]{:S(2)}, u32[]{:S(2)}) collective-permute-start(bf16[64,192]{1,0:T(8,128)(2,1)S(1)} %get-tuple-element.47), channel_id=1, source_target_pairs={{0,2},{1,3},{2,0},{3,1},{4,6},{5,7},{6,4},{7,5},{8,10},{9,11},{10,... | collective-permute-start | bytes 73736 | tf_op jit(solution)/shard_map/ppermute | solution.py:291
  20.6 3.3 %collective-permute-start.11 = (bf16[64,192]{1,0:T(8,128)(2,1)S(1)}, bf16[64,192]{1,0:T(8,128)(2,1)S(1)}, u32[]{:S(2)}, u32[]{:S(2)}) collective-permute-start(bf16[64,192]{1,0:T(8,128)(2,1)S(1)} %get-tuple-element.48), channel_id=1, source_target_pairs={{0,3},{1,2},{2,1},{3,0},{4,7},{5,6},{6,5},{7,4},{8,11},{9,10},{10,... | collective-permute-start | bytes 73736 | tf_op jit(solution)/shard_map/ppermute | solution.py:291
  22.5 1.5 %collective-permute-start.9 = (bf16[64,192]{1,0:T(8,128)(2,1)S(1)}, bf16[64,192]{1,0:T(8,128)(2,1)S(1)}, u32[]{:S(2)}, u32[]{:S(2)}) collective-permute-start(bf16[64,192]{1,0:T(8,128)(2,1)S(1)} %get-tuple-element.46), channel_id=1, source_target_pairs={{0,1},{1,0},{2,3},{3,2},{4,5},{5,4},{6,7},{7,6},{8,9},{9,8},{10,11... | collective-permute-start | bytes 73736 | tf_op jit(solution)/shard_map/ppermute | solution.py:291

commit v7 on v6

--- a/solution.py
+++ b/solution.py
@@ -54,18 +54,17 @@
 
 
 def fetch_kernel(
-    packed, first_there, second_there, slots_there, blocks_there, first, second, masks, second_here, slots, blocks, sems
+    packed, first_there, second_here, slots_there, blocks_there, first, second, masks, slots, blocks, sems
 ):
     del packed
     loads = [
-        pltpu.make_async_copy(second_there, second_here, sems.at[0]),
-        pltpu.make_async_copy(slots_there, slots, sems.at[1]),
-        pltpu.make_async_copy(blocks_there, blocks, sems.at[2]),
-        pltpu.make_async_copy(first_there, first, sems.at[3]),
+        pltpu.make_async_copy(slots_there, slots, sems.at[0]),
+        pltpu.make_async_copy(blocks_there, blocks, sems.at[1]),
+        pltpu.make_async_copy(first_there, first, sems.at[2]),
     ]
     for load in loads:
         load.start()
-    for load in loads[:3]:
+    for load in loads[:2]:
         load.wait()
     me = lax.axis_index("strm")
     for d in range(4):
@@ -78,7 +77,7 @@
     second[pl.ds(0, taps * group), :] = values[:, :128]
     right = jnp.concatenate([values[most:, 128:], values[:group, 128:]], axis=0)
     second[pl.ds(taps * group, most), :] = jnp.concatenate([values[:most, 128:], right], axis=1)
-    loads[3].wait()
+    loads[2].wait()
 
 
 def first_kernel(frames, columns, p0, p1, p2, p3, weight, masks, one, other, two, own, mid):
@@ -146,7 +145,7 @@
     beyond = jnp.where(upper, place >= bands - 2, place <= 1)
     far_first = far_comes_first()
     alone = at_end()
-    channels = pieces[0].shape[-1]
+    channels = pieces[0].shape[-1] // 2
     for p in range(2):
         at = pl.ds(p * half, half)
         after = pl.ds((2 + p) * half, half)
@@ -156,8 +155,8 @@
         extra = jnp.where(outside, 0.0, extra)
         for side in range(2):
             lanes = slice(side * channels, (side + 1) * channels)
-            pieces[2 * p + side][pl.ds(0, half), :] = centre[:, lanes].astype(bf16)
-            pieces[2 * p + side][pl.ds(half, half), :] = extra[:, lanes].astype(bf16)
+            both = jnp.concatenate([centre[:, lanes], extra[:, lanes]], axis=1)
+            pieces[2 * p + side][...] = both.astype(bf16)
 
 
 def view_kernel(columns, mid, one, other, views):
@@ -215,7 +214,8 @@
     channels = out.shape[-1]
     width = 2 * columns
     for e, piece in enumerate((p0, p1, p2, p3)):
-        quarters[me ^ e] = piece[...]
+        quarters[me ^ e, 0] = piece[:, :channels]
+        quarters[me ^ e, 1] = piece[:, channels:]
 
     fields = [quarters[q].astype(f32).reshape(2, frames, columns, channels) for q in range(4)]
     row_of = ((1, 1), (0, 0), (1, 0), (0, 1))
@@ -319,6 +319,7 @@
         pack_kernel,
         "pack",
         4,
+        5,
         out_shape=struct((2 * half + 2 * width, channels)),
         in_specs=[THERE] * 4,
         out_specs=whole(1)[0],
@@ -337,15 +338,14 @@
         16,
         0.05,
         out_shape=[struct(turned_first.shape), struct((41 * group, 128)), struct((4, 4, 1, channels), f32)],
-        in_specs=whole(1) + [THERE] * 4,
+        in_specs=whole(1) + [THERE] + whole(1) + [THERE] * 2,
         out_specs=whole(3),
         scratch_shapes=[
-            pltpu.VMEM(turned_second.shape, bf16),
             pltpu.SMEM(cache_slot.shape, jnp.int32),
             pltpu.SMEM(block_index.shape, jnp.int32),
-            pltpu.SemaphoreType.DMA((4,)),
+            pltpu.SemaphoreType.DMA((3,)),
         ],
-    )(packed, *map(there, (turned_first, turned_second, cache_slot, block_index)))
+    )(packed, there(turned_first), turned_second, there(cache_slot), there(block_index))
     weight_first, across = lax.optimization_barrier((weight_first, across))
     packs = [packed, swapped(packed, 1), across, swapped(across, 1)]
     weights = [weight_own, swapped(weight_own, 1), swapped(weight_own, 2)]
@@ -366,7 +366,7 @@
         "row_sums",
         4,
         1,
-        out_shape=[struct((2 * half, outputs))] * 4,
+        out_shape=[struct((half, 2 * outputs))] * 4,
         in_specs=whole(4),
         out_specs=whole(4),
     )(own, one, other, two)
@@ -402,7 +402,7 @@
         out_shape=struct((1, frames, 2, width, outputs)),
         in_specs=whole(7),
         out_specs=whole(1)[0],
-        scratch_shapes=[pltpu.VMEM((4, 2 * half, outputs), bf16)],
+        scratch_shapes=[pltpu.VMEM((4, 2, half, outputs), bf16)],
     )(*pieces, sums, taps, gain_second)
 
 

time: 25.6 us -> 25.5 us (level)
  starting transfers between devices: 10.5 us -> 10.1 us
  waiting for transfers between devices: 6.77 us -> 7.08 us
    ppermute x9, waiting for transfers between devices: 2.96 us -> 3.24 us  [swapped(): lax.ppermute(value, 'strm', [(i, i ^ distance) for i in range(streams)])]
where the time goes in v7:
time: 25.5 us; the launch traced here: 25.3 us
  starting transfers between devices  10.1 us (40%)
  Pallas kernels  8.1 us (32%)
  waiting for transfers between devices  7.08 us (28%)
    ppermute x9, starting transfers between devices, swapped(): lax.ppermute(value, 'strm', [(i, i ^ distance) for i in range(streams)])  5.38 us
    ppermute x3, starting transfers between devices, along(): return lax.ppermute(value, ('band', 'strm'), pairs)  4.71 us
    ppermute x3, waiting for transfers between devices, along(): return lax.ppermute(value, ('band', 'strm'), pairs)  3.84 us
    ppermute x9, waiting for transfers between devices, swapped(): lax.ppermute(value, 'strm', [(i, i ^ distance) for i in range(streams)])  3.24 us
    pallas_call x1, Pallas kernels, body(): call(fetch_kernel, 'fetch', 16, 0.05, out_shape=[struct(turned_first.shap...  2.15 us
    pallas_call x1, Pallas kernels, body(): call(functools.partial(first_kernel, frames, columns), 'first_conv', 16,...  1.74 us
    pallas_call x1, Pallas kernels, body(): call(functools.partial(second_kernel, frames, columns), 'second_conv', 16...  1.55 us
    pallas_call x1, Pallas kernels, body(): call(functools.partial(cache_kernel, columns), 'cached_conv', 16, 1, out_...  1.16 us
  transfers between devices with their start and end apart: 12, of which 7 were waited for; matrix products, arithmetic and copies ran while one was open for 0% of the time, Pallas kernels for 22%

profile of v7, /device:TPU:0, one launch (start us, length us, event | category | flops | bytes accessed | tf_op | source)
XLA Modules:
  0.0 25.3 jit_solution(10612549348322310763)
XLA Ops:
  0.0 0.0 copy-start
  0.0 1.1 %pack.1.packed.p0 = bf16[128,384]{1,0:T(8,128)(2,1)S(1)} custom-call(bf16[1,2,1,16,384]{4,3,2,1,0:T(8,128)(2,1)} %latents.1, bf16[1,2,1,16,384]{4,3,2,1,0:T(8,128)(2,1)} %first.1, bf16[1,2,2,32,192]{4,3,2,1,0:T(8,128)(2,1)} %second.1, f32[384]{0:T(512)} %gain_there.1), custom_call_target="tpu_custom_call" | custom-call | flops 5000000000 | tf_op jit(solution)/shard_map/pack/pallas_call | solution.py:318
  1.1 3.0 %collective-permute-start.1 = (bf16[128,384]{1,0:T(8,128)(2,1)S(1)}, bf16[128,384]{1,0:T(8,128)(2,1)S(1)}, u32[]{:S(2)}, u32[]{:S(2)}) collective-permute-start(bf16[128,384]{1,0:T(8,128)(2,1)S(1)} %pack.1.packed.p0), channel_id=1, source_target_pairs={{0,2},{1,3},{2,0},{3,1},{4,6},{5,7},{6,4},{7,5},{8,10},{9,11},{10,... | collective-permute-start | bytes 294920 | tf_op jit(solution)/shard_map/ppermute | solution.py:291
  4.1 0.0 copy-done
  4.1 2.2 %fetch.1 = (bf16[3,3,3,192,384]{4,3,2,1,0:T(8,128)(2,1)S(1)}, bf16[1968,128]{1,0:T(8,128)(2,1)S(1)}, f32[4,4,1,384]{3,2,1,0:T(1,128)S(1)}) custom-call(bf16[128,384]{1,0:T(8,128)(2,1)S(1)} %pack.1.packed.p0, bf16[3,3,3,192,384]{4,3,2,1,0:T(8,128)(2,1)} %bitcast.3, bf16[3,3,3,48,192]{4,3,2,1,0:T(8,128)(2,1)S(1)} %bitcast.2, s32[4]{0:T(128)} %slots_there.1, ...), custom_call_target="tpu_custom_call" | custom-call | flops 50000000 | tf_op jit(solution)/shard_map/fetch/pallas_call | solution.py:335
  6.3 0.1 collective-permute-start.6
  6.4 0.1 collective-permute-start
  6.4 0.5 %collective-permute-done.1.p2 = bf16[128,384]{1,0:T(8,128)(2,1)S(1)} collective-permute-done((bf16[128,384]{1,0:T(8,128)(2,1)S(1)}, bf16[128,384]{1,0:T(8,128)(2,1)S(1)}, u32[]{:S(2)}, u32[]{:S(2)}) %collective-permute-start.1) | collective-permute-done | bytes 98336 | tf_op jit(solution)/shard_map/ppermute | solution.py:291
  6.9 0.0 collective-permute-start.2
  6.9 0.8 %collective-permute-done.p1 = bf16[128,384]{1,0:T(8,128)(2,1)S(1)} collective-permute-done((bf16[128,384]{1,0:T(8,128)(2,1)S(1)}, bf16[128,384]{1,0:T(8,128)(2,1)S(1)}, u32[]{:S(2)}, u32[]{:S(2)}) %collective-permute-start) | collective-permute-done | bytes 98336 | tf_op jit(solution)/shard_map/ppermute | solution.py:291
  7.7 0.5 %collective-permute-done.2.p3 = bf16[128,384]{1,0:T(8,128)(2,1)S(1)} collective-permute-done((bf16[128,384]{1,0:T(8,128)(2,1)S(1)}, bf16[128,384]{1,0:T(8,128)(2,1)S(1)}, u32[]{:S(2)}, u32[]{:S(2)}) %collective-permute-start.2) | collective-permute-done | bytes 98336 | tf_op jit(solution)/shard_map/ppermute | solution.py:291
  8.2 1.7 %first_conv.1 = (bf16[160,384]{1,0:T(8,128)(2,1)S(1)}, bf16[160,384]{1,0:T(8,128)(2,1)S(1)}, bf16[64,384]{1,0:T(8,128)(2,1)S(1)}, f32[128,384]{1,0:T(8,128)S(1)}, bf16[64,384]{1,0:T(8,128)(2,1)S(1)}) custom-call(bf16[128,384]{1,0:T(8,128)(2,1)S(1)} %pack.1.packed.p0, bf16[128,384]{1,0:T(8,128)(2,1)S(1)} %collective-permute-done.p1, ...), custom_call_target="tpu_custom_call" | custom-call | flops 1500000000 | tf_op jit(solution)/shard_map/first_conv/pallas_call | solution.py:354
  10.0 0.2 collective-permute-start.3
  10.2 3.3 %collective-permute-start.4 = (bf16[160,384]{1,0:T(8,128)(2,1)S(1)}, bf16[160,384]{1,0:T(8,128)(2,1)S(1)}, u32[]{:S(2)}, u32[]{:S(2)}) collective-permute-start(bf16[160,384]{1,0:T(8,128)(2,1)S(1)} %get-tuple-element.34), channel_id=1, source_target_pairs={{0,4},{1,5},{2,6},{3,7},{4,0},{5,1},{6,2},{7,3},{8,12},{9,13},{10,... | collective-permute-start | bytes 368648 | tf_op jit(solution)/shard_map/ppermute | solution.py:300
  13.5 1.2 %collective-permute-start.5 = (bf16[64,384]{1,0:T(8,128)(2,1)S(1)}, bf16[64,384]{1,0:T(8,128)(2,1)S(1)}, u32[]{:S(2)}, u32[]{:S(2)}) collective-permute-start(bf16[64,384]{1,0:T(8,128)(2,1)S(1)} %get-tuple-element.35), channel_id=1, source_target_pairs={{0,8},{1,9},{2,10},{3,11},{4,12},{5,13},{6,14},{7,15},{8,0},{9,1},... | collective-permute-start | bytes 147464 | tf_op jit(solution)/shard_map/ppermute | solution.py:300
  14.7 0.0 collective-permute-start.7
  14.7 3.8 %collective-permute-done.5.two = bf16[64,384]{1,0:T(8,128)(2,1)S(1)} collective-permute-done((bf16[64,384]{1,0:T(8,128)(2,1)S(1)}, bf16[64,384]{1,0:T(8,128)(2,1)S(1)}, u32[]{:S(2)}, u32[]{:S(2)}) %collective-permute-start.5) | collective-permute-done | bytes 49184 | tf_op jit(solution)/shard_map/ppermute | solution.py:300
  18.5 0.0 collective-permute-done.3.one
  18.5 0.0 collective-permute-done.4.other
  18.5 0.0 copy-start.1
  18.5 0.1 row_sums.1
  18.6 0.3 %cached_views.1.views = bf16[3,128,384]{2,1,0:T(8,128)(2,1)S(1)} custom-call(bf16[64,384]{1,0:T(8,128)(2,1)S(1)} %get-tuple-element.40.mid, bf16[160,384]{1,0:T(8,128)(2,1)S(1)} %collective-permute-done.3.one, bf16[160,384]{1,0:T(8,128)(2,1)S(1)} %collective-permute-done.4.other), custom_call_target="tpu_custom_call" | custom-call | flops 100000000 | tf_op jit(solution)/shard_map/cached_views/pallas_call | solution.py:375
  18.9 0.4 %collective-permute-done.6.w2 = bf16[1968,128]{1,0:T(8,128)(2,1)S(1)} collective-permute-done((bf16[1968,128]{1,0:T(8,128)(2,1)S(1)}, bf16[1968,128]{1,0:T(8,128)(2,1)S(1)}, u32[]{:S(2)}, u32[]{:S(2)}) %collective-permute-start.6) | collective-permute-done | bytes 503840 | tf_op jit(solution)/shard_map/ppermute | solution.py:291
  19.3 0.0 collective-permute-start.8
  19.3 1.2 %collective-permute-start.10 = (bf16[32,384]{1,0:T(8,128)(2,1)S(1)}, bf16[32,384]{1,0:T(8,128)(2,1)S(1)}, u32[]{:S(2)}, u32[]{:S(2)}) collective-permute-start(bf16[32,384]{1,0:T(8,128)(2,1)S(1)} %get-tuple-element.47), channel_id=1, source_target_pairs={{0,2},{1,3},{2,0},{3,1},{4,6},{5,7},{6,4},{7,5},{8,10},{9,11},{10,... | collective-permute-start | bytes 73736 | tf_op jit(solution)/shard_map/ppermute | solution.py:291
  20.5 0.6 %collective-permute-start.11 = (bf16[32,384]{1,0:T(8,128)(2,1)S(1)}, bf16[32,384]{1,0:T(8,128)(2,1)S(1)}, u32[]{:S(2)}, u32[]{:S(2)}) collective-permute-start(bf16[32,384]{1,0:T(8,128)(2,1)S(1)} %get-tuple-element.48), channel_id=1, source_target_pairs={{0,3},{1,2},{2,1},{3,0},{4,7},{5,6},{6,5},{7,4},{8,11},{9,10},{10,... | collective-permute-start | bytes 73736 | tf_op jit(solution)/shard_map/ppermute | solution.py:291
  21.1 0.0 collective-permute-done.7.w1
  21.1 0.0 collective-permute-done.8.w3
  21.2 1.2 %cached_conv.1 = (f32[2,64,192]{2,1,0:T(8,128)S(1)}, bf16[18,192,192]{2,1,0:T(8,128)(2,1)S(1)}) custom-call(bf16[3,128,384]{2,1,0:T(8,128)(2,1)S(1)} %cached_views.1.views, bf16[1968,128]{1,0:T(8,128)(2,1)S(1)} %get-tuple-element.38.w0, bf16[1968,128]{1,0:T(8,128)(2,1)S(1)} %collective-permute-done.7.w1, bf16[1968,128]{1,0:T(8,128)(2,1)S(1)} %collective-permute-done.6.w2, ...), custom_call_target="tpu_custom_call" | custom-call | flops 1000000000 | tf_op jit(solution)/shard_map/cached_conv/pallas_call | solution.py:386
  22.3 0.3 %collective-permute-start.9 = (bf16[32,384]{1,0:T(8,128)(2,1)S(1)}, bf16[32,384]{1,0:T(8,128)(2,1)S(1)}, u32[]{:S(2)}, u32[]{:S(2)}) collective-permute-start(bf16[32,384]{1,0:T(8,128)(2,1)S(1)} %get-tuple-element.46), channel_id=1, source_target_pairs={{0,1},{1,0},{2,3},{3,2},{4,5},{5,4},{6,7},{7,6},{8,9},{9,8},{10,11... | collective-permute-start | bytes 73736 | tf_op jit(solution)/shard_map/ppermute | solution.py:291
  22.7 0.4 %collective-permute-done.10.p2 = bf16[32,384]{1,0:T(8,128)(2,1)S(1)} collective-permute-done((bf16[32,384]{1,0:T(8,128)(2,1)S(1)}, bf16[32,384]{1,0:T(8,128)(2,1)S(1)}, u32[]{:S(2)}, u32[]{:S(2)}) %collective-permute-start.10) | collective-permute-done | bytes 24608 | tf_op jit(solution)/shard_map/ppermute | solution.py:291
  23.1 0.7 %collective-permute-done.11.p3 = bf16[32,384]{1,0:T(8,128)(2,1)S(1)} collective-permute-done((bf16[32,384]{1,0:T(8,128)(2,1)S(1)}, bf16[32,384]{1,0:T(8,128)(2,1)S(1)}, u32[]{:S(2)}, u32[]{:S(2)}) %collective-permute-start.11) | collective-permute-done | bytes 24608 | tf_op jit(solution)/shard_map/ppermute | solution.py:291
  23.8 0.0 collective-permute-done.9.p1
  23.8 0.0 copy-done.1
  23.8 1.6 %second_conv.1 = bf16[1,2,2,32,192]{4,3,2,1,0:T(8,128)(2,1)} custom-call(bf16[32,384]{1,0:T(8,128)(2,1)S(1)} %get-tuple-element.36.p0, bf16[32,384]{1,0:T(8,128)(2,1)S(1)} %collective-permute-done.9.p1, bf16[32,384]{1,0:T(8,128)(2,1)S(1)} %collective-permute-done.10.p2, bf16[32,384]{1,0:T(8,128)(2,1)S(1)} %collective-permute-done.11.p3, ...), custom_call_target="tpu_custom_call" | custom-call | flops 1000000000 | tf_op jit(solution)/shard_map/second_conv/pallas_call | solution.py:398
Async XLA Ops:
  0.0 4.1 %copy-start = (bf16[3,3,3,192,48]{3,4,2,1,0:T(8,128)(2,1)S(1)}, bf16[3,3,3,192,48]{3,4,2,1,0:T(8,128)(2,1)}, u32[]{:S(2)}) copy-start(bf16[3,3,3,192,48]{3,4,2,1,0:T(8,128)(2,1)} %param.15) | copy-start | bytes 1492996
  1.1 5.8 %collective-permute-start.1 = (bf16[128,384]{1,0:T(8,128)(2,1)S(1)}, bf16[128,384]{1,0:T(8,128)(2,1)S(1)}, u32[]{:S(2)}, u32[]{:S(2)}) collective-permute-start(bf16[128,384]{1,0:T(8,128)(2,1)S(1)} %pack.1.packed.p0), channel_id=1, source_target_pairs={{0,2},{1,3},{2,0},{3,1},{4,6},{5,7},{6,4},{7,5},{8,10},{9,11},{10,... | collective-permute-start | bytes 294920 | tf_op jit(solution)/shard_map/ppermute | solution.py:291
  6.3 13.0 %collective-permute-start.6 = (bf16[1968,128]{1,0:T(8,128)(2,1)S(1)}, bf16[1968,128]{1,0:T(8,128)(2,1)S(1)}, u32[]{:S(2)}, u32[]{:S(2)}) collective-permute-start(bf16[1968,128]{1,0:T(8,128)(2,1)S(1)} %get-tuple-element.38.w0), channel_id=1, source_target_pairs={{0,2},{1,3},{2,0},{3,1},{4,6},{5,7},{6,4},{7,5},{8,10},{9,11},{10,... | collective-permute-start | bytes 1511432 | tf_op jit(solution)/shard_map/ppermute | solution.py:291
  6.4 1.4 %collective-permute-start = (bf16[128,384]{1,0:T(8,128)(2,1)S(1)}, bf16[128,384]{1,0:T(8,128)(2,1)S(1)}, u32[]{:S(2)}, u32[]{:S(2)}) collective-permute-start(bf16[128,384]{1,0:T(8,128)(2,1)S(1)} %pack.1.packed.p0), channel_id=1, source_target_pairs={{0,1},{1,0},{2,3},{3,2},{4,5},{5,4},{6,7},{7,6},{8,9},{9,8},{10,11... | collective-permute-start | bytes 294920 | tf_op jit(solution)/shard_map/ppermute | solution.py:291
  6.9 1.3 %collective-permute-start.2 = (bf16[128,384]{1,0:T(8,128)(2,1)S(1)}, bf16[128,384]{1,0:T(8,128)(2,1)S(1)}, u32[]{:S(2)}, u32[]{:S(2)}) collective-permute-start(bf16[128,384]{1,0:T(8,128)(2,1)S(1)} %collective-permute-done.1.p2), channel_id=1, source_target_pairs={{0,1},{1,0},{2,3},{3,2},{4,5},{5,4},{6,7},{7,6},{8,9},{9,8},{10,11... | collective-permute-start | bytes 294920 | tf_op jit(solution)/shard_map/ppermute | solution.py:291
  10.0 8.6 %collective-permute-start.3 = (bf16[160,384]{1,0:T(8,128)(2,1)S(1)}, bf16[160,384]{1,0:T(8,128)(2,1)S(1)}, u32[]{:S(2)}, u32[]{:S(2)}) collective-permute-start(bf16[160,384]{1,0:T(8,128)(2,1)S(1)} %get-tuple-element.33), channel_id=1, source_target_pairs={{0,1},{1,0},{2,3},{3,2},{4,8},{5,9},{6,10},{7,11},{8,4},{9,5},{10,... | collective-permute-start | bytes 368648 | tf_op jit(solution)/shard_map/ppermute | solution.py:300
  10.2 8.4 %collective-permute-start.4 = (bf16[160,384]{1,0:T(8,128)(2,1)S(1)}, bf16[160,384]{1,0:T(8,128)(2,1)S(1)}, u32[]{:S(2)}, u32[]{:S(2)}) collective-permute-start(bf16[160,384]{1,0:T(8,128)(2,1)S(1)} %get-tuple-element.34), channel_id=1, source_target_pairs={{0,4},{1,5},{2,6},{3,7},{4,0},{5,1},{6,2},{7,3},{8,12},{9,13},{10,... | collective-permute-start | bytes 368648 | tf_op jit(solution)/shard_map/ppermute | solution.py:300
  13.5 5.0 %collective-permute-start.5 = (bf16[64,384]{1,0:T(8,128)(2,1)S(1)}, bf16[64,384]{1,0:T(8,128)(2,1)S(1)}, u32[]{:S(2)}, u32[]{:S(2)}) collective-permute-start(bf16[64,384]{1,0:T(8,128)(2,1)S(1)} %get-tuple-element.35), channel_id=1, source_target_pairs={{0,8},{1,9},{2,10},{3,11},{4,12},{5,13},{6,14},{7,15},{8,0},{9,1},... | collective-permute-start | bytes 147464 | tf_op jit(solution)/shard_map/ppermute | solution.py:300
  14.7 6.5 %collective-permute-start.7 = (bf16[1968,128]{1,0:T(8,128)(2,1)S(1)}, bf16[1968,128]{1,0:T(8,128)(2,1)S(1)}, u32[]{:S(2)}, u32[]{:S(2)}) collective-permute-start(bf16[1968,128]{1,0:T(8,128)(2,1)S(1)} %get-tuple-element.38.w0), channel_id=1, source_target_pairs={{0,1},{1,0},{2,3},{3,2},{4,5},{5,4},{6,7},{7,6},{8,9},{9,8},{10,11... | collective-permute-start | bytes 1511432 | tf_op jit(solution)/shard_map/ppermute | solution.py:291
  18.5 5.3 %copy-start.1 = (f32[192]{0:T(256)S(1)}, f32[192]{0:T(256)}, u32[]{:S(2)}) copy-start(f32[192]{0:T(256)} %gain.1) | copy-start | bytes 2308
  19.3 1.9 %collective-permute-start.8 = (bf16[1968,128]{1,0:T(8,128)(2,1)S(1)}, bf16[1968,128]{1,0:T(8,128)(2,1)S(1)}, u32[]{:S(2)}, u32[]{:S(2)}) collective-permute-start(bf16[1968,128]{1,0:T(8,128)(2,1)S(1)} %collective-permute-done.6.w2), channel_id=1, source_target_pairs={{0,1},{1,0},{2,3},{3,2},{4,5},{5,4},{6,7},{7,6},{8,9},{9,8},{10,11... | collective-permute-start | bytes 1511432 | tf_op jit(solution)/shard_map/ppermute | solution.py:291
  19.3 3.8 %collective-permute-start.10 = (bf16[32,384]{1,0:T(8,128)(2,1)S(1)}, bf16[32,384]{1,0:T(8,128)(2,1)S(1)}, u32[]{:S(2)}, u32[]{:S(2)}) collective-permute-start(bf16[32,384]{1,0:T(8,128)(2,1)S(1)} %get-tuple-element.47), channel_id=1, source_target_pairs={{0,2},{1,3},{2,0},{3,1},{4,6},{5,7},{6,4},{7,5},{8,10},{9,11},{10,... | collective-permute-start | bytes 73736 | tf_op jit(solution)/shard_map/ppermute | solution.py:291
  20.5 3.3 %collective-permute-start.11 = (bf16[32,384]{1,0:T(8,128)(2,1)S(1)}, bf16[32,384]{1,0:T(8,128)(2,1)S(1)}, u32[]{:S(2)}, u32[]{:S(2)}) collective-permute-start(bf16[32,384]{1,0:T(8,128)(2,1)S(1)} %get-tuple-element.48), channel_id=1, source_target_pairs={{0,3},{1,2},{2,1},{3,0},{4,7},{5,6},{6,5},{7,4},{8,11},{9,10},{10,... | collective-permute-start | bytes 73736 | tf_op jit(solution)/shard_map/ppermute | solution.py:291
  22.3 1.4 %collective-permute-start.9 = (bf16[32,384]{1,0:T(8,128)(2,1)S(1)}, bf16[32,384]{1,0:T(8,128)(2,1)S(1)}, u32[]{:S(2)}, u32[]{:S(2)}) collective-permute-start(bf16[32,384]{1,0:T(8,128)(2,1)S(1)} %get-tuple-element.46), channel_id=1, source_target_pairs={{0,1},{1,0},{2,3},{3,2},{4,5},{5,4},{6,7},{7,6},{8,9},{9,8},{10,11... | collective-permute-start | bytes 73736 | tf_op jit(solution)/shard_map/ppermute | solution.py:291

commit v8 on v7

--- a/solution.py
+++ b/solution.py
@@ -100,14 +100,16 @@
         for view in shifted(jnp.concatenate(parts, axis=0), columns)
     ]
     rows = 4 * half
-    sums = [jnp.zeros((rows, outputs), f32) for _ in range(3)]
+    turned = jnp.zeros((3 * outputs, rows), f32)
     taps = [jnp.where(upper, 2, 0), 1, jnp.where(upper, 0, 2)]
     for i in range(3):
         window = jnp.concatenate([view[:, i : i + frames].reshape(rows, channels) for view in views], axis=1)
-        for j in range(3):
-            kernel = jnp.concatenate([weight[i, taps[j], l] for l in range(3)], axis=1)
-            sums[j] = sums[j] + dot(window, kernel, True)
-
+        kernel = jnp.concatenate(
+            [jnp.concatenate([weight[i, taps[j], l] for l in range(3)], axis=1) for j in range(3)], axis=0
+        )
+        turned = turned + dot(kernel, window, True)
+
+    sums = [turned[j * outputs : (j + 1) * outputs].T for j in range(3)]
     u, v, w = [[halves(values[: 2 * half]), halves(values[2 * half :])] for values in sums]
     far_first = sends_far_first()
     cached = chosen(0, pl.ds(2 * half, 2 * width))

time: 25.5 us -> 25.3 us (level)
  transfers between devices with their start and end apart: 12 -> 12, of which waited for: 7 -> 7; matrix products, arithmetic and copies ran while one was open for 0% -> 0% of each run, Pallas kernels for 22% -> 21%
where the time goes in v8:
time: 25.3 us; the launch traced here: 25.2 us
  starting transfers between devices  10.1 us (40%)
  Pallas kernels  7.92 us (31%)
  waiting for transfers between devices  7.1 us (28%)
    ppermute x9, starting transfers between devices, swapped(): lax.ppermute(value, 'strm', [(i, i ^ distance) for i in range(streams)])  5.38 us
    ppermute x3, starting transfers between devices, along(): return lax.ppermute(value, ('band', 'strm'), pairs)  4.72 us
    ppermute x3, waiting for transfers between devices, along(): return lax.ppermute(value, ('band', 'strm'), pairs)  3.83 us
    ppermute x9, waiting for transfers between devices, swapped(): lax.ppermute(value, 'strm', [(i, i ^ distance) for i in range(streams)])  3.27 us
    pallas_call x1, Pallas kernels, body(): call(fetch_kernel, 'fetch', 16, 0.05, out_shape=[struct(turned_first.shap...  2.15 us
    pallas_call x1, Pallas kernels, body(): call(functools.partial(first_kernel, frames, columns), 'first_conv', 16,...  1.56 us
    pallas_call x1, Pallas kernels, body(): call(functools.partial(second_kernel, frames, columns), 'second_conv', 16...  1.56 us
    pallas_call x1, Pallas kernels, body(): call(functools.partial(cache_kernel, columns), 'cached_conv', 16, 1, out_...  1.16 us
  transfers between devices with their start and end apart: 12, of which 7 were waited for; matrix products, arithmetic and copies ran while one was open for 0% of the time, Pallas kernels for 21%

profile of v8, /device:TPU:0, one launch (start us, length us, event | category | flops | bytes accessed | tf_op | source)
XLA Modules:
  0.0 25.2 jit_solution(10212947760626330800)
XLA Ops:
  0.0 0.0 copy-start
  0.0 1.1 %pack.1.packed.p0 = bf16[128,384]{1,0:T(8,128)(2,1)S(1)} custom-call(bf16[1,2,1,16,384]{4,3,2,1,0:T(8,128)(2,1)} %latents.1, bf16[1,2,1,16,384]{4,3,2,1,0:T(8,128)(2,1)} %first.1, bf16[1,2,2,32,192]{4,3,2,1,0:T(8,128)(2,1)} %second.1, f32[384]{0:T(512)} %gain_there.1), custom_call_target="tpu_custom_call" | custom-call | flops 5000000000 | tf_op jit(solution)/shard_map/pack/pallas_call | solution.py:320
  1.1 3.0 %collective-permute-start.1 = (bf16[128,384]{1,0:T(8,128)(2,1)S(1)}, bf16[128,384]{1,0:T(8,128)(2,1)S(1)}, u32[]{:S(2)}, u32[]{:S(2)}) collective-permute-start(bf16[128,384]{1,0:T(8,128)(2,1)S(1)} %pack.1.packed.p0), channel_id=1, source_target_pairs={{0,2},{1,3},{2,0},{3,1},{4,6},{5,7},{6,4},{7,5},{8,10},{9,11},{10,... | collective-permute-start | bytes 294920 | tf_op jit(solution)/shard_map/ppermute | solution.py:293
  4.1 0.0 copy-done
  4.1 2.2 %fetch.1 = (bf16[3,3,3,192,384]{4,3,2,1,0:T(8,128)(2,1)S(1)}, bf16[1968,128]{1,0:T(8,128)(2,1)S(1)}, f32[4,4,1,384]{3,2,1,0:T(1,128)S(1)}) custom-call(bf16[128,384]{1,0:T(8,128)(2,1)S(1)} %pack.1.packed.p0, bf16[3,3,3,192,384]{4,3,2,1,0:T(8,128)(2,1)} %bitcast.3, bf16[3,3,3,48,192]{4,3,2,1,0:T(8,128)(2,1)S(1)} %bitcast.2, s32[4]{0:T(128)} %slots_there.1, ...), custom_call_target="tpu_custom_call" | custom-call | flops 50000000 | tf_op jit(solution)/shard_map/fetch/pallas_call | solution.py:337
  6.3 0.1 collective-permute-start.6
  6.4 0.1 collective-permute-start
  6.4 0.5 %collective-permute-done.1.p2 = bf16[128,384]{1,0:T(8,128)(2,1)S(1)} collective-permute-done((bf16[128,384]{1,0:T(8,128)(2,1)S(1)}, bf16[128,384]{1,0:T(8,128)(2,1)S(1)}, u32[]{:S(2)}, u32[]{:S(2)}) %collective-permute-start.1) | collective-permute-done | bytes 98336 | tf_op jit(solution)/shard_map/ppermute | solution.py:293
  6.9 0.0 collective-permute-start.2
  6.9 0.8 %collective-permute-done.p1 = bf16[128,384]{1,0:T(8,128)(2,1)S(1)} collective-permute-done((bf16[128,384]{1,0:T(8,128)(2,1)S(1)}, bf16[128,384]{1,0:T(8,128)(2,1)S(1)}, u32[]{:S(2)}, u32[]{:S(2)}) %collective-permute-start) | collective-permute-done | bytes 98336 | tf_op jit(solution)/shard_map/ppermute | solution.py:293
  7.7 0.5 %collective-permute-done.2.p3 = bf16[128,384]{1,0:T(8,128)(2,1)S(1)} collective-permute-done((bf16[128,384]{1,0:T(8,128)(2,1)S(1)}, bf16[128,384]{1,0:T(8,128)(2,1)S(1)}, u32[]{:S(2)}, u32[]{:S(2)}) %collective-permute-start.2) | collective-permute-done | bytes 98336 | tf_op jit(solution)/shard_map/ppermute | solution.py:293
  8.2 1.6 %first_conv.1 = (bf16[160,384]{1,0:T(8,128)(2,1)S(1)}, bf16[160,384]{1,0:T(8,128)(2,1)S(1)}, bf16[64,384]{1,0:T(8,128)(2,1)S(1)}, f32[128,384]{1,0:T(8,128)S(1)}, bf16[64,384]{1,0:T(8,128)(2,1)S(1)}) custom-call(bf16[128,384]{1,0:T(8,128)(2,1)S(1)} %pack.1.packed.p0, bf16[128,384]{1,0:T(8,128)(2,1)S(1)} %collective-permute-done.p1, ...), custom_call_target="tpu_custom_call" | custom-call | flops 1500000000 | tf_op jit(solution)/shard_map/first_conv/pallas_call | solution.py:356
  9.8 0.2 collective-permute-start.3
  10.0 3.3 %collective-permute-start.4 = (bf16[160,384]{1,0:T(8,128)(2,1)S(1)}, bf16[160,384]{1,0:T(8,128)(2,1)S(1)}, u32[]{:S(2)}, u32[]{:S(2)}) collective-permute-start(bf16[160,384]{1,0:T(8,128)(2,1)S(1)} %get-tuple-element.34), channel_id=1, source_target_pairs={{0,4},{1,5},{2,6},{3,7},{4,0},{5,1},{6,2},{7,3},{8,12},{9,13},{10,... | collective-permute-start | bytes 368648 | tf_op jit(solution)/shard_map/ppermute | solution.py:302
  13.3 1.2 %collective-permute-start.5 = (bf16[64,384]{1,0:T(8,128)(2,1)S(1)}, bf16[64,384]{1,0:T(8,128)(2,1)S(1)}, u32[]{:S(2)}, u32[]{:S(2)}) collective-permute-start(bf16[64,384]{1,0:T(8,128)(2,1)S(1)} %get-tuple-element.35), channel_id=1, source_target_pairs={{0,8},{1,9},{2,10},{3,11},{4,12},{5,13},{6,14},{7,15},{8,0},{9,1},... | collective-permute-start | bytes 147464 | tf_op jit(solution)/shard_map/ppermute | solution.py:302
  14.5 0.0 collective-permute-start.7
  14.5 3.8 %collective-permute-done.5.two = bf16[64,384]{1,0:T(8,128)(2,1)S(1)} collective-permute-done((bf16[64,384]{1,0:T(8,128)(2,1)S(1)}, bf16[64,384]{1,0:T(8,128)(2,1)S(1)}, u32[]{:S(2)}, u32[]{:S(2)}) %collective-permute-start.5) | collective-permute-done | bytes 49184 | tf_op jit(solution)/shard_map/ppermute | solution.py:302
  18.3 0.0 collective-permute-done.3.one
  18.3 0.0 collective-permute-done.4.other
  18.3 0.0 copy-start.1
  18.3 0.1 row_sums.1
  18.5 0.3 %cached_views.1.views = bf16[3,128,384]{2,1,0:T(8,128)(2,1)S(1)} custom-call(bf16[64,384]{1,0:T(8,128)(2,1)S(1)} %get-tuple-element.40.mid, bf16[160,384]{1,0:T(8,128)(2,1)S(1)} %collective-permute-done.3.one, bf16[160,384]{1,0:T(8,128)(2,1)S(1)} %collective-permute-done.4.other), custom_call_target="tpu_custom_call" | custom-call | flops 100000000 | tf_op jit(solution)/shard_map/cached_views/pallas_call | solution.py:377
  18.7 0.6 %collective-permute-done.6.w2 = bf16[1968,128]{1,0:T(8,128)(2,1)S(1)} collective-permute-done((bf16[1968,128]{1,0:T(8,128)(2,1)S(1)}, bf16[1968,128]{1,0:T(8,128)(2,1)S(1)}, u32[]{:S(2)}, u32[]{:S(2)}) %collective-permute-start.6) | collective-permute-done | bytes 503840 | tf_op jit(solution)/shard_map/ppermute | solution.py:293
  19.3 0.0 collective-permute-start.8
  19.3 1.1 %collective-permute-start.10 = (bf16[32,384]{1,0:T(8,128)(2,1)S(1)}, bf16[32,384]{1,0:T(8,128)(2,1)S(1)}, u32[]{:S(2)}, u32[]{:S(2)}) collective-permute-start(bf16[32,384]{1,0:T(8,128)(2,1)S(1)} %get-tuple-element.47), channel_id=1, source_target_pairs={{0,2},{1,3},{2,0},{3,1},{4,6},{5,7},{6,4},{7,5},{8,10},{9,11},{10,... | collective-permute-start | bytes 73736 | tf_op jit(solution)/shard_map/ppermute | solution.py:293
  20.4 0.8 %collective-permute-start.11 = (bf16[32,384]{1,0:T(8,128)(2,1)S(1)}, bf16[32,384]{1,0:T(8,128)(2,1)S(1)}, u32[]{:S(2)}, u32[]{:S(2)}) collective-permute-start(bf16[32,384]{1,0:T(8,128)(2,1)S(1)} %get-tuple-element.48), channel_id=1, source_target_pairs={{0,3},{1,2},{2,1},{3,0},{4,7},{5,6},{6,5},{7,4},{8,11},{9,10},{10,... | collective-permute-start | bytes 73736 | tf_op jit(solution)/shard_map/ppermute | solution.py:293
  21.1 0.0 collective-permute-done.7.w1
  21.1 0.0 collective-permute-done.8.w3
  21.2 1.2 %cached_conv.1 = (f32[2,64,192]{2,1,0:T(8,128)S(1)}, bf16[18,192,192]{2,1,0:T(8,128)(2,1)S(1)}) custom-call(bf16[3,128,384]{2,1,0:T(8,128)(2,1)S(1)} %cached_views.1.views, bf16[1968,128]{1,0:T(8,128)(2,1)S(1)} %get-tuple-element.38.w0, bf16[1968,128]{1,0:T(8,128)(2,1)S(1)} %collective-permute-done.7.w1, bf16[1968,128]{1,0:T(8,128)(2,1)S(1)} %collective-permute-done.6.w2, ...), custom_call_target="tpu_custom_call" | custom-call | flops 1000000000 | tf_op jit(solution)/shard_map/cached_conv/pallas_call | solution.py:388
  22.3 0.3 %collective-permute-start.9 = (bf16[32,384]{1,0:T(8,128)(2,1)S(1)}, bf16[32,384]{1,0:T(8,128)(2,1)S(1)}, u32[]{:S(2)}, u32[]{:S(2)}) collective-permute-start(bf16[32,384]{1,0:T(8,128)(2,1)S(1)} %get-tuple-element.46), channel_id=1, source_target_pairs={{0,1},{1,0},{2,3},{3,2},{4,5},{5,4},{6,7},{7,6},{8,9},{9,8},{10,11... | collective-permute-start | bytes 73736 | tf_op jit(solution)/shard_map/ppermute | solution.py:293
  22.7 0.4 %collective-permute-done.10.p2 = bf16[32,384]{1,0:T(8,128)(2,1)S(1)} collective-permute-done((bf16[32,384]{1,0:T(8,128)(2,1)S(1)}, bf16[32,384]{1,0:T(8,128)(2,1)S(1)}, u32[]{:S(2)}, u32[]{:S(2)}) %collective-permute-start.10) | collective-permute-done | bytes 24608 | tf_op jit(solution)/shard_map/ppermute | solution.py:293
  23.1 0.5 %collective-permute-done.11.p3 = bf16[32,384]{1,0:T(8,128)(2,1)S(1)} collective-permute-done((bf16[32,384]{1,0:T(8,128)(2,1)S(1)}, bf16[32,384]{1,0:T(8,128)(2,1)S(1)}, u32[]{:S(2)}, u32[]{:S(2)}) %collective-permute-start.11) | collective-permute-done | bytes 24608 | tf_op jit(solution)/shard_map/ppermute | solution.py:293
  23.6 0.0 collective-permute-done.9.p1
  23.6 0.0 copy-done.1
  23.6 1.6 %second_conv.1 = bf16[1,2,2,32,192]{4,3,2,1,0:T(8,128)(2,1)} custom-call(bf16[32,384]{1,0:T(8,128)(2,1)S(1)} %get-tuple-element.36.p0, bf16[32,384]{1,0:T(8,128)(2,1)S(1)} %collective-permute-done.9.p1, bf16[32,384]{1,0:T(8,128)(2,1)S(1)} %collective-permute-done.10.p2, bf16[32,384]{1,0:T(8,128)(2,1)S(1)} %collective-permute-done.11.p3, ...), custom_call_target="tpu_custom_call" | custom-call | flops 1000000000 | tf_op jit(solution)/shard_map/second_conv/pallas_call | solution.py:400
Async XLA Ops:
  0.0 4.1 %copy-start = (bf16[3,3,3,192,48]{3,4,2,1,0:T(8,128)(2,1)S(1)}, bf16[3,3,3,192,48]{3,4,2,1,0:T(8,128)(2,1)}, u32[]{:S(2)}) copy-start(bf16[3,3,3,192,48]{3,4,2,1,0:T(8,128)(2,1)} %param.15) | copy-start | bytes 1492996
  1.1 5.8 %collective-permute-start.1 = (bf16[128,384]{1,0:T(8,128)(2,1)S(1)}, bf16[128,384]{1,0:T(8,128)(2,1)S(1)}, u32[]{:S(2)}, u32[]{:S(2)}) collective-permute-start(bf16[128,384]{1,0:T(8,128)(2,1)S(1)} %pack.1.packed.p0), channel_id=1, source_target_pairs={{0,2},{1,3},{2,0},{3,1},{4,6},{5,7},{6,4},{7,5},{8,10},{9,11},{10,... | collective-permute-start | bytes 294920 | tf_op jit(solution)/shard_map/ppermute | solution.py:293
  6.3 13.0 %collective-permute-start.6 = (bf16[1968,128]{1,0:T(8,128)(2,1)S(1)}, bf16[1968,128]{1,0:T(8,128)(2,1)S(1)}, u32[]{:S(2)}, u32[]{:S(2)}) collective-permute-start(bf16[1968,128]{1,0:T(8,128)(2,1)S(1)} %get-tuple-element.38.w0), channel_id=1, source_target_pairs={{0,2},{1,3},{2,0},{3,1},{4,6},{5,7},{6,4},{7,5},{8,10},{9,11},{10,... | collective-permute-start | bytes 1511432 | tf_op jit(solution)/shard_map/ppermute | solution.py:293
  6.4 1.4 %collective-permute-start = (bf16[128,384]{1,0:T(8,128)(2,1)S(1)}, bf16[128,384]{1,0:T(8,128)(2,1)S(1)}, u32[]{:S(2)}, u32[]{:S(2)}) collective-permute-start(bf16[128,384]{1,0:T(8,128)(2,1)S(1)} %pack.1.packed.p0), channel_id=1, source_target_pairs={{0,1},{1,0},{2,3},{3,2},{4,5},{5,4},{6,7},{7,6},{8,9},{9,8},{10,11... | collective-permute-start | bytes 294920 | tf_op jit(solution)/shard_map/ppermute | solution.py:293
  6.9 1.3 %collective-permute-start.2 = (bf16[128,384]{1,0:T(8,128)(2,1)S(1)}, bf16[128,384]{1,0:T(8,128)(2,1)S(1)}, u32[]{:S(2)}, u32[]{:S(2)}) collective-permute-start(bf16[128,384]{1,0:T(8,128)(2,1)S(1)} %collective-permute-done.1.p2), channel_id=1, source_target_pairs={{0,1},{1,0},{2,3},{3,2},{4,5},{5,4},{6,7},{7,6},{8,9},{9,8},{10,11... | collective-permute-start | bytes 294920 | tf_op jit(solution)/shard_map/ppermute | solution.py:293
  9.8 8.6 %collective-permute-start.3 = (bf16[160,384]{1,0:T(8,128)(2,1)S(1)}, bf16[160,384]{1,0:T(8,128)(2,1)S(1)}, u32[]{:S(2)}, u32[]{:S(2)}) collective-permute-start(bf16[160,384]{1,0:T(8,128)(2,1)S(1)} %get-tuple-element.33), channel_id=1, source_target_pairs={{0,1},{1,0},{2,3},{3,2},{4,8},{5,9},{6,10},{7,11},{8,4},{9,5},{10,... | collective-permute-start | bytes 368648 | tf_op jit(solution)/shard_map/ppermute | solution.py:302
  10.0 8.3 %collective-permute-start.4 = (bf16[160,384]{1,0:T(8,128)(2,1)S(1)}, bf16[160,384]{1,0:T(8,128)(2,1)S(1)}, u32[]{:S(2)}, u32[]{:S(2)}) collective-permute-start(bf16[160,384]{1,0:T(8,128)(2,1)S(1)} %get-tuple-element.34), channel_id=1, source_target_pairs={{0,4},{1,5},{2,6},{3,7},{4,0},{5,1},{6,2},{7,3},{8,12},{9,13},{10,... | collective-permute-start | bytes 368648 | tf_op jit(solution)/shard_map/ppermute | solution.py:302
  13.3 5.0 %collective-permute-start.5 = (bf16[64,384]{1,0:T(8,128)(2,1)S(1)}, bf16[64,384]{1,0:T(8,128)(2,1)S(1)}, u32[]{:S(2)}, u32[]{:S(2)}) collective-permute-start(bf16[64,384]{1,0:T(8,128)(2,1)S(1)} %get-tuple-element.35), channel_id=1, source_target_pairs={{0,8},{1,9},{2,10},{3,11},{4,12},{5,13},{6,14},{7,15},{8,0},{9,1},... | collective-permute-start | bytes 147464 | tf_op jit(solution)/shard_map/ppermute | solution.py:302
  14.5 6.6 %collective-permute-start.7 = (bf16[1968,128]{1,0:T(8,128)(2,1)S(1)}, bf16[1968,128]{1,0:T(8,128)(2,1)S(1)}, u32[]{:S(2)}, u32[]{:S(2)}) collective-permute-start(bf16[1968,128]{1,0:T(8,128)(2,1)S(1)} %get-tuple-element.38.w0), channel_id=1, source_target_pairs={{0,1},{1,0},{2,3},{3,2},{4,5},{5,4},{6,7},{7,6},{8,9},{9,8},{10,11... | collective-permute-start | bytes 1511432 | tf_op jit(solution)/shard_map/ppermute | solution.py:293
  18.3 5.3 %copy-start.1 = (f32[192]{0:T(256)S(1)}, f32[192]{0:T(256)}, u32[]{:S(2)}) copy-start(f32[192]{0:T(256)} %gain.1) | copy-start | bytes 2308
  19.3 1.9 %collective-permute-start.8 = (bf16[1968,128]{1,0:T(8,128)(2,1)S(1)}, bf16[1968,128]{1,0:T(8,128)(2,1)S(1)}, u32[]{:S(2)}, u32[]{:S(2)}) collective-permute-start(bf16[1968,128]{1,0:T(8,128)(2,1)S(1)} %collective-permute-done.6.w2), channel_id=1, source_target_pairs={{0,1},{1,0},{2,3},{3,2},{4,5},{5,4},{6,7},{7,6},{8,9},{9,8},{10,11... | collective-permute-start | bytes 1511432 | tf_op jit(solution)/shard_map/ppermute | solution.py:293
  19.3 3.8 %collective-permute-start.10 = (bf16[32,384]{1,0:T(8,128)(2,1)S(1)}, bf16[32,384]{1,0:T(8,128)(2,1)S(1)}, u32[]{:S(2)}, u32[]{:S(2)}) collective-permute-start(bf16[32,384]{1,0:T(8,128)(2,1)S(1)} %get-tuple-element.47), channel_id=1, source_target_pairs={{0,2},{1,3},{2,0},{3,1},{4,6},{5,7},{6,4},{7,5},{8,10},{9,11},{10,... | collective-permute-start | bytes 73736 | tf_op jit(solution)/shard_map/ppermute | solution.py:293
  20.4 3.3 %collective-permute-start.11 = (bf16[32,384]{1,0:T(8,128)(2,1)S(1)}, bf16[32,384]{1,0:T(8,128)(2,1)S(1)}, u32[]{:S(2)}, u32[]{:S(2)}) collective-permute-start(bf16[32,384]{1,0:T(8,128)(2,1)S(1)} %get-tuple-element.48), channel_id=1, source_target_pairs={{0,3},{1,2},{2,1},{3,0},{4,7},{5,6},{6,5},{7,4},{8,11},{9,10},{10,... | collective-permute-start | bytes 73736 | tf_op jit(solution)/shard_map/ppermute | solution.py:293
  22.3 1.3 %collective-permute-start.9 = (bf16[32,384]{1,0:T(8,128)(2,1)S(1)}, bf16[32,384]{1,0:T(8,128)(2,1)S(1)}, u32[]{:S(2)}, u32[]{:S(2)}) collective-permute-start(bf16[32,384]{1,0:T(8,128)(2,1)S(1)} %get-tuple-element.46), channel_id=1, source_target_pairs={{0,1},{1,0},{2,3},{3,2},{4,5},{5,4},{6,7},{7,6},{8,9},{9,8},{10,11... | collective-permute-start | bytes 73736 | tf_op jit(solution)/shard_map/ppermute | solution.py:293

commit v9 on v8

--- a/solution.py
+++ b/solution.py
@@ -395,7 +395,7 @@
         out_specs=whole(2),
         scratch_shapes=[pltpu.VMEM((9, outputs, outputs), bf16)],
     )(views, *weights)
-    beside, sums = lax.optimization_barrier((pieces[1], sums))
+    beside, _ = lax.optimization_barrier((pieces[1], views))
     pieces = [pieces[0], swapped(beside, 1), across, beyond]
     return call(
         functools.partial(second_kernel, frames, columns),

time: 25.3 us -> 25.3 us (level)
  no operation moved by 1% of the time
where the time goes in v9:
time: 25.3 us; the launch traced here: 25.2 us
  starting transfers between devices  10.1 us (40%)
  Pallas kernels  7.92 us (31%)
  waiting for transfers between devices  7.14 us (28%)
    ppermute x9, starting transfers between devices, swapped(): lax.ppermute(value, 'strm', [(i, i ^ distance) for i in range(streams)])  5.33 us
    ppermute x3, starting transfers between devices, along(): return lax.ppermute(value, ('band', 'strm'), pairs)  4.72 us
    ppermute x3, waiting for transfers between devices, along(): return lax.ppermute(value, ('band', 'strm'), pairs)  3.83 us
    ppermute x9, waiting for transfers between devices, swapped(): lax.ppermute(value, 'strm', [(i, i ^ distance) for i in range(streams)])  3.32 us
    pallas_call x1, Pallas kernels, body(): call(fetch_kernel, 'fetch', 16, 0.05, out_shape=[struct(turned_first.shap...  2.15 us
    pallas_call x1, Pallas kernels, body(): call(functools.partial(first_kernel, frames, columns), 'first_conv', 16,...  1.56 us
    pallas_call x1, Pallas kernels, body(): call(functools.partial(second_kernel, frames, columns), 'second_conv', 16...  1.56 us
    pallas_call x1, Pallas kernels, body(): call(functools.partial(cache_kernel, columns), 'cached_conv', 16, 1, out_...  1.17 us
  transfers between devices with their start and end apart: 12, of which 7 were waited for; matrix products, arithmetic and copies ran while one was open for 0% of the time, Pallas kernels for 21%

profile of v9, /device:TPU:0, one launch (start us, length us, event | category | flops | bytes accessed | tf_op | source)
XLA Modules:
  0.0 25.2 jit_solution(9245030130878403631)
XLA Ops:
  0.0 0.0 copy-start
  0.0 1.1 %pack.1.packed.p0 = bf16[128,384]{1,0:T(8,128)(2,1)S(1)} custom-call(bf16[1,2,1,16,384]{4,3,2,1,0:T(8,128)(2,1)} %latents.1, bf16[1,2,1,16,384]{4,3,2,1,0:T(8,128)(2,1)} %first.1, bf16[1,2,2,32,192]{4,3,2,1,0:T(8,128)(2,1)} %second.1, f32[384]{0:T(512)} %gain_there.1), custom_call_target="tpu_custom_call" | custom-call | flops 5000000000 | tf_op jit(solution)/shard_map/pack/pallas_call | solution.py:320
  1.1 3.0 %collective-permute-start.1 = (bf16[128,384]{1,0:T(8,128)(2,1)S(1)}, bf16[128,384]{1,0:T(8,128)(2,1)S(1)}, u32[]{:S(2)}, u32[]{:S(2)}) collective-permute-start(bf16[128,384]{1,0:T(8,128)(2,1)S(1)} %pack.1.packed.p0), channel_id=1, source_target_pairs={{0,2},{1,3},{2,0},{3,1},{4,6},{5,7},{6,4},{7,5},{8,10},{9,11},{10,... | collective-permute-start | bytes 294920 | tf_op jit(solution)/shard_map/ppermute | solution.py:293
  4.1 0.0 copy-done
  4.1 2.2 %fetch.1 = (bf16[3,3,3,192,384]{4,3,2,1,0:T(8,128)(2,1)S(1)}, bf16[1968,128]{1,0:T(8,128)(2,1)S(1)}, f32[4,4,1,384]{3,2,1,0:T(1,128)S(1)}) custom-call(bf16[128,384]{1,0:T(8,128)(2,1)S(1)} %pack.1.packed.p0, bf16[3,3,3,192,384]{4,3,2,1,0:T(8,128)(2,1)} %bitcast.3, bf16[3,3,3,48,192]{4,3,2,1,0:T(8,128)(2,1)S(1)} %bitcast.2, s32[4]{0:T(128)} %slots_there.1, ...), custom_call_target="tpu_custom_call" | custom-call | flops 50000000 | tf_op jit(solution)/shard_map/fetch/pallas_call | solution.py:337
  6.3 0.1 collective-permute-start.6
  6.4 0.1 collective-permute-start
  6.4 0.5 %collective-permute-done.1.p2 = bf16[128,384]{1,0:T(8,128)(2,1)S(1)} collective-permute-done((bf16[128,384]{1,0:T(8,128)(2,1)S(1)}, bf16[128,384]{1,0:T(8,128)(2,1)S(1)}, u32[]{:S(2)}, u32[]{:S(2)}) %collective-permute-start.1) | collective-permute-done | bytes 98336 | tf_op jit(solution)/shard_map/ppermute | solution.py:293
  6.9 0.0 collective-permute-start.2
  6.9 0.8 %collective-permute-done.p1 = bf16[128,384]{1,0:T(8,128)(2,1)S(1)} collective-permute-done((bf16[128,384]{1,0:T(8,128)(2,1)S(1)}, bf16[128,384]{1,0:T(8,128)(2,1)S(1)}, u32[]{:S(2)}, u32[]{:S(2)}) %collective-permute-start) | collective-permute-done | bytes 98336 | tf_op jit(solution)/shard_map/ppermute | solution.py:293
  7.7 0.5 %collective-permute-done.2.p3 = bf16[128,384]{1,0:T(8,128)(2,1)S(1)} collective-permute-done((bf16[128,384]{1,0:T(8,128)(2,1)S(1)}, bf16[128,384]{1,0:T(8,128)(2,1)S(1)}, u32[]{:S(2)}, u32[]{:S(2)}) %collective-permute-start.2) | collective-permute-done | bytes 98336 | tf_op jit(solution)/shard_map/ppermute | solution.py:293
  8.2 1.6 %first_conv.1 = (bf16[160,384]{1,0:T(8,128)(2,1)S(1)}, bf16[160,384]{1,0:T(8,128)(2,1)S(1)}, bf16[64,384]{1,0:T(8,128)(2,1)S(1)}, f32[128,384]{1,0:T(8,128)S(1)}, bf16[64,384]{1,0:T(8,128)(2,1)S(1)}) custom-call(bf16[128,384]{1,0:T(8,128)(2,1)S(1)} %pack.1.packed.p0, bf16[128,384]{1,0:T(8,128)(2,1)S(1)} %collective-permute-done.p1, ...), custom_call_target="tpu_custom_call" | custom-call | flops 1500000000 | tf_op jit(solution)/shard_map/first_conv/pallas_call | solution.py:356
  9.8 0.2 collective-permute-start.3
  10.0 3.3 %collective-permute-start.4 = (bf16[160,384]{1,0:T(8,128)(2,1)S(1)}, bf16[160,384]{1,0:T(8,128)(2,1)S(1)}, u32[]{:S(2)}, u32[]{:S(2)}) collective-permute-start(bf16[160,384]{1,0:T(8,128)(2,1)S(1)} %get-tuple-element.33), channel_id=1, source_target_pairs={{0,4},{1,5},{2,6},{3,7},{4,0},{5,1},{6,2},{7,3},{8,12},{9,13},{10,... | collective-permute-start | bytes 368648 | tf_op jit(solution)/shard_map/ppermute | solution.py:302
  13.3 1.2 %collective-permute-start.5 = (bf16[64,384]{1,0:T(8,128)(2,1)S(1)}, bf16[64,384]{1,0:T(8,128)(2,1)S(1)}, u32[]{:S(2)}, u32[]{:S(2)}) collective-permute-start(bf16[64,384]{1,0:T(8,128)(2,1)S(1)} %get-tuple-element.34), channel_id=1, source_target_pairs={{0,8},{1,9},{2,10},{3,11},{4,12},{5,13},{6,14},{7,15},{8,0},{9,1},... | collective-permute-start | bytes 147464 | tf_op jit(solution)/shard_map/ppermute | solution.py:302
  14.5 0.0 collective-permute-start.10
  14.5 3.8 %collective-permute-done.5.two = bf16[64,384]{1,0:T(8,128)(2,1)S(1)} collective-permute-done((bf16[64,384]{1,0:T(8,128)(2,1)S(1)}, bf16[64,384]{1,0:T(8,128)(2,1)S(1)}, u32[]{:S(2)}, u32[]{:S(2)}) %collective-permute-start.5) | collective-permute-done | bytes 49184 | tf_op jit(solution)/shard_map/ppermute | solution.py:302
  18.3 0.0 collective-permute-done.3.one
  18.3 0.0 collective-permute-done.4.other
  18.3 0.0 copy-start.1
  18.3 0.1 row_sums.1
  18.5 0.3 %cached_views.1.views = bf16[3,128,384]{2,1,0:T(8,128)(2,1)S(1)} custom-call(bf16[64,384]{1,0:T(8,128)(2,1)S(1)} %get-tuple-element.39.mid, bf16[160,384]{1,0:T(8,128)(2,1)S(1)} %collective-permute-done.3.one, bf16[160,384]{1,0:T(8,128)(2,1)S(1)} %collective-permute-done.4.other), custom_call_target="tpu_custom_call" | custom-call | flops 100000000 | tf_op jit(solution)/shard_map/cached_views/pallas_call | solution.py:377
  18.7 0.6 %collective-permute-done.6.w2 = bf16[1968,128]{1,0:T(8,128)(2,1)S(1)} collective-permute-done((bf16[1968,128]{1,0:T(8,128)(2,1)S(1)}, bf16[1968,128]{1,0:T(8,128)(2,1)S(1)}, u32[]{:S(2)}, u32[]{:S(2)}) %collective-permute-start.6) | collective-permute-done | bytes 503840 | tf_op jit(solution)/shard_map/ppermute | solution.py:293
  19.3 0.0 collective-permute-start.11
  19.3 1.1 %collective-permute-start.8 = (bf16[32,384]{1,0:T(8,128)(2,1)S(1)}, bf16[32,384]{1,0:T(8,128)(2,1)S(1)}, u32[]{:S(2)}, u32[]{:S(2)}) collective-permute-start(bf16[32,384]{1,0:T(8,128)(2,1)S(1)} %get-tuple-element.44), channel_id=1, source_target_pairs={{0,2},{1,3},{2,0},{3,1},{4,6},{5,7},{6,4},{7,5},{8,10},{9,11},{10,... | collective-permute-start | bytes 73736 | tf_op jit(solution)/shard_map/ppermute | solution.py:293
  20.4 0.8 %collective-permute-start.9 = (bf16[32,384]{1,0:T(8,128)(2,1)S(1)}, bf16[32,384]{1,0:T(8,128)(2,1)S(1)}, u32[]{:S(2)}, u32[]{:S(2)}) collective-permute-start(bf16[32,384]{1,0:T(8,128)(2,1)S(1)} %get-tuple-element.45), channel_id=1, source_target_pairs={{0,3},{1,2},{2,1},{3,0},{4,7},{5,6},{6,5},{7,4},{8,11},{9,10},{10,... | collective-permute-start | bytes 73736 | tf_op jit(solution)/shard_map/ppermute | solution.py:293
  21.1 0.3 %collective-permute-start.7 = (bf16[32,384]{1,0:T(8,128)(2,1)S(1)}, bf16[32,384]{1,0:T(8,128)(2,1)S(1)}, u32[]{:S(2)}, u32[]{:S(2)}) collective-permute-start(bf16[32,384]{1,0:T(8,128)(2,1)S(1)} %get-tuple-element.43), channel_id=1, source_target_pairs={{0,1},{1,0},{2,3},{3,2},{4,5},{5,4},{6,7},{7,6},{8,9},{9,8},{10,11... | collective-permute-start | bytes 73736 | tf_op jit(solution)/shard_map/ppermute | solution.py:293
  21.4 0.0 collective-permute-done.10.w1
  21.4 0.0 collective-permute-done.11.w3
  21.4 1.2 %cached_conv.1 = (f32[2,64,192]{2,1,0:T(8,128)S(1)}, bf16[18,192,192]{2,1,0:T(8,128)(2,1)S(1)}) custom-call(bf16[3,128,384]{2,1,0:T(8,128)(2,1)S(1)} %cached_views.1.views, bf16[1968,128]{1,0:T(8,128)(2,1)S(1)} %get-tuple-element.37.w0, bf16[1968,128]{1,0:T(8,128)(2,1)S(1)} %collective-permute-done.10.w1, bf16[1968,128]{1,0:T(8,128)(2,1)S(1)} %collective-permute-done.6.w2, ...), custom_call_target="tpu_custom_call" | custom-call | flops 1000000000 | tf_op jit(solution)/shard_map/cached_conv/pallas_call | solution.py:388
  22.6 0.5 %collective-permute-done.8.p2 = bf16[32,384]{1,0:T(8,128)(2,1)S(1)} collective-permute-done((bf16[32,384]{1,0:T(8,128)(2,1)S(1)}, bf16[32,384]{1,0:T(8,128)(2,1)S(1)}, u32[]{:S(2)}, u32[]{:S(2)}) %collective-permute-start.8) | collective-permute-done | bytes 24608 | tf_op jit(solution)/shard_map/ppermute | solution.py:293
  23.1 0.5 %collective-permute-done.9.p3 = bf16[32,384]{1,0:T(8,128)(2,1)S(1)} collective-permute-done((bf16[32,384]{1,0:T(8,128)(2,1)S(1)}, bf16[32,384]{1,0:T(8,128)(2,1)S(1)}, u32[]{:S(2)}, u32[]{:S(2)}) %collective-permute-start.9) | collective-permute-done | bytes 24608 | tf_op jit(solution)/shard_map/ppermute | solution.py:293
  23.6 0.0 collective-permute-done.7.p1
  23.6 0.0 copy-done.1
  23.6 1.6 %second_conv.1 = bf16[1,2,2,32,192]{4,3,2,1,0:T(8,128)(2,1)} custom-call(bf16[32,384]{1,0:T(8,128)(2,1)S(1)} %get-tuple-element.35.p0, bf16[32,384]{1,0:T(8,128)(2,1)S(1)} %collective-permute-done.7.p1, bf16[32,384]{1,0:T(8,128)(2,1)S(1)} %collective-permute-done.8.p2, bf16[32,384]{1,0:T(8,128)(2,1)S(1)} %collective-permute-done.9.p3, ...), custom_call_target="tpu_custom_call" | custom-call | flops 1000000000 | tf_op jit(solution)/shard_map/second_conv/pallas_call | solution.py:400
Async XLA Ops:
  0.0 4.1 %copy-start = (bf16[3,3,3,192,48]{3,4,2,1,0:T(8,128)(2,1)S(1)}, bf16[3,3,3,192,48]{3,4,2,1,0:T(8,128)(2,1)}, u32[]{:S(2)}) copy-start(bf16[3,3,3,192,48]{3,4,2,1,0:T(8,128)(2,1)} %param.15) | copy-start | bytes 1492996
  1.1 5.8 %collective-permute-start.1 = (bf16[128,384]{1,0:T(8,128)(2,1)S(1)}, bf16[128,384]{1,0:T(8,128)(2,1)S(1)}, u32[]{:S(2)}, u32[]{:S(2)}) collective-permute-start(bf16[128,384]{1,0:T(8,128)(2,1)S(1)} %pack.1.packed.p0), channel_id=1, source_target_pairs={{0,2},{1,3},{2,0},{3,1},{4,6},{5,7},{6,4},{7,5},{8,10},{9,11},{10,... | collective-permute-start | bytes 294920 | tf_op jit(solution)/shard_map/ppermute | solution.py:293
  6.3 13.0 %collective-permute-start.6 = (bf16[1968,128]{1,0:T(8,128)(2,1)S(1)}, bf16[1968,128]{1,0:T(8,128)(2,1)S(1)}, u32[]{:S(2)}, u32[]{:S(2)}) collective-permute-start(bf16[1968,128]{1,0:T(8,128)(2,1)S(1)} %get-tuple-element.37.w0), channel_id=1, source_target_pairs={{0,2},{1,3},{2,0},{3,1},{4,6},{5,7},{6,4},{7,5},{8,10},{9,11},{10,... | collective-permute-start | bytes 1511432 | tf_op jit(solution)/shard_map/ppermute | solution.py:293
  6.4 1.4 %collective-permute-start = (bf16[128,384]{1,0:T(8,128)(2,1)S(1)}, bf16[128,384]{1,0:T(8,128)(2,1)S(1)}, u32[]{:S(2)}, u32[]{:S(2)}) collective-permute-start(bf16[128,384]{1,0:T(8,128)(2,1)S(1)} %pack.1.packed.p0), channel_id=1, source_target_pairs={{0,1},{1,0},{2,3},{3,2},{4,5},{5,4},{6,7},{7,6},{8,9},{9,8},{10,11... | collective-permute-start | bytes 294920 | tf_op jit(solution)/shard_map/ppermute | solution.py:293
  6.9 1.3 %collective-permute-start.2 = (bf16[128,384]{1,0:T(8,128)(2,1)S(1)}, bf16[128,384]{1,0:T(8,128)(2,1)S(1)}, u32[]{:S(2)}, u32[]{:S(2)}) collective-permute-start(bf16[128,384]{1,0:T(8,128)(2,1)S(1)} %collective-permute-done.1.p2), channel_id=1, source_target_pairs={{0,1},{1,0},{2,3},{3,2},{4,5},{5,4},{6,7},{7,6},{8,9},{9,8},{10,11... | collective-permute-start | bytes 294920 | tf_op jit(solution)/shard_map/ppermute | solution.py:293
  9.8 8.6 %collective-permute-start.3 = (bf16[160,384]{1,0:T(8,128)(2,1)S(1)}, bf16[160,384]{1,0:T(8,128)(2,1)S(1)}, u32[]{:S(2)}, u32[]{:S(2)}) collective-permute-start(bf16[160,384]{1,0:T(8,128)(2,1)S(1)} %get-tuple-element.32), channel_id=1, source_target_pairs={{0,1},{1,0},{2,3},{3,2},{4,8},{5,9},{6,10},{7,11},{8,4},{9,5},{10,... | collective-permute-start | bytes 368648 | tf_op jit(solution)/shard_map/ppermute | solution.py:302
  10.0 8.3 %collective-permute-start.4 = (bf16[160,384]{1,0:T(8,128)(2,1)S(1)}, bf16[160,384]{1,0:T(8,128)(2,1)S(1)}, u32[]{:S(2)}, u32[]{:S(2)}) collective-permute-start(bf16[160,384]{1,0:T(8,128)(2,1)S(1)} %get-tuple-element.33), channel_id=1, source_target_pairs={{0,4},{1,5},{2,6},{3,7},{4,0},{5,1},{6,2},{7,3},{8,12},{9,13},{10,... | collective-permute-start | bytes 368648 | tf_op jit(solution)/shard_map/ppermute | solution.py:302
  13.3 5.0 %collective-permute-start.5 = (bf16[64,384]{1,0:T(8,128)(2,1)S(1)}, bf16[64,384]{1,0:T(8,128)(2,1)S(1)}, u32[]{:S(2)}, u32[]{:S(2)}) collective-permute-start(bf16[64,384]{1,0:T(8,128)(2,1)S(1)} %get-tuple-element.34), channel_id=1, source_target_pairs={{0,8},{1,9},{2,10},{3,11},{4,12},{5,13},{6,14},{7,15},{8,0},{9,1},... | collective-permute-start | bytes 147464 | tf_op jit(solution)/shard_map/ppermute | solution.py:302
  14.5 6.9 %collective-permute-start.10 = (bf16[1968,128]{1,0:T(8,128)(2,1)S(1)}, bf16[1968,128]{1,0:T(8,128)(2,1)S(1)}, u32[]{:S(2)}, u32[]{:S(2)}) collective-permute-start(bf16[1968,128]{1,0:T(8,128)(2,1)S(1)} %get-tuple-element.37.w0), channel_id=1, source_target_pairs={{0,1},{1,0},{2,3},{3,2},{4,5},{5,4},{6,7},{7,6},{8,9},{9,8},{10,11... | collective-permute-start | bytes 1511432 | tf_op jit(solution)/shard_map/ppermute | solution.py:293
  18.3 5.3 %copy-start.1 = (f32[192]{0:T(256)S(1)}, f32[192]{0:T(256)}, u32[]{:S(2)}) copy-start(f32[192]{0:T(256)} %gain.1) | copy-start | bytes 2308
  19.3 2.2 %collective-permute-start.11 = (bf16[1968,128]{1,0:T(8,128)(2,1)S(1)}, bf16[1968,128]{1,0:T(8,128)(2,1)S(1)}, u32[]{:S(2)}, u32[]{:S(2)}) collective-permute-start(bf16[1968,128]{1,0:T(8,128)(2,1)S(1)} %collective-permute-done.6.w2), channel_id=1, source_target_pairs={{0,1},{1,0},{2,3},{3,2},{4,5},{5,4},{6,7},{7,6},{8,9},{9,8},{10,11... | collective-permute-start | bytes 1511432 | tf_op jit(solution)/shard_map/ppermute | solution.py:293
  19.3 3.8 %collective-permute-start.8 = (bf16[32,384]{1,0:T(8,128)(2,1)S(1)}, bf16[32,384]{1,0:T(8,128)(2,1)S(1)}, u32[]{:S(2)}, u32[]{:S(2)}) collective-permute-start(bf16[32,384]{1,0:T(8,128)(2,1)S(1)} %get-tuple-element.44), channel_id=1, source_target_pairs={{0,2},{1,3},{2,0},{3,1},{4,6},{5,7},{6,4},{7,5},{8,10},{9,11},{10,... | collective-permute-start | bytes 73736 | tf_op jit(solution)/shard_map/ppermute | solution.py:293
  20.4 3.3 %collective-permute-start.9 = (bf16[32,384]{1,0:T(8,128)(2,1)S(1)}, bf16[32,384]{1,0:T(8,128)(2,1)S(1)}, u32[]{:S(2)}, u32[]{:S(2)}) collective-permute-start(bf16[32,384]{1,0:T(8,128)(2,1)S(1)} %get-tuple-element.45), channel_id=1, source_target_pairs={{0,3},{1,2},{2,1},{3,0},{4,7},{5,6},{6,5},{7,4},{8,11},{9,10},{10,... | collective-permute-start | bytes 73736 | tf_op jit(solution)/shard_map/ppermute | solution.py:293
  21.1 2.5 %collective-permute-start.7 = (bf16[32,384]{1,0:T(8,128)(2,1)S(1)}, bf16[32,384]{1,0:T(8,128)(2,1)S(1)}, u32[]{:S(2)}, u32[]{:S(2)}) collective-permute-start(bf16[32,384]{1,0:T(8,128)(2,1)S(1)} %get-tuple-element.43), channel_id=1, source_target_pairs={{0,1},{1,0},{2,3},{3,2},{4,5},{5,4},{6,7},{7,6},{8,9},{9,8},{10,11... | collective-permute-start | bytes 73736 | tf_op jit(solution)/shard_map/ppermute | solution.py:293

commit v10 on v8

--- a/solution.py
+++ b/solution.py
@@ -58,13 +58,13 @@
 ):
     del packed
     loads = [
+        pltpu.make_async_copy(first_there, first, sems.at[2]),
         pltpu.make_async_copy(slots_there, slots, sems.at[0]),
         pltpu.make_async_copy(blocks_there, blocks, sems.at[1]),
-        pltpu.make_async_copy(first_there, first, sems.at[2]),
     ]
     for load in loads:
         load.start()
-    for load in loads[:2]:
+    for load in loads[1:]:
         load.wait()
     me = lax.axis_index("strm")
     for d in range(4):
@@ -77,7 +77,7 @@
     second[pl.ds(0, taps * group), :] = values[:, :128]
     right = jnp.concatenate([values[most:, 128:], values[:group, 128:]], axis=0)
     second[pl.ds(taps * group, most), :] = jnp.concatenate([values[:most, 128:], right], axis=1)
-    loads[2].wait()
+    loads[0].wait()
 
 
 def first_kernel(frames, columns, p0, p1, p2, p3, weight, masks, one, other, two, own, mid):

time: 25.3 us -> 25.3 us (level)
  no operation moved by 1% of the time
where the time goes in v10:
time: 25.3 us; the launch traced here: 25.2 us
  starting transfers between devices  10.1 us (40%)
  Pallas kernels  7.91 us (31%)
  waiting for transfers between devices  7.1 us (28%)
    ppermute x9, starting transfers between devices, swapped(): lax.ppermute(value, 'strm', [(i, i ^ distance) for i in range(streams)])  5.38 us
    ppermute x3, starting transfers between devices, along(): return lax.ppermute(value, ('band', 'strm'), pairs)  4.72 us
    ppermute x3, waiting for transfers between devices, along(): return lax.ppermute(value, ('band', 'strm'), pairs)  3.83 us
    ppermute x9, waiting for transfers between devices, swapped(): lax.ppermute(value, 'strm', [(i, i ^ distance) for i in range(streams)])  3.27 us
    pallas_call x1, Pallas kernels, body(): call(fetch_kernel, 'fetch', 16, 0.05, out_shape=[struct(turned_first.shap...  2.15 us
    pallas_call x1, Pallas kernels, body(): call(functools.partial(first_kernel, frames, columns), 'first_conv', 16,...  1.56 us
    pallas_call x1, Pallas kernels, body(): call(functools.partial(second_kernel, frames, columns), 'second_conv', 16...  1.56 us
    pallas_call x1, Pallas kernels, body(): call(functools.partial(cache_kernel, columns), 'cached_conv', 16, 1, out_...  1.16 us
  transfers between devices with their start and end apart: 12, of which 7 were waited for; matrix products, arithmetic and copies ran while one was open for 0% of the time, Pallas kernels for 21%

profile of v10, /device:TPU:0, one launch (start us, length us, event | category | flops | bytes accessed | tf_op | source)
XLA Modules:
  0.0 25.2 jit_solution(6850208375487013714)
XLA Ops:
  0.0 0.0 copy-start
  0.0 1.1 %pack.1.packed.p0 = bf16[128,384]{1,0:T(8,128)(2,1)S(1)} custom-call(bf16[1,2,1,16,384]{4,3,2,1,0:T(8,128)(2,1)} %latents.1, bf16[1,2,1,16,384]{4,3,2,1,0:T(8,128)(2,1)} %first.1, bf16[1,2,2,32,192]{4,3,2,1,0:T(8,128)(2,1)} %second.1, f32[384]{0:T(512)} %gain_there.1), custom_call_target="tpu_custom_call" | custom-call | flops 5000000000 | tf_op jit(solution)/shard_map/pack/pallas_call | solution.py:320
  1.1 3.0 %collective-permute-start.1 = (bf16[128,384]{1,0:T(8,128)(2,1)S(1)}, bf16[128,384]{1,0:T(8,128)(2,1)S(1)}, u32[]{:S(2)}, u32[]{:S(2)}) collective-permute-start(bf16[128,384]{1,0:T(8,128)(2,1)S(1)} %pack.1.packed.p0), channel_id=1, source_target_pairs={{0,2},{1,3},{2,0},{3,1},{4,6},{5,7},{6,4},{7,5},{8,10},{9,11},{10,... | collective-permute-start | bytes 294920 | tf_op jit(solution)/shard_map/ppermute | solution.py:293
  4.1 0.0 copy-done
  4.1 2.2 %fetch.1 = (bf16[3,3,3,192,384]{4,3,2,1,0:T(8,128)(2,1)S(1)}, bf16[1968,128]{1,0:T(8,128)(2,1)S(1)}, f32[4,4,1,384]{3,2,1,0:T(1,128)S(1)}) custom-call(bf16[128,384]{1,0:T(8,128)(2,1)S(1)} %pack.1.packed.p0, bf16[3,3,3,192,384]{4,3,2,1,0:T(8,128)(2,1)} %bitcast.3, bf16[3,3,3,48,192]{4,3,2,1,0:T(8,128)(2,1)S(1)} %bitcast.2, s32[4]{0:T(128)} %slots_there.1, ...), custom_call_target="tpu_custom_call" | custom-call | flops 50000000 | tf_op jit(solution)/shard_map/fetch/pallas_call | solution.py:337
  6.3 0.1 collective-permute-start.6
  6.4 0.1 collective-permute-start
  6.4 0.5 %collective-permute-done.1.p2 = bf16[128,384]{1,0:T(8,128)(2,1)S(1)} collective-permute-done((bf16[128,384]{1,0:T(8,128)(2,1)S(1)}, bf16[128,384]{1,0:T(8,128)(2,1)S(1)}, u32[]{:S(2)}, u32[]{:S(2)}) %collective-permute-start.1) | collective-permute-done | bytes 98336 | tf_op jit(solution)/shard_map/ppermute | solution.py:293
  6.9 0.0 collective-permute-start.2
  6.9 0.8 %collective-permute-done.p1 = bf16[128,384]{1,0:T(8,128)(2,1)S(1)} collective-permute-done((bf16[128,384]{1,0:T(8,128)(2,1)S(1)}, bf16[128,384]{1,0:T(8,128)(2,1)S(1)}, u32[]{:S(2)}, u32[]{:S(2)}) %collective-permute-start) | collective-permute-done | bytes 98336 | tf_op jit(solution)/shard_map/ppermute | solution.py:293
  7.7 0.5 %collective-permute-done.2.p3 = bf16[128,384]{1,0:T(8,128)(2,1)S(1)} collective-permute-done((bf16[128,384]{1,0:T(8,128)(2,1)S(1)}, bf16[128,384]{1,0:T(8,128)(2,1)S(1)}, u32[]{:S(2)}, u32[]{:S(2)}) %collective-permute-start.2) | collective-permute-done | bytes 98336 | tf_op jit(solution)/shard_map/ppermute | solution.py:293
  8.2 1.6 %first_conv.1 = (bf16[160,384]{1,0:T(8,128)(2,1)S(1)}, bf16[160,384]{1,0:T(8,128)(2,1)S(1)}, bf16[64,384]{1,0:T(8,128)(2,1)S(1)}, f32[128,384]{1,0:T(8,128)S(1)}, bf16[64,384]{1,0:T(8,128)(2,1)S(1)}) custom-call(bf16[128,384]{1,0:T(8,128)(2,1)S(1)} %pack.1.packed.p0, bf16[128,384]{1,0:T(8,128)(2,1)S(1)} %collective-permute-done.p1, ...), custom_call_target="tpu_custom_call" | custom-call | flops 1500000000 | tf_op jit(solution)/shard_map/first_conv/pallas_call | solution.py:356
  9.8 0.2 collective-permute-start.3
  10.0 3.3 %collective-permute-start.4 = (bf16[160,384]{1,0:T(8,128)(2,1)S(1)}, bf16[160,384]{1,0:T(8,128)(2,1)S(1)}, u32[]{:S(2)}, u32[]{:S(2)}) collective-permute-start(bf16[160,384]{1,0:T(8,128)(2,1)S(1)} %get-tuple-element.34), channel_id=1, source_target_pairs={{0,4},{1,5},{2,6},{3,7},{4,0},{5,1},{6,2},{7,3},{8,12},{9,13},{10,... | collective-permute-start | bytes 368648 | tf_op jit(solution)/shard_map/ppermute | solution.py:302
  13.3 1.2 %collective-permute-start.5 = (bf16[64,384]{1,0:T(8,128)(2,1)S(1)}, bf16[64,384]{1,0:T(8,128)(2,1)S(1)}, u32[]{:S(2)}, u32[]{:S(2)}) collective-permute-start(bf16[64,384]{1,0:T(8,128)(2,1)S(1)} %get-tuple-element.35), channel_id=1, source_target_pairs={{0,8},{1,9},{2,10},{3,11},{4,12},{5,13},{6,14},{7,15},{8,0},{9,1},... | collective-permute-start | bytes 147464 | tf_op jit(solution)/shard_map/ppermute | solution.py:302
  14.5 0.0 collective-permute-start.7
  14.5 3.8 %collective-permute-done.5.two = bf16[64,384]{1,0:T(8,128)(2,1)S(1)} collective-permute-done((bf16[64,384]{1,0:T(8,128)(2,1)S(1)}, bf16[64,384]{1,0:T(8,128)(2,1)S(1)}, u32[]{:S(2)}, u32[]{:S(2)}) %collective-permute-start.5) | collective-permute-done | bytes 49184 | tf_op jit(solution)/shard_map/ppermute | solution.py:302
  18.3 0.0 collective-permute-done.3.one
  18.3 0.0 collective-permute-done.4.other
  18.3 0.0 copy-start.1
  18.3 0.1 row_sums.1
  18.5 0.3 %cached_views.1.views = bf16[3,128,384]{2,1,0:T(8,128)(2,1)S(1)} custom-call(bf16[64,384]{1,0:T(8,128)(2,1)S(1)} %get-tuple-element.40.mid, bf16[160,384]{1,0:T(8,128)(2,1)S(1)} %collective-permute-done.3.one, bf16[160,384]{1,0:T(8,128)(2,1)S(1)} %collective-permute-done.4.other), custom_call_target="tpu_custom_call" | custom-call | flops 100000000 | tf_op jit(solution)/shard_map/cached_views/pallas_call | solution.py:377
  18.7 0.5 %collective-permute-done.6.w2 = bf16[1968,128]{1,0:T(8,128)(2,1)S(1)} collective-permute-done((bf16[1968,128]{1,0:T(8,128)(2,1)S(1)}, bf16[1968,128]{1,0:T(8,128)(2,1)S(1)}, u32[]{:S(2)}, u32[]{:S(2)}) %collective-permute-start.6) | collective-permute-done | bytes 503840 | tf_op jit(solution)/shard_map/ppermute | solution.py:293
  19.3 0.0 collective-permute-start.8
  19.3 1.1 %collective-permute-start.10 = (bf16[32,384]{1,0:T(8,128)(2,1)S(1)}, bf16[32,384]{1,0:T(8,128)(2,1)S(1)}, u32[]{:S(2)}, u32[]{:S(2)}) collective-permute-start(bf16[32,384]{1,0:T(8,128)(2,1)S(1)} %get-tuple-element.47), channel_id=1, source_target_pairs={{0,2},{1,3},{2,0},{3,1},{4,6},{5,7},{6,4},{7,5},{8,10},{9,11},{10,... | collective-permute-start | bytes 73736 | tf_op jit(solution)/shard_map/ppermute | solution.py:293
  20.4 0.8 %collective-permute-start.11 = (bf16[32,384]{1,0:T(8,128)(2,1)S(1)}, bf16[32,384]{1,0:T(8,128)(2,1)S(1)}, u32[]{:S(2)}, u32[]{:S(2)}) collective-permute-start(bf16[32,384]{1,0:T(8,128)(2,1)S(1)} %get-tuple-element.48), channel_id=1, source_target_pairs={{0,3},{1,2},{2,1},{3,0},{4,7},{5,6},{6,5},{7,4},{8,11},{9,10},{10,... | collective-permute-start | bytes 73736 | tf_op jit(solution)/shard_map/ppermute | solution.py:293
  21.1 0.0 collective-permute-done.7.w1
  21.1 0.0 collective-permute-done.8.w3
  21.2 1.2 %cached_conv.1 = (f32[2,64,192]{2,1,0:T(8,128)S(1)}, bf16[18,192,192]{2,1,0:T(8,128)(2,1)S(1)}) custom-call(bf16[3,128,384]{2,1,0:T(8,128)(2,1)S(1)} %cached_views.1.views, bf16[1968,128]{1,0:T(8,128)(2,1)S(1)} %get-tuple-element.38.w0, bf16[1968,128]{1,0:T(8,128)(2,1)S(1)} %collective-permute-done.7.w1, bf16[1968,128]{1,0:T(8,128)(2,1)S(1)} %collective-permute-done.6.w2, ...), custom_call_target="tpu_custom_call" | custom-call | flops 1000000000 | tf_op jit(solution)/shard_map/cached_conv/pallas_call | solution.py:388
  22.3 0.3 %collective-permute-start.9 = (bf16[32,384]{1,0:T(8,128)(2,1)S(1)}, bf16[32,384]{1,0:T(8,128)(2,1)S(1)}, u32[]{:S(2)}, u32[]{:S(2)}) collective-permute-start(bf16[32,384]{1,0:T(8,128)(2,1)S(1)} %get-tuple-element.46), channel_id=1, source_target_pairs={{0,1},{1,0},{2,3},{3,2},{4,5},{5,4},{6,7},{7,6},{8,9},{9,8},{10,11... | collective-permute-start | bytes 73736 | tf_op jit(solution)/shard_map/ppermute | solution.py:293
  22.7 0.4 %collective-permute-done.10.p2 = bf16[32,384]{1,0:T(8,128)(2,1)S(1)} collective-permute-done((bf16[32,384]{1,0:T(8,128)(2,1)S(1)}, bf16[32,384]{1,0:T(8,128)(2,1)S(1)}, u32[]{:S(2)}, u32[]{:S(2)}) %collective-permute-start.10) | collective-permute-done | bytes 24608 | tf_op jit(solution)/shard_map/ppermute | solution.py:293
  23.1 0.5 %collective-permute-done.11.p3 = bf16[32,384]{1,0:T(8,128)(2,1)S(1)} collective-permute-done((bf16[32,384]{1,0:T(8,128)(2,1)S(1)}, bf16[32,384]{1,0:T(8,128)(2,1)S(1)}, u32[]{:S(2)}, u32[]{:S(2)}) %collective-permute-start.11) | collective-permute-done | bytes 24608 | tf_op jit(solution)/shard_map/ppermute | solution.py:293
  23.6 0.0 collective-permute-done.9.p1
  23.6 0.0 copy-done.1
  23.6 1.6 %second_conv.1 = bf16[1,2,2,32,192]{4,3,2,1,0:T(8,128)(2,1)} custom-call(bf16[32,384]{1,0:T(8,128)(2,1)S(1)} %get-tuple-element.36.p0, bf16[32,384]{1,0:T(8,128)(2,1)S(1)} %collective-permute-done.9.p1, bf16[32,384]{1,0:T(8,128)(2,1)S(1)} %collective-permute-done.10.p2, bf16[32,384]{1,0:T(8,128)(2,1)S(1)} %collective-permute-done.11.p3, ...), custom_call_target="tpu_custom_call" | custom-call | flops 1000000000 | tf_op jit(solution)/shard_map/second_conv/pallas_call | solution.py:400
Async XLA Ops:
  0.0 4.1 %copy-start = (bf16[3,3,3,192,48]{3,4,2,1,0:T(8,128)(2,1)S(1)}, bf16[3,3,3,192,48]{3,4,2,1,0:T(8,128)(2,1)}, u32[]{:S(2)}) copy-start(bf16[3,3,3,192,48]{3,4,2,1,0:T(8,128)(2,1)} %param.15) | copy-start | bytes 1492996
  1.1 5.8 %collective-permute-start.1 = (bf16[128,384]{1,0:T(8,128)(2,1)S(1)}, bf16[128,384]{1,0:T(8,128)(2,1)S(1)}, u32[]{:S(2)}, u32[]{:S(2)}) collective-permute-start(bf16[128,384]{1,0:T(8,128)(2,1)S(1)} %pack.1.packed.p0), channel_id=1, source_target_pairs={{0,2},{1,3},{2,0},{3,1},{4,6},{5,7},{6,4},{7,5},{8,10},{9,11},{10,... | collective-permute-start | bytes 294920 | tf_op jit(solution)/shard_map/ppermute | solution.py:293
  6.3 13.0 %collective-permute-start.6 = (bf16[1968,128]{1,0:T(8,128)(2,1)S(1)}, bf16[1968,128]{1,0:T(8,128)(2,1)S(1)}, u32[]{:S(2)}, u32[]{:S(2)}) collective-permute-start(bf16[1968,128]{1,0:T(8,128)(2,1)S(1)} %get-tuple-element.38.w0), channel_id=1, source_target_pairs={{0,2},{1,3},{2,0},{3,1},{4,6},{5,7},{6,4},{7,5},{8,10},{9,11},{10,... | collective-permute-start | bytes 1511432 | tf_op jit(solution)/shard_map/ppermute | solution.py:293
  6.4 1.4 %collective-permute-start = (bf16[128,384]{1,0:T(8,128)(2,1)S(1)}, bf16[128,384]{1,0:T(8,128)(2,1)S(1)}, u32[]{:S(2)}, u32[]{:S(2)}) collective-permute-start(bf16[128,384]{1,0:T(8,128)(2,1)S(1)} %pack.1.packed.p0), channel_id=1, source_target_pairs={{0,1},{1,0},{2,3},{3,2},{4,5},{5,4},{6,7},{7,6},{8,9},{9,8},{10,11... | collective-permute-start | bytes 294920 | tf_op jit(solution)/shard_map/ppermute | solution.py:293
  6.9 1.3 %collective-permute-start.2 = (bf16[128,384]{1,0:T(8,128)(2,1)S(1)}, bf16[128,384]{1,0:T(8,128)(2,1)S(1)}, u32[]{:S(2)}, u32[]{:S(2)}) collective-permute-start(bf16[128,384]{1,0:T(8,128)(2,1)S(1)} %collective-permute-done.1.p2), channel_id=1, source_target_pairs={{0,1},{1,0},{2,3},{3,2},{4,5},{5,4},{6,7},{7,6},{8,9},{9,8},{10,11... | collective-permute-start | bytes 294920 | tf_op jit(solution)/shard_map/ppermute | solution.py:293
  9.8 8.6 %collective-permute-start.3 = (bf16[160,384]{1,0:T(8,128)(2,1)S(1)}, bf16[160,384]{1,0:T(8,128)(2,1)S(1)}, u32[]{:S(2)}, u32[]{:S(2)}) collective-permute-start(bf16[160,384]{1,0:T(8,128)(2,1)S(1)} %get-tuple-element.33), channel_id=1, source_target_pairs={{0,1},{1,0},{2,3},{3,2},{4,8},{5,9},{6,10},{7,11},{8,4},{9,5},{10,... | collective-permute-start | bytes 368648 | tf_op jit(solution)/shard_map/ppermute | solution.py:302
  10.0 8.3 %collective-permute-start.4 = (bf16[160,384]{1,0:T(8,128)(2,1)S(1)}, bf16[160,384]{1,0:T(8,128)(2,1)S(1)}, u32[]{:S(2)}, u32[]{:S(2)}) collective-permute-start(bf16[160,384]{1,0:T(8,128)(2,1)S(1)} %get-tuple-element.34), channel_id=1, source_target_pairs={{0,4},{1,5},{2,6},{3,7},{4,0},{5,1},{6,2},{7,3},{8,12},{9,13},{10,... | collective-permute-start | bytes 368648 | tf_op jit(solution)/shard_map/ppermute | solution.py:302
  13.3 5.0 %collective-permute-start.5 = (bf16[64,384]{1,0:T(8,128)(2,1)S(1)}, bf16[64,384]{1,0:T(8,128)(2,1)S(1)}, u32[]{:S(2)}, u32[]{:S(2)}) collective-permute-start(bf16[64,384]{1,0:T(8,128)(2,1)S(1)} %get-tuple-element.35), channel_id=1, source_target_pairs={{0,8},{1,9},{2,10},{3,11},{4,12},{5,13},{6,14},{7,15},{8,0},{9,1},... | collective-permute-start | bytes 147464 | tf_op jit(solution)/shard_map/ppermute | solution.py:302
  14.5 6.6 %collective-permute-start.7 = (bf16[1968,128]{1,0:T(8,128)(2,1)S(1)}, bf16[1968,128]{1,0:T(8,128)(2,1)S(1)}, u32[]{:S(2)}, u32[]{:S(2)}) collective-permute-start(bf16[1968,128]{1,0:T(8,128)(2,1)S(1)} %get-tuple-element.38.w0), channel_id=1, source_target_pairs={{0,1},{1,0},{2,3},{3,2},{4,5},{5,4},{6,7},{7,6},{8,9},{9,8},{10,11... | collective-permute-start | bytes 1511432 | tf_op jit(solution)/shard_map/ppermute | solution.py:293
  18.3 5.3 %copy-start.1 = (f32[192]{0:T(256)S(1)}, f32[192]{0:T(256)}, u32[]{:S(2)}) copy-start(f32[192]{0:T(256)} %gain.1) | copy-start | bytes 2308
  19.3 1.9 %collective-permute-start.8 = (bf16[1968,128]{1,0:T(8,128)(2,1)S(1)}, bf16[1968,128]{1,0:T(8,128)(2,1)S(1)}, u32[]{:S(2)}, u32[]{:S(2)}) collective-permute-start(bf16[1968,128]{1,0:T(8,128)(2,1)S(1)} %collective-permute-done.6.w2), channel_id=1, source_target_pairs={{0,1},{1,0},{2,3},{3,2},{4,5},{5,4},{6,7},{7,6},{8,9},{9,8},{10,11... | collective-permute-start | bytes 1511432 | tf_op jit(solution)/shard_map/ppermute | solution.py:293
  19.3 3.8 %collective-permute-start.10 = (bf16[32,384]{1,0:T(8,128)(2,1)S(1)}, bf16[32,384]{1,0:T(8,128)(2,1)S(1)}, u32[]{:S(2)}, u32[]{:S(2)}) collective-permute-start(bf16[32,384]{1,0:T(8,128)(2,1)S(1)} %get-tuple-element.47), channel_id=1, source_target_pairs={{0,2},{1,3},{2,0},{3,1},{4,6},{5,7},{6,4},{7,5},{8,10},{9,11},{10,... | collective-permute-start | bytes 73736 | tf_op jit(solution)/shard_map/ppermute | solution.py:293
  20.4 3.3 %collective-permute-start.11 = (bf16[32,384]{1,0:T(8,128)(2,1)S(1)}, bf16[32,384]{1,0:T(8,128)(2,1)S(1)}, u32[]{:S(2)}, u32[]{:S(2)}) collective-permute-start(bf16[32,384]{1,0:T(8,128)(2,1)S(1)} %get-tuple-element.48), channel_id=1, source_target_pairs={{0,3},{1,2},{2,1},{3,0},{4,7},{5,6},{6,5},{7,4},{8,11},{9,10},{10,... | collective-permute-start | bytes 73736 | tf_op jit(solution)/shard_map/ppermute | solution.py:293
  22.3 1.3 %collective-permute-start.9 = (bf16[32,384]{1,0:T(8,128)(2,1)S(1)}, bf16[32,384]{1,0:T(8,128)(2,1)S(1)}, u32[]{:S(2)}, u32[]{:S(2)}) collective-permute-start(bf16[32,384]{1,0:T(8,128)(2,1)S(1)} %get-tuple-element.46), channel_id=1, source_target_pairs={{0,1},{1,0},{2,3},{3,2},{4,5},{5,4},{6,7},{7,6},{8,9},{9,8},{10,11... | collective-permute-start | bytes 73736 | tf_op jit(solution)/shard_map/ppermute | solution.py:293
